TPU v7x, 256 devices: a whole 4x4x8 slice. The times are simulated.
256 devices in a mesh: grp: 2 (over core), brick: 128 (over z, y, x).
Axes of the slice: x: 4, y: 4, z: 8, core: 2. Of those that a mesh axis runs over, the one named last changes fastest.
Arguments:
- density: float32 [512, 64, 256], P('brick', None, 'grp'), may hold values from 0.5 to 2
- energy_field: float32 [512, 64, 256], P('brick', None, 'grp'), may hold values from -6 to 6
- lepton_field: float32 [512, 64, 256], P('brick', None, 'grp'), may hold values from 0.1 to 0.6
- velocity: float32 [3, 512, 64, 256], P(None, 'brick', None, 'grp'), may hold values from -4 to 4
- abundance: float32 [2, 128, 1024, 128], P('grp', 'brick'), may hold values from -1.2 to 1.2
- tracer_mass: float32 [2, 128, 1024], P('grp', 'brick'), may hold values from 0.2 to 1
- tracer_cell: int32 [2, 128, 1024], P('grp', 'brick'), may hold values from 0 to 32767
- tracer_count: int32 [2, 128], P('grp', 'brick'), may hold values from 1 to 1024, as said below
- weak_rates: float32 [128, 128], replicated, may hold values from -0.5 to 0.5
- capture_rates: float32 [128, 128], replicated, may hold values from -0.5 to 0.5
- binding: float32 [128], replicated, may hold values from -6 to 6
- charge_ratio: float32 [128], replicated, may hold values from 0 to 1
Outputs:
- density_out: float32 [512, 64, 256], P('brick', None, 'grp')
- energy_out: float32 [512, 64, 256], P('brick', None, 'grp')
- lepton_out: float32 [512, 64, 256], P('brick', None, 'grp')
- abundance_out: float32 [2, 128, 1024, 128], P('grp', 'brick')
Inputs may be any that keep to these rules, and one draw needn't show every extreme that they name: `tracer_count`: for each index of grp the counts sum to 65536; exactly one brick of each half holds 1024, the most; every other brick holds at most 512, and some brick of each half holds exactly 512.
All inputs are finite; a program needn't handle non-finite values.
Results may differ from a plain program's by a relative error of at most 0.00029.
Values sent between devices are 32-bit elements; how exact they have to be, the bound alone decides.
No kernel may reach another device: no remote copies, remote signals or barrier semaphores. Data moves between devices by JAX's collectives and lax.ppermute only.
A program may use at most 64 MiB of HBM per device.

v0:
```python
import functools

import jax
import jax.numpy as jnp
from jax import lax
from jax.experimental import pallas as pl
from jax.experimental.pallas import tpu as pltpu
from jax.sharding import PartitionSpec as P

SWEEPS = 8
CHUNK = 512
BLOCK = 128
COURANT = 0.8
F32 = jnp.float32
BF16 = jnp.bfloat16


def split(values):
    high = values.astype(BF16)
    return high, (values - high.astype(F32)).astype(BF16)


def matmul(a, b):
    return lax.dot_general(a, b, (((1,), (0,)), ((), ())), preferred_element_type=F32)


def lanes(rows=64):
    return lax.broadcasted_iota(jnp.int32, (rows, 128), 1)


def pack_z(packed, tile, number, lane):
    moved = pltpu.roll(tile, 4 * number + 2, 1)
    inside = jnp.logical_and(lane >= 4 * number, lane < 4 * number + 4)
    return jnp.where(inside, moved, packed)


def along_z(tile, packed, number, lane):
    other = pltpu.roll(packed, (126 - 4 * number) % 128, 1)
    next1 = pltpu.roll(jnp.where(lane == 0, other, tile), 127, 1)
    next2 = pltpu.roll(jnp.where(lane < 2, other, tile), 126, 1)
    last1 = pltpu.roll(jnp.where(lane == 127, other, tile), 1, 1)
    last2 = pltpu.roll(jnp.where(lane >= 126, other, tile), 2, 1)
    return 8.0 * (next1 - last1) - (next2 - last2)


def along_y(tile):
    size = tile.shape[0]
    return 8.0 * (pltpu.roll(tile, size - 1, 0) - pltpu.roll(tile, 1, 0)) - (
        pltpu.roll(tile, size - 2, 0) - pltpu.roll(tile, 2, 0)
    )


def edges_kernel(density, energy, lepton, velocity, low, high, packed):
    lane = lanes()
    pack = jnp.zeros((64, 128), F32)
    for f, field in enumerate((density, energy, lepton)):
        for i in range(2):
            low[f, i] = velocity[0, i] * field[i]
            high[f, i] = velocity[0, i + 2] * field[i + 2]
        for i in range(4):
            pack = pack_z(pack, velocity[2, i] * field[i], 4 * f + i, lane)
    packed[...] = pack


def sum_of_differences(get, velocity, from_low, from_high, from_other, f, lane):
    planes = [get(i) for i in range(4)]
    speed_x = [from_low[f, 0], from_low[f, 1]]
    speed_x += [velocity[0, i] * planes[i] for i in range(4)]
    speed_x += [from_high[f, 0], from_high[f, 1]]
    packed = from_other[...]
    for i in range(4):
        along_x = 8.0 * (speed_x[i + 3] - speed_x[i + 1]) - (speed_x[i + 4] - speed_x[i])
        total = along_x + along_y(velocity[1, i] * planes[i])
        total = total + along_z(velocity[2, i] * planes[i], packed, 4 * f + i, lane)
        yield i, total


def midpoint_kernel(
    density, energy, lepton, velocity, from_low, from_high, from_other, mid, low, high, packed
):
    lane = lanes()
    pack = jnp.zeros((64, 128), F32)
    for f, field in enumerate((density, energy, lepton)):
        for i, total in sum_of_differences(
            lambda i: field[i], velocity, from_low, from_high, from_other, f, lane
        ):
            value = field[i] - (0.5 * COURANT / 12.0) * total
            mid[f, i] = value
            if i < 2:
                low[f, i] = velocity[0, i] * value
            else:
                high[f, i - 2] = velocity[0, i] * value
            pack = pack_z(pack, velocity[2, i] * value, 4 * f + i, lane)
    packed[...] = pack


def final_kernel(
    density, energy, lepton, velocity, mid, from_low, from_high, from_other, deposit,
    density_out, energy_out, lepton_out,
):
    lane = lanes()
    outs = (density_out, energy_out, lepton_out)
    for f, field in enumerate((density, energy, lepton)):
        for i, total in sum_of_differences(
            lambda i: mid[f, i], velocity, from_low, from_high, from_other, f, lane
        ):
            value = field[i] - (COURANT / 12.0) * total
            if f > 0:
                value = value + deposit[f - 1, pl.ds(64 * i, 64), :]
            outs[f][i] = value


def column(row):
    return jnp.transpose(jnp.broadcast_to(row, (128, 128)))


def load_matrices(weak, capture, both, rest):
    matrix = jnp.concatenate([weak[...], capture[...]], axis=1)
    high, low = split(matrix)
    both[...] = jnp.concatenate([high, high], axis=0)
    rest[...] = low


def newton(base, start, get_target, rows_of, both, rest, w_ref, c_ref, x_ref, t_ref, k_ref, a_ref, finish):
    blocks = CHUNK // BLOCK

    def products(b):
        x = x_ref[pl.ds(b * BLOCK, BLOCK), :]
        return matmul(x, both[...]) + matmul(x[:, :128], rest[...])

    def put(b, values):
        high, low = split(values)
        x_ref[pl.ds(b * BLOCK, BLOCK), :] = jnp.concatenate([high, low], axis=1)

    for b in range(blocks):
        put(b, rows_of(b))
    for b in range(blocks):
        at = pl.ds(b * BLOCK, BLOCK)
        here = pl.ds(base + b * BLOCK, BLOCK)
        product = products(b)
        rows = rows_of(b)
        rate_weak, rate_capture = w_ref[here, :], c_ref[here, :]
        alpha = rate_capture * rows[:, 0:1]
        target = rate_weak * product[:, :128] + alpha * product[:, 128:]
        target = get_target(b, rows, target)
        a_ref[at, :] = alpha
        k_ref[at, :] = rate_capture * product[:, 128:]
        t_ref[at, :] = target
        put(b, target)
        start(b, target)
    for sweep in range(SWEEPS):
        for b in range(blocks):
            at = pl.ds(b * BLOCK, BLOCK)
            here = pl.ds(base + b * BLOCK, BLOCK)
            product = products(b)
            before = finish.last[b]
            update = t_ref[at, :] + (
                w_ref[here, :] * product[:, :128]
                + a_ref[at, :] * product[:, 128:]
                + before * k_ref[at, :]
            )
            if sweep < SWEEPS - 1:
                put(b, update)
                start(b, update)
            else:
                finish(b, rows_of(b) + update)


class Finish:
    def __init__(self, write):
        self.last = {}
        self.write = write

    def keep(self, b, values):
        self.last[b] = values[:, 0:1]

    def __call__(self, b, values):
        self.write(b, values)


def first_kernel(
    count, density, energy, lepton, cells, rows, weak, capture,
    iterate, w_out, c_out,
    table, both, rest, x_ref, t_ref, k_ref, a_ref,
):
    load_matrices(weak, capture, both, rest)
    rho = density[...].reshape(256, 128)
    eps = energy[...].reshape(256, 128)
    lam = lepton[...].reshape(256, 128)
    inverse = 1.0 / rho
    weak_high, weak_low = split(0.62 + 0.04 * rho + 0.05 * (lam * inverse))
    capture_high, capture_low = split(0.3 * jax.nn.sigmoid(eps * inverse))
    table[...] = jnp.concatenate([weak_high, weak_low, capture_high, capture_low], axis=1)
    lane = lanes(BLOCK)
    ones = jnp.ones((256, 128), BF16)

    def chunk(k, carry):
        base = k * CHUNK
        for b in range(CHUNK // BLOCK):
            at = pl.ds(pl.multiple_of(base + b * BLOCK, BLOCK), BLOCK)
            cell = column(cells[pl.ds(k * (CHUNK // BLOCK) + b, 1), :])
            row_id = lax.shift_right_logical(cell, 7)
            hot = jnp.concatenate([row_id == lane, row_id == lane + 128], axis=1)
            picked = matmul(jnp.where(hot, 1.0, 0.0).astype(BF16), table[...])
            here = jnp.bitwise_and(cell, 127) == lane
            here = jnp.concatenate([here, here, here, here], axis=1)
            picked = jnp.where(here, picked, 0.0).astype(BF16)
            w_out[at, :] = matmul(picked[:, :256], ones)
            c_out[at, :] = matmul(picked[:, 256:], ones)

        def rows_of(b):
            return rows[pl.ds(pl.multiple_of(base + b * BLOCK, BLOCK), BLOCK), :]

        def write(b, values):
            iterate[pl.ds(pl.multiple_of(base + b * BLOCK, BLOCK), BLOCK), :] = values

        finish = Finish(write)
        newton(
            base, finish.keep, lambda b, rows, target: target, rows_of, both, rest,
            w_out, c_out, x_ref, t_ref, k_ref, a_ref, finish,
        )
        return carry

    lax.fori_loop(0, (count[0, 0] + CHUNK - 1) // CHUNK, chunk, 0)


def second_kernel(
    count, cells, rows, weak, capture, iterate, w_in, c_in, mass, binding, charge,
    rows_out, deposit,
    both, rest, x_ref, t_ref, k_ref, a_ref, gain_both, gain_rest,
):
    load_matrices(weak, capture, both, rest)
    gains = jnp.concatenate([column(binding[...]), column(charge[...])], axis=1)
    high, low = split(gains)
    gain_both[...] = jnp.concatenate([high, high], axis=0)
    gain_rest[...] = low
    rows_out[...] = jnp.zeros(rows_out.shape, F32)
    deposit[...] = jnp.zeros(deposit.shape, F32)
    lane = lanes(BLOCK)
    sublane = lax.broadcasted_iota(jnp.int32, (256, 128), 0)

    def chunk(k, carry):
        base = k * CHUNK

        def place(b):
            return pl.ds(pl.multiple_of(base + b * BLOCK, BLOCK), BLOCK)

        def rows_of(b):
            return iterate[place(b), :]

        def get_target(b, current, target):
            return target - (current - rows[place(b), :])

        def write(b, values):
            slot = base + b * BLOCK + lax.broadcasted_iota(jnp.int32, (BLOCK, 128), 0)
            occupied = slot < count[0, 0]
            rows_out[place(b), :] = jnp.where(occupied, values, 0.0)
            change = jnp.where(occupied, values - rows[place(b), :], 0.0)
            high, low = split(change)
            x_ref[pl.ds(b * BLOCK, BLOCK), :] = jnp.concatenate([high, low], axis=1)

        finish = Finish(write)
        newton(
            base, finish.keep, get_target, rows_of, both, rest,
            w_in, c_in, x_ref, t_ref, k_ref, a_ref, finish,
        )
        hots, values = [], []
        for b in range(CHUNK // BLOCK):
            number = pl.ds(k * (CHUNK // BLOCK) + b, 1)
            cell = cells[number, :]
            hot = lax.shift_right_logical(cell, 7) == sublane
            hots.append(jnp.where(hot, 1.0, 0.0).astype(BF16))
            x = x_ref[pl.ds(b * BLOCK, BLOCK), :]
            gain = matmul(x, gain_both[...]) + matmul(x[:, :128], gain_rest[...])
            weight = jnp.where(
                jnp.bitwise_and(column(cell), 127) == lane, column(mass[number, :]), 0.0
            )
            gain = gain * jnp.concatenate([weight, weight], axis=1)
            high, low = split(gain)
            values.append(jnp.concatenate([high, low], axis=1))
        sums = matmul(jnp.concatenate(hots, axis=1), jnp.concatenate(values, axis=0))
        deposit[0] += sums[:, :128] + sums[:, 256:384]
        deposit[1] += sums[:, 128:256] + sums[:, 384:]
        return carry

    lax.fori_loop(0, (count[0, 0] + CHUNK - 1) // CHUNK, chunk, 0)


VMEM = pl.BlockSpec(memory_space=pltpu.VMEM)
SMEM = pl.BlockSpec(memory_space=pltpu.SMEM)


def call(kernel, name, outs, args, scratch=(), flops=0, smem=0):
    moved = sum(a.size * 4 for a in args) + sum(4 * functools.reduce(lambda p, s: p * s, o) for o in outs)
    return pl.pallas_call(
        kernel,
        name=name,
        out_shape=[jax.ShapeDtypeStruct(o, F32) for o in outs],
        in_specs=[SMEM] * smem + [VMEM] * (len(args) - smem),
        out_specs=[VMEM] * len(outs),
        scratch_shapes=list(scratch),
        compiler_params=pltpu.CompilerParams(vmem_limit_bytes=24 * 2**20),
        cost_estimate=pl.CostEstimate(flops=flops, bytes_accessed=moved, transcendentals=0),
    )(*args)


def exchange(low, high, packed):
    count = lax.axis_size("brick")
    forward = [(i, (i + 1) % count) for i in range(count)]
    backward = [(b, a) for a, b in forward]
    halves = lax.axis_size("grp")
    swap = [(i, (i + 1) % halves) for i in range(halves)]
    from_low = lax.ppermute(high, "brick", forward)
    from_high = lax.ppermute(low, "brick", backward)
    from_other = lax.ppermute(packed, "grp", swap)
    return from_low, from_high, from_other


def on_device(
    density,
    energy_field,
    lepton_field,
    velocity,
    abundance,
    tracer_mass,
    tracer_cell,
    tracer_count,
    weak_rates,
    capture_rates,
    binding,
    charge_ratio,
):
    fields = (density, energy_field, lepton_field)
    edge, tile, all_rows = (3, 2, 64, 128), (64, 128), (1024, 128)
    edges = call(edges_kernel, "edges", [edge, edge, tile], (*fields, velocity))
    arrived = exchange(*edges)

    rows = abundance.reshape(1024, 128)
    cells = tracer_cell.reshape(8, 128)
    mass = tracer_mass.reshape(8, 128)
    matrices = [pltpu.VMEM((256, 256), BF16), pltpu.VMEM((128, 256), BF16)]
    state = [pltpu.VMEM((CHUNK, 256), BF16)] + [pltpu.VMEM((CHUNK, 128), F32)] * 3
    flops = 6 * 2 * 1024 * 128 * 256 * 9
    iterate, rate_weak, rate_capture = call(
        first_kernel, "newton_first", [all_rows] * 3,
        (tracer_count, *fields, cells, rows, weak_rates, capture_rates),
        [pltpu.VMEM((256, 512), BF16), *matrices, *state], flops, 1,
    )
    mid, *edges = call(
        midpoint_kernel, "midpoint", [(3, 4, 64, 128), edge, edge, tile], (*fields, velocity, *arrived)
    )
    arrived = exchange(*edges)
    finished, deposit = call(
        second_kernel, "newton_second", [all_rows, (2, 256, 128)],
        (
            tracer_count, cells, rows, weak_rates, capture_rates, iterate, rate_weak, rate_capture,
            mass, binding.reshape(1, 128), charge_ratio.reshape(1, 128),
        ),
        [*matrices, *state, *matrices], flops, 1,
    )
    outs = call(
        final_kernel, "advance", [(4, 64, 128)] * 3, (*fields, velocity, mid, *arrived, deposit)
    )
    return (*outs, finished[None, None])


def solution(mesh):
    return jax.shard_map(
        on_device,
        mesh=mesh,
        in_specs=(
            P("brick", None, "grp"),
            P("brick", None, "grp"),
            P("brick", None, "grp"),
            P(None, "brick", None, "grp"),
            P("grp", "brick", None, None),
            P("grp", "brick", None),
            P("grp", "brick", None),
            P("grp", "brick"),
            P(),
            P(),
            P(),
            P(),
        ),
        out_specs=(
            P("brick", None, "grp"),
            P("brick", None, "grp"),
            P("brick", None, "grp"),
            P("grp", "brick", None, None),
        ),
        check_vma=False,
    )
```

profile of v0, /device:TPU:1, one launch (start us, length us, event | category | flops | bytes accessed | tf_op | source)
XLA Modules:
  0.0 36.5 jit_solution(8082780377325937876)
XLA Ops:
  0.6 0.0 copy-start
  0.6 1.0 %copy-done = f32[3,4,64,128]{3,2,1,0:T(8,128)S(1)} copy-done((f32[3,4,64,128]{3,2,1,0:T(8,128)S(1)}, f32[3,4,64,128]{3,2,1,0:T(8,128)}, u32[]{:S(2)}) %copy-start) | copy-done | bytes 393240
  1.6 0.9 %copy-done.2 = f32[4,64,128]{2,1,0:T(8,128)S(1)} copy-done((f32[4,64,128]{2,1,0:T(8,128)S(1)}, f32[4,64,128]{2,1,0:T(8,128)}, u32[]{:S(2)}) %copy-start.2) | copy-done | bytes 131096
  2.5 0.9 %copy-done.4 = f32[4,64,128]{2,1,0:T(8,128)S(1)} copy-done((f32[4,64,128]{2,1,0:T(8,128)S(1)}, f32[4,64,128]{2,1,0:T(8,128)}, u32[]{:S(2)}) %copy-start.4) | copy-done | bytes 131096
  3.4 0.9 %copy-done.6 = f32[4,64,128]{2,1,0:T(8,128)S(1)} copy-done((f32[4,64,128]{2,1,0:T(8,128)S(1)}, f32[4,64,128]{2,1,0:T(8,128)}, u32[]{:S(2)}) %copy-start.6) | copy-done | bytes 131096
  4.4 0.2 edges.1
  4.5 2.1 %collective-permute-start = (f32[3,2,64,128]{3,2,1,0:T(8,128)S(1)}, f32[3,2,64,128]{3,2,1,0:T(8,128)S(1)}, u32[]{:S(2)}, u32[]{:S(2)}) collective-permute-start(f32[3,2,64,128]{3,2,1,0:T(8,128)S(1)} %get-tuple-element.19), channel_id=1, source_target_pairs={{0,1},{1,2},{2,3},{3,4},{4,5},{5,6},{6,7},{7,8},{8,9},{9,10},{10,1... | collective-permute-start | bytes 589832 | tf_op jit(solution)/shard_map/ppermute | solution.py:313
  6.6 9.1 %collective-permute-start.1 = (f32[3,2,64,128]{3,2,1,0:T(8,128)S(1)}, f32[3,2,64,128]{3,2,1,0:T(8,128)S(1)}, u32[]{:S(2)}, u32[]{:S(2)}) collective-permute-start(f32[3,2,64,128]{3,2,1,0:T(8,128)S(1)} %get-tuple-element.20), channel_id=1, source_target_pairs={{1,0},{2,1},{3,2},{4,3},{5,4},{6,5},{7,6},{8,7},{9,8},{10,9},{11,1... | collective-permute-start | bytes 589832 | tf_op jit(solution)/shard_map/ppermute | solution.py:314
  15.8 1.0 %collective-permute-start.2 = (f32[64,128]{1,0:T(8,128)S(1)}, f32[64,128]{1,0:T(8,128)S(1)}, u32[]{:S(2)}, u32[]{:S(2)}) collective-permute-start(f32[64,128]{1,0:T(8,128)S(1)} %get-tuple-element.21), channel_id=1, source_target_pairs={{0,128},{128,0},{1,129},{129,1},{2,130},{130,2},{3,131},{131,3},{4... | collective-permute-start | bytes 98312 | tf_op jit(solution)/shard_map/ppermute | solution.py:315
  17.4 0.0 copy-start.1
  17.4 2.5 %newton_first.1 = (f32[1024,128]{1,0:T(8,128)S(1)}, f32[1024,128]{1,0:T(8,128)S(1)}, f32[1024,128]{1,0:T(8,128)S(1)}) custom-call(s32[1,1]{1,0:T(1,128)S(6)} %copy.16.count, f32[4,64,128]{2,1,0:T(8,128)S(1)} %copy-done.2, f32[4,64,128]{2,1,0:T(8,128)S(1)} %copy-done.4, f32[4,64,128]{2,1,0:T(8,128)S(1)} %copy-done.6, s32[8,128]{1,0:T(8,128)S(1)} %bitcast.8, ...), custom_call_target="tpu_custom_call" | custom-call | flops 3623878656 | bytes 2625540 | tf_op jit(solution)/shard_map/newton_first/pallas_call | solution.py:295
  19.9 0.0 collective-permute-done.2.from_other
  19.9 0.4 %collective-permute-done.from_low = f32[3,2,64,128]{3,2,1,0:T(8,128)S(1)} collective-permute-done((f32[3,2,64,128]{3,2,1,0:T(8,128)S(1)}, f32[3,2,64,128]{3,2,1,0:T(8,128)S(1)}, u32[]{:S(2)}, u32[]{:S(2)}) %collective-permute-start) | collective-permute-done | bytes 196640 | tf_op jit(solution)/shard_map/ppermute | solution.py:313
  20.3 0.0 collective-permute-done.1.from_high
  20.3 1.8 %midpoint.1 = (f32[3,4,64,128]{3,2,1,0:T(8,128)S(1)}, f32[3,2,64,128]{3,2,1,0:T(8,128)S(1)}, f32[3,2,64,128]{3,2,1,0:T(8,128)S(1)}, f32[64,128]{1,0:T(8,128)S(1)}) custom-call(f32[4,64,128]{2,1,0:T(8,128)S(1)} %copy-done.2, f32[4,64,128]{2,1,0:T(8,128)S(1)} %copy-done.4, f32[4,64,128]{2,1,0:T(8,128)S(1)} %copy-done.6, f32[3,4,64,128]{3,2,1,0:T(8,128)S(1)} %copy-done.1, ...), custom_call_target="tpu_custom_call" | custom-call | bytes 2031616 | tf_op jit(solution)/shard_map/midpoint/pallas_call | solution.py:295
  22.1 0.1 collective-permute-start.3
  22.2 6.9 %collective-permute-start.4 = (f32[3,2,64,128]{3,2,1,0:T(8,128)S(1)}, f32[3,2,64,128]{3,2,1,0:T(8,128)S(1)}, u32[]{:S(2)}, u32[]{:S(2)}) collective-permute-start(f32[3,2,64,128]{3,2,1,0:T(8,128)S(1)} %get-tuple-element.24), channel_id=1, source_target_pairs={{1,0},{2,1},{3,2},{4,3},{5,4},{6,5},{7,6},{8,7},{9,8},{10,9},{11,1... | collective-permute-start | bytes 589832 | tf_op jit(solution)/shard_map/ppermute | solution.py:314
  29.1 1.8 %collective-permute-start.5 = (f32[64,128]{1,0:T(8,128)S(1)}, f32[64,128]{1,0:T(8,128)S(1)}, u32[]{:S(2)}, u32[]{:S(2)}) collective-permute-start(f32[64,128]{1,0:T(8,128)S(1)} %get-tuple-element.25), channel_id=1, source_target_pairs={{0,128},{128,0},{1,129},{129,1},{2,130},{130,2},{3,131},{131,3},{4... | collective-permute-start | bytes 98312 | tf_op jit(solution)/shard_map/ppermute | solution.py:315
  30.9 0.7 %copy-done.12 = f32[1,1,1024]{2,1,0:T(1,128)S(1)} copy-done((f32[1,1,1024]{2,1,0:T(1,128)S(1)}, f32[1,1,1024]{2,1,0:T(1,128)}, u32[]{:S(2)}) %copy-start.12) | copy-done | bytes 4120
  31.6 0.0 copy-start.7
  31.6 3.1 %newton_second.1 = (f32[1024,128]{1,0:T(8,128)}, f32[2,256,128]{2,1,0:T(8,128)S(1)}) custom-call(s32[1,1]{1,0:T(1,128)S(6)} %copy.16.count, s32[8,128]{1,0:T(8,128)S(1)} %bitcast.9, f32[1024,128]{1,0:T(8,128)S(1)} %bitcast.7, f32[128,128]{1,0:T(8,128)S(1)} %copy-done.9, f32[128,128]{1,0:T(8,128)S(1)} %copy-done.10, ...), custom_call_target="tpu_custom_call" | custom-call | flops 3623878656 | bytes 3023876 | tf_op jit(solution)/shard_map/newton_second/pallas_call | solution.py:295
  34.6 0.0 collective-permute-done.3.from_low
  34.7 0.0 collective-permute-done.4.from_high
  34.7 1.8 %advance.1 = (f32[4,64,128]{2,1,0:T(8,128)}, f32[4,64,128]{2,1,0:T(8,128)}, f32[4,64,128]{2,1,0:T(8,128)}) custom-call(f32[4,64,128]{2,1,0:T(8,128)S(1)} %copy-done.3, f32[4,64,128]{2,1,0:T(8,128)S(1)} %copy-done.5, f32[4,64,128]{2,1,0:T(8,128)S(1)} %copy-done.7, f32[3,4,64,128]{3,2,1,0:T(8,128)S(1)} %copy-done.1, ...), custom_call_target="tpu_custom_call" | custom-call | bytes 2260992 | tf_op jit(solution)/shard_map/advance/pallas_call | solution.py:295
  (23 shorter events, 0.0 us)
Async XLA Ops:
  0.6 1.0 %copy-start = (f32[3,4,64,128]{3,2,1,0:T(8,128)S(1)}, f32[3,4,64,128]{3,2,1,0:T(8,128)}, u32[]{:S(2)}) copy-start(f32[3,4,64,128]{3,2,1,0:T(8,128)} %velocity.5) | copy-start | bytes 1179652
  1.6 0.9 %copy-start.2 = (f32[4,64,128]{2,1,0:T(8,128)S(1)}, f32[4,64,128]{2,1,0:T(8,128)}, u32[]{:S(2)}) copy-start(f32[4,64,128]{2,1,0:T(8,128)} %density.7) | copy-start | bytes 393220
  2.5 0.9 %copy-start.4 = (f32[4,64,128]{2,1,0:T(8,128)S(1)}, f32[4,64,128]{2,1,0:T(8,128)}, u32[]{:S(2)}) copy-start(f32[4,64,128]{2,1,0:T(8,128)} %energy.7) | copy-start | bytes 393220
  3.4 0.9 %copy-start.6 = (f32[4,64,128]{2,1,0:T(8,128)S(1)}, f32[4,64,128]{2,1,0:T(8,128)}, u32[]{:S(2)}) copy-start(f32[4,64,128]{2,1,0:T(8,128)} %lepton.7) | copy-start | bytes 393220
  4.3 13.0 %copy-start.8 = (f32[1,1,1024,128]{3,2,1,0:T(8,128)S(1)}, f32[1,1,1024,128]{3,2,1,0:T(8,128)}, u32[]{:S(2)}) copy-start(f32[1,1,1024,128]{3,2,1,0:T(8,128)} %param.16) | copy-start | bytes 1572868
  4.3 13.0 %copy-start.9 = (f32[128,128]{1,0:T(8,128)S(1)}, f32[128,128]{1,0:T(8,128)}, u32[]{:S(2)}) copy-start(f32[128,128]{1,0:T(8,128)} %weak.3) | copy-start | bytes 196612
  4.3 13.0 %copy-start.10 = (f32[128,128]{1,0:T(8,128)S(1)}, f32[128,128]{1,0:T(8,128)}, u32[]{:S(2)}) copy-start(f32[128,128]{1,0:T(8,128)} %capture.3) | copy-start | bytes 196612
  4.5 15.8 %collective-permute-start = (f32[3,2,64,128]{3,2,1,0:T(8,128)S(1)}, f32[3,2,64,128]{3,2,1,0:T(8,128)S(1)}, u32[]{:S(2)}, u32[]{:S(2)}) collective-permute-start(f32[3,2,64,128]{3,2,1,0:T(8,128)S(1)} %get-tuple-element.19), channel_id=1, source_target_pairs={{0,1},{1,2},{2,3},{3,4},{4,5},{5,6},{6,7},{7,8},{8,9},{9,10},{10,1... | collective-permute-start | bytes 589832 | tf_op jit(solution)/shard_map/ppermute | solution.py:313
  6.6 10.8 %copy-start.11 = (s32[1,1,1024]{2,1,0:T(1,128)S(1)}, s32[1,1,1024]{2,1,0:T(1,128)}, u32[]{:S(2)}) copy-start(s32[1,1,1024]{2,1,0:T(1,128)} %param.18) | copy-start | bytes 12292
  6.6 13.6 %collective-permute-start.1 = (f32[3,2,64,128]{3,2,1,0:T(8,128)S(1)}, f32[3,2,64,128]{3,2,1,0:T(8,128)S(1)}, u32[]{:S(2)}, u32[]{:S(2)}) collective-permute-start(f32[3,2,64,128]{3,2,1,0:T(8,128)S(1)} %get-tuple-element.20), channel_id=1, source_target_pairs={{1,0},{2,1},{3,2},{4,3},{5,4},{6,5},{7,6},{8,7},{9,8},{10,9},{11,1... | collective-permute-start | bytes 589832 | tf_op jit(solution)/shard_map/ppermute | solution.py:314
  15.8 4.1 %collective-permute-start.2 = (f32[64,128]{1,0:T(8,128)S(1)}, f32[64,128]{1,0:T(8,128)S(1)}, u32[]{:S(2)}, u32[]{:S(2)}) collective-permute-start(f32[64,128]{1,0:T(8,128)S(1)} %get-tuple-element.21), channel_id=1, source_target_pairs={{0,128},{128,0},{1,129},{129,1},{2,130},{130,2},{3,131},{131,3},{4... | collective-permute-start | bytes 98312 | tf_op jit(solution)/shard_map/ppermute | solution.py:315
  17.4 2.9 %copy-start.1 = (f32[3,4,64,128]{3,2,1,0:T(8,128)S(1)}, f32[3,4,64,128]{3,2,1,0:T(8,128)}, u32[]{:S(2)}) copy-start(f32[3,4,64,128]{3,2,1,0:T(8,128)} %velocity.5) | copy-start | bytes 1179652
  22.1 12.6 %collective-permute-start.3 = (f32[3,2,64,128]{3,2,1,0:T(8,128)S(1)}, f32[3,2,64,128]{3,2,1,0:T(8,128)S(1)}, u32[]{:S(2)}, u32[]{:S(2)}) collective-permute-start(f32[3,2,64,128]{3,2,1,0:T(8,128)S(1)} %get-tuple-element.23), channel_id=1, source_target_pairs={{0,1},{1,2},{2,3},{3,4},{4,5},{5,6},{6,7},{7,8},{8,9},{9,10},{10,1... | collective-permute-start | bytes 589832 | tf_op jit(solution)/shard_map/ppermute | solution.py:313
  22.2 12.5 %collective-permute-start.4 = (f32[3,2,64,128]{3,2,1,0:T(8,128)S(1)}, f32[3,2,64,128]{3,2,1,0:T(8,128)S(1)}, u32[]{:S(2)}, u32[]{:S(2)}) collective-permute-start(f32[3,2,64,128]{3,2,1,0:T(8,128)S(1)} %get-tuple-element.24), channel_id=1, source_target_pairs={{1,0},{2,1},{3,2},{4,3},{5,4},{6,5},{7,6},{8,7},{9,8},{10,9},{11,1... | collective-permute-start | bytes 589832 | tf_op jit(solution)/shard_map/ppermute | solution.py:314
  29.1 5.6 %collective-permute-start.5 = (f32[64,128]{1,0:T(8,128)S(1)}, f32[64,128]{1,0:T(8,128)S(1)}, u32[]{:S(2)}, u32[]{:S(2)}) collective-permute-start(f32[64,128]{1,0:T(8,128)S(1)} %get-tuple-element.25), channel_id=1, source_target_pairs={{0,128},{128,0},{1,129},{129,1},{2,130},{130,2},{3,131},{131,3},{4... | collective-permute-start | bytes 98312 | tf_op jit(solution)/shard_map/ppermute | solution.py:315
  30.9 0.7 %copy-start.12 = (f32[1,1,1024]{2,1,0:T(1,128)S(1)}, f32[1,1,1024]{2,1,0:T(1,128)}, u32[]{:S(2)}) copy-start(f32[1,1,1024]{2,1,0:T(1,128)} %param.17) | copy-start | bytes 12292
  30.9 0.7 %copy-start.13 = (f32[128]{0:T(128)S(1)}, f32[128]{0:T(128)}, u32[]{:S(2)}) copy-start(f32[128]{0:T(128)} %param.22) | copy-start | bytes 1540
  30.9 0.7 %copy-start.14 = (f32[128]{0:T(128)S(1)}, f32[128]{0:T(128)}, u32[]{:S(2)}) copy-start(f32[128]{0:T(128)} %param.23) | copy-start | bytes 1540
  31.5 3.1 %copy-start.3 = (f32[4,64,128]{2,1,0:T(8,128)S(1)}, f32[4,64,128]{2,1,0:T(8,128)}, u32[]{:S(2)}) copy-start(f32[4,64,128]{2,1,0:T(8,128)} %density.7) | copy-start | bytes 393220
  31.5 3.1 %copy-start.5 = (f32[4,64,128]{2,1,0:T(8,128)S(1)}, f32[4,64,128]{2,1,0:T(8,128)}, u32[]{:S(2)}) copy-start(f32[4,64,128]{2,1,0:T(8,128)} %energy.7) | copy-start | bytes 393220
  31.6 3.1 %copy-start.7 = (f32[4,64,128]{2,1,0:T(8,128)S(1)}, f32[4,64,128]{2,1,0:T(8,128)}, u32[]{:S(2)}) copy-start(f32[4,64,128]{2,1,0:T(8,128)} %lepton.7) | copy-start | bytes 393220
where the time goes:
time: 36.8 us; the launch traced here: 36.5 us
  starting transfers between devices  20.9 us (57%)
  Pallas kernels  9.35 us (25%)
  local copies, waits for them, and re-layouts  4.43 us (12%)
  between operations  1.43 us (4%)
  waiting for transfers between devices  0.38 us (1%)
    ppermute x2, starting transfers between devices, exchange(): from_high = lax.ppermute(low, 'brick', backward)  16 us
    pallas_call x5, Pallas kernels, call(): pl.pallas_call(kernel, name=name, out_shape=[jax.ShapeDtypeStruct(o, F32)...  9.35 us
    unnamed x30, local copies, waits for them, and re-layouts  4.43 us
    ppermute x2, starting transfers between devices, exchange(): from_other = lax.ppermute(packed, 'grp', swap)  2.74 us
    ppermute x2, starting transfers between devices, exchange(): from_low = lax.ppermute(high, 'brick', forward)  2.2 us
  transfers between devices with their start and end apart: 6, of which 1 were waited for; matrix products, arithmetic and copies ran while one was open for 0% of the time, Pallas kernels for 15%

commit v1 on v0

v1 whole, which is shorter than its diff:
```python
import math

import jax
import jax.numpy as jnp
from jax import lax
from jax.experimental import pallas as pl
from jax.experimental.pallas import tpu as pltpu
from jax.sharding import PartitionSpec as P

SWEEPS = 8
CHUNK = 512
BLOCK = 128
COURANT = 0.8
HALF = 0.5 * COURANT / 12.0
FULL = COURANT / 12.0
F32 = jnp.float32
BF16 = jnp.bfloat16


def split(values):
    high = values.astype(BF16)
    return high, (values - high.astype(F32)).astype(BF16)


def matmul(a, b):
    return lax.dot_general(a, b, (((1,), (0,)), ((), ())), preferred_element_type=F32)


def lanes(rows=64):
    return lax.broadcasted_iota(jnp.int32, (rows, 128), 1)


def pack_z(packed, tile, first, lane):
    moved = pltpu.roll(tile, first + 2, 1)
    inside = jnp.logical_and(lane >= first, lane < first + 4)
    return jnp.where(inside, moved, packed)


def unpack_z(packed, first, lane):
    moved = pltpu.roll(packed, (126 - first) % 128, 1)
    return jnp.where(jnp.logical_or(lane < 2, lane >= 126), moved, 0.0)


def edge_correction(other, own, lane):
    lack = other - own
    place = jnp.bitwise_and(lane, 3)
    far = jnp.where(place < 2, -pltpu.roll(lack, 126, 1), pltpu.roll(lack, 2, 1))
    near = jnp.where(place == 1, pltpu.roll(lack, 127, 1), 0.0)
    near = near - jnp.where(place == 2, pltpu.roll(lack, 1, 1), 0.0)
    return far + 8.0 * near


def along_z(tile):
    after = 8.0 * tile - pltpu.roll(tile, 127, 1)
    before = 8.0 * tile - pltpu.roll(tile, 1, 1)
    return pltpu.roll(after, 127, 1) - pltpu.roll(before, 1, 1)


def along_y(tile, pad):
    pad[pl.ds(8, 64), :] = tile
    pad[pl.ds(0, 8), :] = tile[56:]
    pad[pl.ds(72, 8), :] = tile[:8]
    return 8.0 * (pad[pl.ds(9, 64), :] - pad[pl.ds(7, 64), :]) - (
        pad[pl.ds(10, 64), :] - pad[pl.ds(6, 64), :]
    )


def inner_differences(get, velocity, pads, f):
    for i in range(4):
        plane = [velocity[0, j] * get(j) for j in range(4) if 0 < abs(j - i) < 3]
        if i == 0:
            total = 8.0 * plane[0] - plane[1]
        elif i == 1:
            total = 8.0 * (plane[1] - plane[0]) - plane[2]
        elif i == 2:
            total = 8.0 * (plane[2] - plane[1]) + plane[0]
        else:
            total = plane[0] - 8.0 * plane[1]
        total = total + along_y(velocity[1, i] * get(i), pads.at[4 * f + i])
        yield i, total + along_z(velocity[2, i] * get(i))


def sides():
    odd = jnp.bitwise_and(lax.axis_index("brick"), 1)
    even = 1 - odd
    return (
        (3 * even, 1 + even, (1 - 2 * odd).astype(F32)),
        (3 * odd, 1 + odd, (2 * odd - 1).astype(F32)),
    )


def edges_kernel(
    density, energy, lepton, speeds, state, velocity, partial, first, second, packed, pads, sems
):
    copies = [
        pltpu.make_async_copy(ref, state.at[f], sems.at[f])
        for f, ref in enumerate((density, energy, lepton))
    ]
    copies.append(pltpu.make_async_copy(speeds, velocity, sems.at[3]))
    for copy in copies:
        copy.start()
    for copy in copies:
        copy.wait()
    lane = lanes()
    pack = jnp.zeros((64, 128), F32)
    for f in range(3):
        for i, total in inner_differences(lambda i: state[f, i], velocity, pads, f):
            partial[f, i] = total
            pack = pack_z(pack, velocity[2, i] * state[f, i], 4 * (4 * f + i), lane)
    packed[...] = pack
    for (near, far, _), out, start in zip(sides(), (first, second), (48, 72)):
        pack = jnp.zeros((64, 128), F32)
        for k, plane in enumerate((near, far)):
            speed = velocity[0, plane]
            out[12 + k] = speed
            for f in range(3):
                value = state[f, plane]
                out[2 * f + k] = speed * value
                out[6 + 2 * f + k] = speed * (value - HALF * partial[f, plane])
                pack = pack_z(pack, velocity[2, plane] * value, start + 4 * (2 * f + k), lane)
        out[14] = pack


def midpoint_kernel(
    state, velocity, partial, first, second, packed, from_other, deposit, mid, exchanged, total
):
    lane = lanes()
    correction = edge_correction(from_other[...], packed[...], lane)
    for f in range(3):
        for i in range(4):
            total[i] = partial[f, i] + unpack_z(correction, 4 * (4 * f + i), lane)
        for (near, far, sign), side in zip(sides(), (first, second)):
            total[near] += sign * (8.0 * side[2 * f] - side[2 * f + 1])
            total[far] += -sign * side[2 * f]
        for i in range(4):
            mid[f, i] = state[f, i] - HALF * total[i]
    pack = jnp.where(lane < 72, first[14], second[14])
    for f in range(3):
        for i in range(4):
            pack = pack_z(pack, velocity[2, i] * mid[f, i], 4 * (4 * f + i), lane)
    exchanged[...] = pack


def advance_kernel(state, velocity, mid, first, second, deposit, advanced, pads):
    for f in range(3):
        for i, total in inner_differences(lambda i: mid[f, i], velocity, pads, f):
            value = state[f, i] - FULL * total
            if f > 0:
                value = value + deposit[f - 1, pl.ds(64 * i, 64), :]
            advanced[f, i] = value
        for (near, far, sign), side in zip(sides(), (first, second)):
            here = velocity[0, near] * state[f, near]
            behind = velocity[0, far] * state[f, far]
            step = sign * HALF
            close = side[6 + 2 * f] + step * (side[12] * (8.0 * here - behind))
            remote = side[7 + 2 * f] - step * (side[13] * here)
            advanced[f, near] += (-FULL * sign) * (8.0 * close - remote)
            advanced[f, far] += (FULL * sign) * close


def finish_kernel(
    advanced, first, second, sent, from_other, density_out, energy_out, lepton_out, total
):
    lane = lanes()
    correction = edge_correction(from_other[...], sent[...], lane)
    outs = (density_out, energy_out, lepton_out)
    for f in range(3):
        for i in range(4):
            total[i] = unpack_z(correction, 4 * (4 * f + i), lane)
        for (near, far, sign), side, start in zip(sides(), (first, second), (48, 72)):
            start = start + 8 * f
            close = (sign * HALF) * (side[12] * unpack_z(correction, start, lane))
            remote = (sign * HALF) * (side[13] * unpack_z(correction, start + 4, lane))
            total[near] += remote - 8.0 * close
            total[far] += close
        for i in range(4):
            outs[f][i] = advanced[f, i] - FULL * total[i]


def column(row):
    return jnp.transpose(jnp.broadcast_to(row, (128, 128)))


def load_matrices(weak, capture, both, rest):
    matrix = jnp.concatenate([weak[...], capture[...]], axis=1)
    high, low = split(matrix)
    both[...] = jnp.concatenate([high, high], axis=0)
    rest[...] = low


def newton(base, start, get_target, rows_of, both, rest, w_ref, c_ref, x_ref, t_ref, k_ref, a_ref, finish):
    blocks = CHUNK // BLOCK

    def products(b):
        x = x_ref[pl.ds(b * BLOCK, BLOCK), :]
        return matmul(x, both[...]) + matmul(x[:, :128], rest[...])

    def put(b, values):
        high, low = split(values)
        x_ref[pl.ds(b * BLOCK, BLOCK), :] = jnp.concatenate([high, low], axis=1)

    for b in range(blocks):
        put(b, rows_of(b))
    for b in range(blocks):
        at = pl.ds(b * BLOCK, BLOCK)
        here = pl.ds(base + b * BLOCK, BLOCK)
        product = products(b)
        rows = rows_of(b)
        rate_weak, rate_capture = w_ref[here, :], c_ref[here, :]
        alpha = rate_capture * rows[:, 0:1]
        target = rate_weak * product[:, :128] + alpha * product[:, 128:]
        target = get_target(b, rows, target)
        a_ref[at, :] = alpha
        k_ref[at, :] = rate_capture * product[:, 128:]
        t_ref[at, :] = target
        put(b, target)
        start(b, target)
    for sweep in range(SWEEPS):
        for b in range(blocks):
            at = pl.ds(b * BLOCK, BLOCK)
            here = pl.ds(base + b * BLOCK, BLOCK)
            product = products(b)
            before = finish.last[b]
            update = t_ref[at, :] + (
                w_ref[here, :] * product[:, :128]
                + a_ref[at, :] * product[:, 128:]
                + before * k_ref[at, :]
            )
            if sweep < SWEEPS - 1:
                put(b, update)
                start(b, update)
            else:
                finish(b, rows_of(b) + update)


class Finish:
    def __init__(self, write):
        self.last = {}
        self.write = write

    def keep(self, b, values):
        self.last[b] = values[:, 0:1]

    def __call__(self, b, values):
        self.write(b, values)


def network_kernel(
    count, state, cells, rows, weak, capture, mass, binding, charge,
    rows_out, deposit,
    table, both, rest, x_ref, t_ref, k_ref, a_ref, w_ref, c_ref, iterate, gain_both, gain_rest,
):
    load_matrices(weak, capture, both, rest)
    rho, eps, lam = (state[f].reshape(256, 128) for f in range(3))
    inverse = 1.0 / rho
    weak_high, weak_low = split(0.62 + 0.04 * rho + 0.05 * (lam * inverse))
    capture_high, capture_low = split(0.3 * jax.nn.sigmoid(eps * inverse))
    table[...] = jnp.concatenate([weak_high, weak_low, capture_high, capture_low], axis=1)
    gains = jnp.concatenate([column(binding[...]), column(charge[...])], axis=1)
    high, low = split(gains)
    gain_both[...] = jnp.concatenate([high, high], axis=0)
    gain_rest[...] = low
    rows_out[...] = jnp.zeros(rows_out.shape, F32)
    deposit[...] = jnp.zeros(deposit.shape, F32)
    lane = lanes(BLOCK)
    sublane = lax.broadcasted_iota(jnp.int32, (256, 128), 0)
    ones = jnp.ones((256, 128), BF16)

    def chunk(k, carry):
        base = k * CHUNK

        def place(b):
            return pl.ds(pl.multiple_of(base + b * BLOCK, BLOCK), BLOCK)

        def inside(b):
            return pl.ds(b * BLOCK, BLOCK)

        for b in range(CHUNK // BLOCK):
            cell = column(cells[pl.ds(k * (CHUNK // BLOCK) + b, 1), :])
            row_id = lax.shift_right_logical(cell, 7)
            hot = jnp.concatenate([row_id == lane, row_id == lane + 128], axis=1)
            picked = matmul(jnp.where(hot, 1.0, 0.0).astype(BF16), table[...])
            here = jnp.bitwise_and(cell, 127) == lane
            here = jnp.concatenate([here, here, here, here], axis=1)
            picked = jnp.where(here, picked, 0.0).astype(BF16)
            w_ref[inside(b), :] = matmul(picked[:, :256], ones)
            c_ref[inside(b), :] = matmul(picked[:, 256:], ones)

        def write_first(b, values):
            iterate[inside(b), :] = values

        def write_last(b, values):
            slot = base + b * BLOCK + lax.broadcasted_iota(jnp.int32, (BLOCK, 128), 0)
            occupied = slot < count[0, 0]
            rows_out[place(b), :] = jnp.where(occupied, values, 0.0)
            change = jnp.where(occupied, values - rows[place(b), :], 0.0)
            high, low = split(change)
            x_ref[inside(b), :] = jnp.concatenate([high, low], axis=1)

        finish = Finish(write_first)
        newton(
            0, finish.keep, lambda b, current, target: target, lambda b: rows[place(b), :],
            both, rest, w_ref, c_ref, x_ref, t_ref, k_ref, a_ref, finish,
        )
        finish = Finish(write_last)
        newton(
            0, finish.keep, lambda b, current, target: target - (current - rows[place(b), :]),
            lambda b: iterate[inside(b), :],
            both, rest, w_ref, c_ref, x_ref, t_ref, k_ref, a_ref, finish,
        )
        hots, values = [], []
        for b in range(CHUNK // BLOCK):
            number = pl.ds(k * (CHUNK // BLOCK) + b, 1)
            cell = cells[number, :]
            hot = lax.shift_right_logical(cell, 7) == sublane
            hots.append(jnp.where(hot, 1.0, 0.0).astype(BF16))
            x = x_ref[inside(b), :]
            gain = matmul(x, gain_both[...]) + matmul(x[:, :128], gain_rest[...])
            weight = jnp.where(
                jnp.bitwise_and(column(cell), 127) == lane, column(mass[number, :]), 0.0
            )
            gain = gain * jnp.concatenate([weight, weight], axis=1)
            high, low = split(gain)
            values.append(jnp.concatenate([high, low], axis=1))
        sums = matmul(jnp.concatenate(hots, axis=1), jnp.concatenate(values, axis=0))
        deposit[0] += sums[:, :128] + sums[:, 256:384]
        deposit[1] += sums[:, 128:256] + sums[:, 384:]
        return carry

    lax.fori_loop(0, (count[0, 0] + CHUNK - 1) // CHUNK, chunk, 0)


VMEM = pl.BlockSpec(memory_space=pltpu.VMEM)
SMEM = pl.BlockSpec(memory_space=pltpu.SMEM)
HBM = pl.BlockSpec(memory_space=pltpu.HBM)


def call(kernel, name, outs, args, scratch=(), flops=0, first=()):
    args = [
        pltpu.with_memory_space_constraint(a, pltpu.HBM) if s is HBM else a
        for a, s in zip(args, list(first) + [None] * len(args))
    ]
    moved = sum(a.size * 4 for a in args) + sum(4 * math.prod(o) for o in outs)
    return pl.pallas_call(
        kernel,
        name=name,
        out_shape=[jax.ShapeDtypeStruct(o, F32) for o in outs],
        in_specs=list(first) + [VMEM] * (len(args) - len(first)),
        out_specs=[VMEM] * len(outs),
        scratch_shapes=list(scratch),
        compiler_params=pltpu.CompilerParams(vmem_limit_bytes=24 * 2**20),
        cost_estimate=pl.CostEstimate(flops=flops, bytes_accessed=moved, transcendentals=0),
    )(*args)


def swap_halves(packed):
    halves = lax.axis_size("grp")
    return lax.ppermute(packed, "grp", [(i, (i + 1) % halves) for i in range(halves)])


def swap_pairs(first, second):
    count = lax.axis_size("brick")
    even = [(i, i ^ 1) for i in range(count)]
    odd = [(i, (i + 1) % count if i % 2 else (i - 1) % count) for i in range(count)]
    return lax.ppermute(first, "brick", even), lax.ppermute(second, "brick", odd)


def on_device(
    density,
    energy_field,
    lepton_field,
    velocity,
    abundance,
    tracer_mass,
    tracer_cell,
    tracer_count,
    weak_rates,
    capture_rates,
    binding,
    charge_ratio,
):
    fields = (density, energy_field, lepton_field)
    whole, side, tile = (3, 4, 64, 128), (15, 64, 128), (64, 128)
    pads = pltpu.VMEM((12, 80, 128), F32)
    planes = pltpu.VMEM((4, 64, 128), F32)
    state, speeds, partial, first, second, packed = call(
        edges_kernel, "edges", [whole, whole, whole, side, side, tile], (*fields, velocity),
        [pads, pltpu.SemaphoreType.DMA((4,))], 0, [HBM] * 4,
    )
    first, second = swap_pairs(first, second)
    from_other = swap_halves(packed)

    rows = pltpu.VMEM((CHUNK, 128), F32)
    matrices = [pltpu.VMEM((256, 256), BF16), pltpu.VMEM((128, 256), BF16)]
    finished, deposit = call(
        network_kernel, "network", [(1024, 128), (2, 256, 128)],
        (
            tracer_count, state, tracer_cell.reshape(8, 128), abundance.reshape(1024, 128),
            weak_rates, capture_rates, tracer_mass.reshape(8, 128),
            binding.reshape(1, 128), charge_ratio.reshape(1, 128),
        ),
        [pltpu.VMEM((256, 512), BF16), *matrices, pltpu.VMEM((CHUNK, 256), BF16)]
        + [rows] * 6 + matrices,
        6 * 2 * 1024 * 128 * 256 * 18, [SMEM],
    )
    mid, sent = call(
        midpoint_kernel, "midpoint", [whole, tile],
        (state, speeds, partial, first, second, packed, from_other, deposit), [planes],
    )
    from_other = swap_halves(sent)
    (advanced,) = call(
        advance_kernel, "advance", [whole], (state, speeds, mid, first, second, deposit), [pads]
    )
    outs = call(
        finish_kernel, "finish", [(4, 64, 128)] * 3, (advanced, first, second, sent, from_other), [planes]
    )
    return (*outs, finished[None, None])


def solution(mesh):
    return jax.shard_map(
        on_device,
        mesh=mesh,
        in_specs=(
            P("brick", None, "grp"),
            P("brick", None, "grp"),
            P("brick", None, "grp"),
            P(None, "brick", None, "grp"),
            P("grp", "brick", None, None),
            P("grp", "brick", None),
            P("grp", "brick", None),
            P("grp", "brick"),
            P(),
            P(),
            P(),
            P(),
        ),
        out_specs=(
            P("brick", None, "grp"),
            P("brick", None, "grp"),
            P("brick", None, "grp"),
            P("grp", "brick", None, None),
        ),
        check_vma=False,
    )
```

time: 36.8 us -> 30.7 us (0.83)
  starting transfers between devices: 20.9 us -> 13.3 us
  waiting for transfers between devices: 0.38 us -> 4.58 us
  local copies, waits for them, and re-layouts: 4.43 us -> 0.66 us
  Pallas kernels: 9.35 us -> 10.6 us
    ppermute x6 -> x4, starting transfers between devices: 20.9 us -> 13.3 us  [the longest x1 9.05 us: swap_pairs(): lax.ppermute(second, 'brick', odd)]
    ppermute x6 -> x4, waiting for transfers between devices: 0.38 us -> 4.58 us  [the longest x1 4.57 us: swap_pairs(): lax.ppermute(second, 'brick', odd)]
    unnamed x30 -> x14, local copies, waits for them, and re-layouts: 4.43 us -> 0.66 us
    pallas_call x5, Pallas kernels: 9.35 us -> 10.6 us  [call(): pl.pallas_call(kernel, name=name, out_shape=[jax.ShapeDtypeStruct(o, F32)...]
  transfers between devices with their start and end apart: 6 -> 4, of which waited for: 1 -> 1; matrix products, arithmetic and copies ran while one was open for 0% -> 0% of each run, Pallas kernels for 15% -> 21%
where the time goes in v1:
time: 30.7 us; the launch traced here: 30.6 us
  starting transfers between devices  13.3 us (43%)
  Pallas kernels  10.6 us (35%)
  waiting for transfers between devices  4.58 us (15%)
  between operations  1.4 us (5%)
  local copies, waits for them, and re-layouts  0.66 us (2%)
    pallas_call x5, Pallas kernels, call(): pl.pallas_call(kernel, name=name, out_shape=[jax.ShapeDtypeStruct(o, F32)...  10.6 us
    ppermute x1, starting transfers between devices, swap_pairs(): lax.ppermute(second, 'brick', odd)  9.05 us
    ppermute x1, waiting for transfers between devices, swap_pairs(): lax.ppermute(second, 'brick', odd)  4.57 us
    ppermute x2, starting transfers between devices, swap_halves(): lax.ppermute(packed, 'grp', [(i, (i + 1) % halves) for i in range(halves)])  4.29 us
    unnamed x14, local copies, waits for them, and re-layouts  0.66 us
  transfers between devices with their start and end apart: 4, of which 1 were waited for; matrix products, arithmetic and copies ran while one was open for 0% of the time, Pallas kernels for 21%

profile of v1, /device:TPU:1, one launch (start us, length us, event | category | flops | bytes accessed | tf_op | source)
XLA Modules:
  0.0 30.6 jit_solution(4081968977123414984)
XLA Ops:
  0.6 0.0 copy-start.2
  0.6 0.0 copy-start.1
  0.7 0.0 copy-start
  0.7 2.6 %edges.1 = (f32[3,4,64,128]{3,2,1,0:T(8,128)S(1)}, f32[3,4,64,128]{3,2,1,0:T(8,128)S(1)}, f32[3,4,64,128]{3,2,1,0:T(8,128)S(1)}, f32[15,64,128]{2,1,0:T(8,128)S(...) custom-call(f32[4,64,128]{2,1,0:T(8,128)} %density.1, f32[4,64,128]{2,1,0:T(8,128)} %energy.1, ...), custom_call_target="tpu_custom_call" | custom-call | bytes 2981888 | tf_op jit(solution)/shard_map/edges/pallas_call | solution.py:344
  3.3 3.3 %collective-permute-start.2 = (f32[64,128]{1,0:T(8,128)S(1)}, f32[64,128]{1,0:T(8,128)S(1)}, u32[]{:S(2)}, u32[]{:S(2)}) collective-permute-start(f32[64,128]{1,0:T(8,128)S(1)} %get-tuple-element.22.packed), channel_id=1, source_target_pairs={{0,128},{128,0},{1,129},{129,1},{2,130},{130,2},{3,131},{131,3},{4... | collective-permute-start | bytes 98312 | tf_op jit(solution)/shard_map/ppermute | solution.py:358
  6.6 0.0 collective-permute-start
  6.6 9.0 %collective-permute-start.1 = (f32[15,64,128]{2,1,0:T(8,128)S(1)}, f32[15,64,128]{2,1,0:T(8,128)S(1)}, u32[]{:S(2)}, u32[]{:S(2)}) collective-permute-start(f32[15,64,128]{2,1,0:T(8,128)S(1)} %get-tuple-element.21), channel_id=1, source_target_pairs={{0,127},{1,2},{2,1},{3,4},{4,3},{5,6},{6,5},{7,8},{8,7},{9,10},{10... | collective-permute-start | bytes 1474568 | tf_op jit(solution)/shard_map/ppermute | solution.py:365
  16.3 0.0 copy-start.4
  16.3 0.0 copy-start.3
  16.3 0.0 copy-start.5
  16.4 0.0 copy-start.6
  16.4 0.0 copy-done.2
  16.4 0.6 %copy-done.4 = f32[1,1,1024]{2,1,0:T(1,128)S(1)} copy-done((f32[1,1,1024]{2,1,0:T(1,128)S(1)}, f32[1,1,1024]{2,1,0:T(1,128)}, u32[]{:S(2)}) %copy-start.4) | copy-done | bytes 4120
  17.0 0.0 copy-done.3
  17.0 0.0 copy-done.5
  17.0 5.4 %network.1 = (f32[1024,128]{1,0:T(8,128)}, f32[2,256,128]{2,1,0:T(8,128)S(1)}) custom-call(s32[1,1]{1,0:T(1,128)S(6)} %copy.16.count, f32[3,4,64,128]{3,2,1,0:T(8,128)S(1)} %get-tuple-element.17.state, s32[8,128]{1,0:T(8,128)S(1)} %bitcast.7, f32[1024,128]{1,0:T(8,128)S(1)} %bitcast.6, f32[128,128]{1,0:T(8,128)S(1)} %copy-done.1, f32[128,128]{1,0:T(8,128)S(1)} %copy-done.2, ...), custom_call_target="tpu_custom_call" | custom-call | flops 7247757312 | bytes 1844228 | tf_op jit(solution)/shard_map/network/pallas_call | solution.py:344
  22.4 0.0 collective-permute-done.2.from_other
  22.4 0.0 collective-permute-done.first
  22.4 4.6 %collective-permute-done.1.second = f32[15,64,128]{2,1,0:T(8,128)S(1)} collective-permute-done((f32[15,64,128]{2,1,0:T(8,128)S(1)}, f32[15,64,128]{2,1,0:T(8,128)S(1)}, u32[]{:S(2)}, u32[]{:S(2)}) %collective-permute-start.1) | collective-permute-done | bytes 491552 | tf_op jit(solution)/shard_map/ppermute | solution.py:365
  27.0 0.6 %midpoint.1 = (f32[3,4,64,128]{3,2,1,0:T(8,128)S(1)}, f32[64,128]{1,0:T(8,128)S(1)}) custom-call(f32[3,4,64,128]{3,2,1,0:T(8,128)S(1)} %get-tuple-element.17.state, f32[3,4,64,128]{3,2,1,0:T(8,128)S(1)} %get-tuple-element.18.velocity, f32[3,4,64,128]{3,2,1,0:T(8,128)S(1)} %get-tuple-element.19.partial, f32[15,64,128]{2,1,0:T(8,128)S(1)} %collective-permute-done.first, ...), custom_call_target="tpu_custom_call" | custom-call | bytes 2916352 | tf_op jit(solution)/shard_map/midpoint/pallas_call | solution.py:344
  27.5 1.0 %collective-permute-start.3 = (f32[64,128]{1,0:T(8,128)S(1)}, f32[64,128]{1,0:T(8,128)S(1)}, u32[]{:S(2)}, u32[]{:S(2)}) collective-permute-start(f32[64,128]{1,0:T(8,128)S(1)} %get-tuple-element.25.sent), channel_id=1, source_target_pairs={{0,128},{128,0},{1,129},{129,1},{2,130},{130,2},{3,131},{131,3},{4... | collective-permute-start | bytes 98312 | tf_op jit(solution)/shard_map/ppermute | solution.py:358
  28.5 1.0 %advance.1.advanced = f32[3,4,64,128]{3,2,1,0:T(8,128)S(1)} custom-call(f32[3,4,64,128]{3,2,1,0:T(8,128)S(1)} %get-tuple-element.17.state, f32[3,4,64,128]{3,2,1,0:T(8,128)S(1)} %get-tuple-element.18.velocity, f32[3,4,64,128]{3,2,1,0:T(8,128)S(1)} %get-tuple-element.24.mid, f32[15,64,128]{2,1,0:T(8,128)S(1)} %collective-permute-done.first, ...), custom_call_target="tpu_custom_call" | custom-call | bytes 2818048 | tf_op jit(solution)/shard_map/advance/pallas_call | solution.py:344
  29.5 0.0 collective-permute-done.3.from_other
  29.5 1.1 %finish.1 = (f32[4,64,128]{2,1,0:T(8,128)}, f32[4,64,128]{2,1,0:T(8,128)}, f32[4,64,128]{2,1,0:T(8,128)}) custom-call(f32[3,4,64,128]{3,2,1,0:T(8,128)S(1)} %advance.1.advanced, f32[15,64,128]{2,1,0:T(8,128)S(1)} %collective-permute-done.first, f32[15,64,128]{2,1,0:T(8,128)S(1)} %collective-permute-done.1.second, f32[64,128]{1,0:T(8,128)S(1)} %get-tuple-element.25.sent, ...), custom_call_target="tpu_custom_call" | custom-call | bytes 1835008 | tf_op jit(solution)/shard_map/finish/pallas_call | solution.py:344
  (3 shorter events, 0.0 us)
Async XLA Ops:
  0.6 15.7 %copy-start.2 = (f32[128,128]{1,0:T(8,128)S(1)}, f32[128,128]{1,0:T(8,128)}, u32[]{:S(2)}) copy-start(f32[128,128]{1,0:T(8,128)} %capture.1) | copy-start | bytes 196612
  0.6 15.7 %copy-start.1 = (f32[128,128]{1,0:T(8,128)S(1)}, f32[128,128]{1,0:T(8,128)}, u32[]{:S(2)}) copy-start(f32[128,128]{1,0:T(8,128)} %weak.1) | copy-start | bytes 196612
  0.7 15.7 %copy-start = (f32[1,1,1024,128]{3,2,1,0:T(8,128)S(1)}, f32[1,1,1024,128]{3,2,1,0:T(8,128)}, u32[]{:S(2)}) copy-start(f32[1,1,1024,128]{3,2,1,0:T(8,128)} %param.16) | copy-start | bytes 1572868
  3.3 19.1 %collective-permute-start.2 = (f32[64,128]{1,0:T(8,128)S(1)}, f32[64,128]{1,0:T(8,128)S(1)}, u32[]{:S(2)}, u32[]{:S(2)}) collective-permute-start(f32[64,128]{1,0:T(8,128)S(1)} %get-tuple-element.22.packed), channel_id=1, source_target_pairs={{0,128},{128,0},{1,129},{129,1},{2,130},{130,2},{3,131},{131,3},{4... | collective-permute-start | bytes 98312 | tf_op jit(solution)/shard_map/ppermute | solution.py:358
  6.6 15.8 %collective-permute-start = (f32[15,64,128]{2,1,0:T(8,128)S(1)}, f32[15,64,128]{2,1,0:T(8,128)S(1)}, u32[]{:S(2)}, u32[]{:S(2)}) collective-permute-start(f32[15,64,128]{2,1,0:T(8,128)S(1)} %get-tuple-element.20), channel_id=1, source_target_pairs={{0,1},{1,0},{2,3},{3,2},{4,5},{5,4},{6,7},{7,6},{8,9},{9,8},{10,11... | collective-permute-start | bytes 1474568 | tf_op jit(solution)/shard_map/ppermute | solution.py:365
  6.6 20.4 %collective-permute-start.1 = (f32[15,64,128]{2,1,0:T(8,128)S(1)}, f32[15,64,128]{2,1,0:T(8,128)S(1)}, u32[]{:S(2)}, u32[]{:S(2)}) collective-permute-start(f32[15,64,128]{2,1,0:T(8,128)S(1)} %get-tuple-element.21), channel_id=1, source_target_pairs={{0,127},{1,2},{2,1},{3,4},{4,3},{5,6},{6,5},{7,8},{8,7},{9,10},{10... | collective-permute-start | bytes 1474568 | tf_op jit(solution)/shard_map/ppermute | solution.py:365
  16.3 0.7 %copy-start.4 = (f32[1,1,1024]{2,1,0:T(1,128)S(1)}, f32[1,1,1024]{2,1,0:T(1,128)}, u32[]{:S(2)}) copy-start(f32[1,1,1024]{2,1,0:T(1,128)} %param.17) | copy-start | bytes 12292
  16.3 0.7 %copy-start.3 = (s32[1,1,1024]{2,1,0:T(1,128)S(1)}, s32[1,1,1024]{2,1,0:T(1,128)}, u32[]{:S(2)}) copy-start(s32[1,1,1024]{2,1,0:T(1,128)} %param.18) | copy-start | bytes 12292
  16.3 0.7 %copy-start.5 = (f32[128]{0:T(128)S(1)}, f32[128]{0:T(128)}, u32[]{:S(2)}) copy-start(f32[128]{0:T(128)} %param.22) | copy-start | bytes 1540
  16.4 0.7 %copy-start.6 = (f32[128]{0:T(128)S(1)}, f32[128]{0:T(128)}, u32[]{:S(2)}) copy-start(f32[128]{0:T(128)} %param.23) | copy-start | bytes 1540
  27.5 1.9 %collective-permute-start.3 = (f32[64,128]{1,0:T(8,128)S(1)}, f32[64,128]{1,0:T(8,128)S(1)}, u32[]{:S(2)}, u32[]{:S(2)}) collective-permute-start(f32[64,128]{1,0:T(8,128)S(1)} %get-tuple-element.25.sent), channel_id=1, source_target_pairs={{0,128},{128,0},{1,129},{129,1},{2,130},{130,2},{3,131},{131,3},{4... | collective-permute-start | bytes 98312 | tf_op jit(solution)/shard_map/ppermute | solution.py:358

commit v2 on v1

--- a/solution.py
+++ b/solution.py
@@ -30,10 +30,31 @@
     return lax.broadcasted_iota(jnp.int32, (rows, 128), 1)
 
 
-def pack_z(packed, tile, first, lane):
-    moved = pltpu.roll(tile, first + 2, 1)
-    inside = jnp.logical_and(lane >= first, lane < first + 4)
-    return jnp.where(inside, moved, packed)
+def groups():
+    return lax.shift_right_logical(lanes(), 2)
+
+
+def spreading():
+    row = lax.broadcasted_iota(jnp.int32, (128, 128), 0)
+    source = jnp.bitwise_and(126 + jnp.bitwise_and(lanes(128), 3), 127)
+    return jnp.where(row == source, 1.0, 0.0)
+
+
+def circulant():
+    row = lax.broadcasted_iota(jnp.int32, (128, 128), 0)
+    offset = jnp.bitwise_and(row - lanes(128), 127)
+    near = jnp.where(offset == 1, 8.0, jnp.where(offset == 127, -8.0, 0.0))
+    return jnp.where(offset == 2, -1.0, jnp.where(offset == 126, 1.0, near))
+
+
+def twice(matrix):
+    matrix = matrix.astype(BF16)
+    return jnp.concatenate([matrix, matrix], axis=0)
+
+
+def parts(values):
+    high, low = split(values)
+    return jnp.concatenate([high, low], axis=1)
 
 
 def unpack_z(packed, first, lane):
@@ -50,12 +71,6 @@
     return far + 8.0 * near
 
 
-def along_z(tile):
-    after = 8.0 * tile - pltpu.roll(tile, 127, 1)
-    before = 8.0 * tile - pltpu.roll(tile, 1, 1)
-    return pltpu.roll(after, 127, 1) - pltpu.roll(before, 1, 1)
-
-
 def along_y(tile, pad):
     pad[pl.ds(8, 64), :] = tile
     pad[pl.ds(0, 8), :] = tile[56:]
@@ -65,7 +80,9 @@
     )
 
 
-def inner_differences(get, velocity, pads, f):
+def inner_differences(get, velocity, pads, f, weights):
+    speed_z = [parts(velocity[2, i] * get(i)) for i in range(4)]
+    along_z = matmul(jnp.concatenate(speed_z, axis=0), weights)
     for i in range(4):
         plane = [velocity[0, j] * get(j) for j in range(4) if 0 < abs(j - i) < 3]
         if i == 0:
@@ -77,7 +94,8 @@
         else:
             total = plane[0] - 8.0 * plane[1]
         total = total + along_y(velocity[1, i] * get(i), pads.at[4 * f + i])
-        yield i, total + along_z(velocity[2, i] * get(i))
+        here = along_z[64 * i : 64 * i + 64]
+        yield i, total + here[:, :128], here[:, 128:]
 
 
 def sides():
@@ -89,36 +107,50 @@
     )
 
 
+def rows_of_tile(number):
+    return pl.ds(64 * number, 64)
+
+
 def edges_kernel(
-    density, energy, lepton, speeds, state, velocity, partial, first, second, packed, pads, sems
+    density, energy, lepton, speeds,
+    state, velocity, partial, first, second, packed,
+    pads, spread, sems,
 ):
+    wait_speeds = pltpu.make_async_copy(speeds, velocity, sems.at[3])
+    wait_speeds.start()
     copies = [
         pltpu.make_async_copy(ref, state.at[f], sems.at[f])
         for f, ref in enumerate((density, energy, lepton))
     ]
-    copies.append(pltpu.make_async_copy(speeds, velocity, sems.at[3]))
     for copy in copies:
         copy.start()
-    for copy in copies:
-        copy.wait()
-    lane = lanes()
+    weights = twice(jnp.concatenate([circulant(), spreading()], axis=1))
+    group = groups()
     pack = jnp.zeros((64, 128), F32)
+    wait_speeds.wait()
     for f in range(3):
-        for i, total in inner_differences(lambda i: state[f, i], velocity, pads, f):
+        copies[f].wait()
+        for i, total, edge in inner_differences(
+            lambda i: state[f, i], velocity, pads, f, weights
+        ):
             partial[f, i] = total
-            pack = pack_z(pack, velocity[2, i] * state[f, i], 4 * (4 * f + i), lane)
+            spread[f, i] = edge
+            pack = jnp.where(group == 4 * f + i, edge, pack)
     packed[...] = pack
-    for (near, far, _), out, start in zip(sides(), (first, second), (48, 72)):
-        pack = jnp.zeros((64, 128), F32)
+    group = group[:32]
+    for (near, far, _), out in zip(sides(), (first, second)):
+        pack = jnp.zeros((32, 128), F32)
         for k, plane in enumerate((near, far)):
             speed = velocity[0, plane]
-            out[12 + k] = speed
+            out[rows_of_tile(12 + k), :] = speed
             for f in range(3):
                 value = state[f, plane]
-                out[2 * f + k] = speed * value
-                out[6 + 2 * f + k] = speed * (value - HALF * partial[f, plane])
-                pack = pack_z(pack, velocity[2, plane] * value, start + 4 * (2 * f + k), lane)
-        out[14] = pack
+                out[rows_of_tile(2 * f + k), :] = speed * value
+                out[rows_of_tile(6 + 2 * f + k), :] = speed * (value - HALF * partial[f, plane])
+                place = 4 * f + 3 - plane
+                pack = jnp.where(group == place, spread[f, plane, pl.ds(0, 32), :], pack)
+                pack = jnp.where(group == place + 16, spread[f, plane, pl.ds(32, 32), :], pack)
+        out[pl.ds(64 * 14, 32), :] = pack
 
 
 def midpoint_kernel(
@@ -126,24 +158,42 @@
 ):
     lane = lanes()
     correction = edge_correction(from_other[...], packed[...], lane)
+    group = groups()
+    weights = twice(spreading())
+    pack = jnp.zeros((64, 128), F32)
     for f in range(3):
         for i in range(4):
             total[i] = partial[f, i] + unpack_z(correction, 4 * (4 * f + i), lane)
         for (near, far, sign), side in zip(sides(), (first, second)):
-            total[near] += sign * (8.0 * side[2 * f] - side[2 * f + 1])
-            total[far] += -sign * side[2 * f]
+            close = side[rows_of_tile(2 * f), :]
+            total[near] += sign * (8.0 * close - side[rows_of_tile(2 * f + 1), :])
+            total[far] += -sign * close
+        speed_z = []
         for i in range(4):
-            mid[f, i] = state[f, i] - HALF * total[i]
-    pack = jnp.where(lane < 72, first[14], second[14])
+            value = state[f, i] - HALF * total[i]
+            mid[f, i] = value
+            speed_z.append(parts(velocity[2, i] * value))
+        edge = matmul(jnp.concatenate(speed_z, axis=0), weights)
+        for i in range(4):
+            pack = jnp.where(group == 4 * f + i, edge[64 * i : 64 * i + 64], pack)
+    exchanged[pl.ds(0, 64), :] = pack
+    odd = jnp.bitwise_and(lax.axis_index("brick"), 1)
+    upper = jnp.bitwise_and(lax.shift_right_logical(group[:32], 1), 1)
+    folded = jnp.where(
+        upper != odd, first[pl.ds(64 * 14, 32), :], second[pl.ds(64 * 14, 32), :]
+    )
+    exchanged[pl.ds(64, 32), :] = folded
+    exchanged[pl.ds(96, 32), :] = pltpu.roll(
+        jnp.where(upper != odd, first[pl.ds(64 * 14, 32), :], second[pl.ds(64 * 14, 32), :]), 64, 1
+    )
+
+
+def advance_kernel(
+    state, velocity, mid, first, second, deposit, advanced, edge_speed, pads
+):
+    weights = twice(circulant())
     for f in range(3):
-        for i in range(4):
-            pack = pack_z(pack, velocity[2, i] * mid[f, i], 4 * (4 * f + i), lane)
-    exchanged[...] = pack
-
-
-def advance_kernel(state, velocity, mid, first, second, deposit, advanced, pads):
-    for f in range(3):
-        for i, total in inner_differences(lambda i: mid[f, i], velocity, pads, f):
+        for i, total, _ in inner_differences(lambda i: mid[f, i], velocity, pads, f, weights):
             value = state[f, i] - FULL * total
             if f > 0:
                 value = value + deposit[f - 1, pl.ds(64 * i, 64), :]
@@ -152,29 +202,42 @@
             here = velocity[0, near] * state[f, near]
             behind = velocity[0, far] * state[f, far]
             step = sign * HALF
-            close = side[6 + 2 * f] + step * (side[12] * (8.0 * here - behind))
-            remote = side[7 + 2 * f] - step * (side[13] * here)
+            speed, speed_far = side[rows_of_tile(12), :], side[rows_of_tile(13), :]
+            close = side[rows_of_tile(6 + 2 * f), :] + step * (speed * (8.0 * here - behind))
+            remote = side[rows_of_tile(7 + 2 * f), :] - step * (speed_far * here)
             advanced[f, near] += (-FULL * sign) * (8.0 * close - remote)
             advanced[f, far] += (FULL * sign) * close
+    weights = twice(spreading())
+    plane = jnp.bitwise_and(groups(), 3)
+    pack = jnp.zeros((64, 128), F32)
+    for (near, far, _), side in zip(sides(), (first, second)):
+        for k, number in enumerate((near, far)):
+            edge = matmul(parts(side[rows_of_tile(12 + k), :]), weights)
+            pack = jnp.where(plane == number, edge, pack)
+    edge_speed[...] = pack
 
 
 def finish_kernel(
-    advanced, first, second, sent, from_other, density_out, energy_out, lepton_out, total
+    advanced, edge_speed, sent, from_other, density_out, energy_out, lepton_out, result, sems
 ):
     lane = lanes()
-    correction = edge_correction(from_other[...], sent[...], lane)
-    outs = (density_out, energy_out, lepton_out)
-    for f in range(3):
+    own, side = pl.ds(0, 64), pl.ds(64, 64)
+    correction = edge_correction(from_other[own, :], sent[own, :], lane)
+    moved = edge_correction(from_other[side, :], sent[side, :], lane)
+    moved = HALF * (edge_speed[...] * moved)
+    before, after = pltpu.roll(moved, 4, 1), pltpu.roll(moved, 124, 1)
+    plane = jnp.bitwise_and(groups(), 3)
+    low = jnp.where(plane == 0, 8.0 * moved - after, -before)
+    high = jnp.where(plane == 2, after, before - 8.0 * moved)
+    correction = FULL * (correction + jnp.where(plane < 2, low, high))
+    copies = []
+    for f, out in enumerate((density_out, energy_out, lepton_out)):
         for i in range(4):
-            total[i] = unpack_z(correction, 4 * (4 * f + i), lane)
-        for (near, far, sign), side, start in zip(sides(), (first, second), (48, 72)):
-            start = start + 8 * f
-            close = (sign * HALF) * (side[12] * unpack_z(correction, start, lane))
-            remote = (sign * HALF) * (side[13] * unpack_z(correction, start + 4, lane))
-            total[near] += remote - 8.0 * close
-            total[far] += close
-        for i in range(4):
-            outs[f][i] = advanced[f, i] - FULL * total[i]
+            result[f, i] = advanced[f, i] - unpack_z(correction, 4 * (4 * f + i), lane)
+        copies.append(pltpu.make_async_copy(result.at[f], out, sems.at[f]))
+        copies[f].start()
+    for copy in copies:
+        copy.wait()
 
 
 def column(row):
@@ -335,7 +398,7 @@
 HBM = pl.BlockSpec(memory_space=pltpu.HBM)
 
 
-def call(kernel, name, outs, args, scratch=(), flops=0, first=()):
+def call(kernel, name, outs, args, scratch=(), flops=0, first=(), out=VMEM):
     args = [
         pltpu.with_memory_space_constraint(a, pltpu.HBM) if s is HBM else a
         for a, s in zip(args, list(first) + [None] * len(args))
@@ -346,7 +409,7 @@
         name=name,
         out_shape=[jax.ShapeDtypeStruct(o, F32) for o in outs],
         in_specs=list(first) + [VMEM] * (len(args) - len(first)),
-        out_specs=[VMEM] * len(outs),
+        out_specs=[out] * len(outs),
         scratch_shapes=list(scratch),
         compiler_params=pltpu.CompilerParams(vmem_limit_bytes=24 * 2**20),
         cost_estimate=pl.CostEstimate(flops=flops, bytes_accessed=moved, transcendentals=0),
@@ -380,15 +443,14 @@
     charge_ratio,
 ):
     fields = (density, energy_field, lepton_field)
-    whole, side, tile = (3, 4, 64, 128), (15, 64, 128), (64, 128)
+    whole, side, tile = (3, 4, 64, 128), (928, 128), (64, 128)
     pads = pltpu.VMEM((12, 80, 128), F32)
     planes = pltpu.VMEM((4, 64, 128), F32)
     state, speeds, partial, first, second, packed = call(
         edges_kernel, "edges", [whole, whole, whole, side, side, tile], (*fields, velocity),
-        [pads, pltpu.SemaphoreType.DMA((4,))], 0, [HBM] * 4,
+        [pads, pltpu.VMEM(whole, F32), pltpu.SemaphoreType.DMA((4,))], 0, [HBM] * 4,
     )
     first, second = swap_pairs(first, second)
-    from_other = swap_halves(packed)
 
     rows = pltpu.VMEM((CHUNK, 128), F32)
     matrices = [pltpu.VMEM((256, 256), BF16), pltpu.VMEM((128, 256), BF16)]
@@ -403,16 +465,19 @@
         + [rows] * 6 + matrices,
         6 * 2 * 1024 * 128 * 256 * 18, [SMEM],
     )
+    packed, deposit = lax.optimization_barrier((packed, deposit))
+    from_other = swap_halves(packed)
     mid, sent = call(
-        midpoint_kernel, "midpoint", [whole, tile],
+        midpoint_kernel, "midpoint", [whole, (128, 128)],
         (state, speeds, partial, first, second, packed, from_other, deposit), [planes],
     )
     from_other = swap_halves(sent)
-    (advanced,) = call(
-        advance_kernel, "advance", [whole], (state, speeds, mid, first, second, deposit), [pads]
+    advanced, edge_speed = call(
+        advance_kernel, "advance", [whole, tile], (state, speeds, mid, first, second, deposit), [pads]
     )
     outs = call(
-        finish_kernel, "finish", [(4, 64, 128)] * 3, (advanced, first, second, sent, from_other), [planes]
+        finish_kernel, "finish", [(4, 64, 128)] * 3, (advanced, edge_speed, sent, from_other),
+        [pltpu.VMEM(whole, F32), pltpu.SemaphoreType.DMA((3,))], 0, (), pl.BlockSpec(memory_space=pl.ANY),
     )
     return (*outs, finished[None, None])
 

time: 30.7 us -> 28.8 us (0.938)
  waiting for transfers between devices: 4.58 us -> 2.55 us
  starting transfers between devices: 13.3 us -> 14.5 us
  Pallas kernels: 10.6 us -> 9.52 us
    ppermute x1, waiting for transfers between devices: 4.57 us -> 1.44 us  [swap_pairs(): lax.ppermute(second, 'brick', odd)]
    ppermute x1, starting transfers between devices: 0.01 us -> 2.13 us  [swap_pairs(): lax.ppermute(first, 'brick', even)]
    ppermute x2, starting transfers between devices: 4.29 us -> 2.86 us  [swap_halves(): lax.ppermute(packed, 'grp', [(i, (i + 1) % halves) for i in range(halves)])]
    ppermute x2, waiting for transfers between devices: 0.01 us -> 1.11 us  [swap_halves(): lax.ppermute(packed, 'grp', [(i, (i + 1) % halves) for i in range(halves)])]
    pallas_call x5, Pallas kernels: 10.6 us -> 9.52 us  [call(): pl.pallas_call(kernel, name=name, out_shape=[jax.ShapeDtypeStruct(o, F32)...]
    ppermute x1, starting transfers between devices: 9.05 us -> 9.56 us  [swap_pairs(): lax.ppermute(second, 'brick', odd)]
  transfers between devices with their start and end apart: 4 -> 4, of which waited for: 1 -> 3; matrix products, arithmetic and copies ran while one was open for 0% -> 0% of each run, Pallas kernels for 21% -> 21%
where the time goes in v2:
time: 28.8 us; the launch traced here: 28.7 us
  starting transfers between devices  14.5 us (50%)
  Pallas kernels  9.52 us (33%)
  waiting for transfers between devices  2.55 us (9%)
  between operations  1.39 us (5%)
  local copies, waits for them, and re-layouts  0.66 us (2%)
    ppermute x1, starting transfers between devices, swap_pairs(): lax.ppermute(second, 'brick', odd)  9.56 us
    pallas_call x5, Pallas kernels, call(): pl.pallas_call(kernel, name=name, out_shape=[jax.ShapeDtypeStruct(o, F32)...  9.52 us
    ppermute x2, starting transfers between devices, swap_halves(): lax.ppermute(packed, 'grp', [(i, (i + 1) % halves) for i in range(halves)])  2.86 us
    ppermute x1, starting transfers between devices, swap_pairs(): lax.ppermute(first, 'brick', even)  2.13 us
    ppermute x1, waiting for transfers between devices, swap_pairs(): lax.ppermute(second, 'brick', odd)  1.44 us
    ppermute x2, waiting for transfers between devices, swap_halves(): lax.ppermute(packed, 'grp', [(i, (i + 1) % halves) for i in range(halves)])  1.11 us
    unnamed x14, local copies, waits for them, and re-layouts  0.66 us
  transfers between devices with their start and end apart: 4, of which 3 were waited for; matrix products, arithmetic and copies ran while one was open for 0% of the time, Pallas kernels for 21%

profile of v2, /device:TPU:1, one launch (start us, length us, event | category | flops | bytes accessed | tf_op | source)
XLA Modules:
  0.0 28.7 jit_solution(9394055908388123164)
XLA Ops:
  0.6 0.0 copy-start.2
  0.6 0.0 copy-start.1
  0.7 0.0 copy-start
  0.7 1.9 %edges.1 = (f32[3,4,64,128]{3,2,1,0:T(8,128)S(1)}, f32[3,4,64,128]{3,2,1,0:T(8,128)S(1)}, f32[3,4,64,128]{3,2,1,0:T(8,128)S(1)}, f32[928,128]{1,0:T(8,128)S(1)},...) custom-call(f32[4,64,128]{2,1,0:T(8,128)} %density.1, f32[4,64,128]{2,1,0:T(8,128)} %energy.1, f32[4,64,128]{2,1,0:T(8,128)} %lepton.1, ...), custom_call_target="tpu_custom_call" | custom-call | bytes 2949120 | tf_op jit(solution)/shard_map/edges/pallas_call | solution.py:407
  2.5 2.1 %collective-permute-start = (f32[928,128]{1,0:T(8,128)S(1)}, f32[928,128]{1,0:T(8,128)S(1)}, u32[]{:S(2)}, u32[]{:S(2)}) collective-permute-start(f32[928,128]{1,0:T(8,128)S(1)} %get-tuple-element.24), channel_id=1, source_target_pairs={{0,1},{1,0},{2,3},{3,2},{4,5},{5,4},{6,7},{7,6},{8,9},{9,8},{10,11... | collective-permute-start | bytes 1425416 | tf_op jit(solution)/shard_map/ppermute | solution.py:428
  4.7 9.6 %collective-permute-start.1 = (f32[928,128]{1,0:T(8,128)S(1)}, f32[928,128]{1,0:T(8,128)S(1)}, u32[]{:S(2)}, u32[]{:S(2)}) collective-permute-start(f32[928,128]{1,0:T(8,128)S(1)} %get-tuple-element.25), channel_id=1, source_target_pairs={{0,127},{1,2},{2,1},{3,4},{4,3},{5,6},{6,5},{7,8},{8,7},{9,10},{10... | collective-permute-start | bytes 1425416 | tf_op jit(solution)/shard_map/ppermute | solution.py:428
  14.9 0.0 copy-start.4
  14.9 0.0 copy-start.3
  14.9 0.0 copy-start.5
  14.9 0.0 copy-start.6
  14.9 0.0 copy-done.2
  14.9 0.6 %copy-done.4 = f32[1,1,1024]{2,1,0:T(1,128)S(1)} copy-done((f32[1,1,1024]{2,1,0:T(1,128)S(1)}, f32[1,1,1024]{2,1,0:T(1,128)}, u32[]{:S(2)}) %copy-start.4) | copy-done | bytes 4120
  15.6 0.0 copy-done.3
  15.6 0.0 copy-done.5
  15.6 5.4 %network.1 = (f32[1024,128]{1,0:T(8,128)}, f32[2,256,128]{2,1,0:T(8,128)S(1)}) custom-call(s32[1,1]{1,0:T(1,128)S(6)} %copy.16.count, f32[3,4,64,128]{3,2,1,0:T(8,128)S(1)} %get-tuple-element.21.state, s32[8,128]{1,0:T(8,128)S(1)} %bitcast.7, f32[1024,128]{1,0:T(8,128)S(1)} %bitcast.6, f32[128,128]{1,0:T(8,128)S(1)} %copy-done.1, f32[128,128]{1,0:T(8,128)S(1)} %copy-done.2, ...), custom_call_target="tpu_custom_call" | custom-call | flops 7247757312 | bytes 1844228 | tf_op jit(solution)/shard_map/network/pallas_call | solution.py:407
  21.0 1.2 %collective-permute-start.2 = (f32[64,128]{1,0:T(8,128)S(1)}, f32[64,128]{1,0:T(8,128)S(1)}, u32[]{:S(2)}, u32[]{:S(2)}) collective-permute-start(f32[64,128]{1,0:T(8,128)S(1)} %get-tuple-element.28.packed), channel_id=1, source_target_pairs={{0,128},{128,0},{1,129},{129,1},{2,130},{130,2},{3,131},{131,3},{4... | collective-permute-start | bytes 98312 | tf_op jit(solution)/shard_map/ppermute | solution.py:421
  22.2 0.9 %collective-permute-done.2.from_other = f32[64,128]{1,0:T(8,128)S(1)} collective-permute-done((f32[64,128]{1,0:T(8,128)S(1)}, f32[64,128]{1,0:T(8,128)S(1)}, u32[]{:S(2)}, u32[]{:S(2)}) %collective-permute-start.2) | collective-permute-done | bytes 32800 | tf_op jit(solution)/shard_map/ppermute | solution.py:421
  23.0 0.0 collective-permute-done.first
  23.0 1.4 %collective-permute-done.1.second = f32[928,128]{1,0:T(8,128)S(1)} collective-permute-done((f32[928,128]{1,0:T(8,128)S(1)}, f32[928,128]{1,0:T(8,128)S(1)}, u32[]{:S(2)}, u32[]{:S(2)}) %collective-permute-start.1) | collective-permute-done | bytes 475168 | tf_op jit(solution)/shard_map/ppermute | solution.py:428
  24.5 0.6 %midpoint.1 = (f32[3,4,64,128]{3,2,1,0:T(8,128)S(1)}, f32[128,128]{1,0:T(8,128)S(1)}) custom-call(f32[3,4,64,128]{3,2,1,0:T(8,128)S(1)} %get-tuple-element.21.state, f32[3,4,64,128]{3,2,1,0:T(8,128)S(1)} %get-tuple-element.22.velocity, f32[3,4,64,128]{3,2,1,0:T(8,128)S(1)} %get-tuple-element.23.partial, f32[928,128]{1,0:T(8,128)S(1)} %collective-permute-done.first, ...), custom_call_target="tpu_custom_call" | custom-call | bytes 2916352 | tf_op jit(solution)/shard_map/midpoint/pallas_call | solution.py:407
  25.1 1.6 %collective-permute-start.3 = (f32[128,128]{1,0:T(8,128)S(1)}, f32[128,128]{1,0:T(8,128)S(1)}, u32[]{:S(2)}, u32[]{:S(2)}) collective-permute-start(f32[128,128]{1,0:T(8,128)S(1)} %get-tuple-element.33.sent), channel_id=1, source_target_pairs={{0,128},{128,0},{1,129},{129,1},{2,130},{130,2},{3,131},{131,3},{4... | collective-permute-start | bytes 196616 | tf_op jit(solution)/shard_map/ppermute | solution.py:421
  26.7 0.6 %advance.1 = (f32[3,4,64,128]{3,2,1,0:T(8,128)S(1)}, f32[64,128]{1,0:T(8,128)S(1)}) custom-call(f32[3,4,64,128]{3,2,1,0:T(8,128)S(1)} %get-tuple-element.21.state, f32[3,4,64,128]{3,2,1,0:T(8,128)S(1)} %get-tuple-element.22.velocity, f32[3,4,64,128]{3,2,1,0:T(8,128)S(1)} %get-tuple-element.30.mid, f32[928,128]{1,0:T(8,128)S(1)} %collective-permute-done.first, ...), custom_call_target="tpu_custom_call" | custom-call | bytes 2818048 | tf_op jit(solution)/shard_map/advance/pallas_call | solution.py:407
  27.3 0.3 collective-permute-done.3.from_other
  27.6 1.1 %finish.1 = (f32[4,64,128]{2,1,0:T(8,128)}, f32[4,64,128]{2,1,0:T(8,128)}, f32[4,64,128]{2,1,0:T(8,128)}) custom-call(f32[3,4,64,128]{3,2,1,0:T(8,128)S(1)} %get-tuple-element.31.advanced, f32[64,128]{1,0:T(8,128)S(1)} %get-tuple-element.32.edge_speed, f32[128,128]{1,0:T(8,128)S(1)} %get-tuple-element.33.sent, f32[128,128]{1,0:T(8,128)S(1)} %collective-permute-done.3.from_other), custom_call_target="tpu_custom_call" | custom-call | bytes 950272 | tf_op jit(solution)/shard_map/finish/pallas_call | solution.py:407
  (3 shorter events, 0.0 us)
Async XLA Ops:
  0.6 14.3 %copy-start.2 = (f32[128,128]{1,0:T(8,128)S(1)}, f32[128,128]{1,0:T(8,128)}, u32[]{:S(2)}) copy-start(f32[128,128]{1,0:T(8,128)} %capture.1) | copy-start | bytes 196612
  0.6 14.3 %copy-start.1 = (f32[128,128]{1,0:T(8,128)S(1)}, f32[128,128]{1,0:T(8,128)}, u32[]{:S(2)}) copy-start(f32[128,128]{1,0:T(8,128)} %weak.1) | copy-start | bytes 196612
  0.7 14.3 %copy-start = (f32[1,1,1024,128]{3,2,1,0:T(8,128)S(1)}, f32[1,1,1024,128]{3,2,1,0:T(8,128)}, u32[]{:S(2)}) copy-start(f32[1,1,1024,128]{3,2,1,0:T(8,128)} %param.16) | copy-start | bytes 1572868
  2.5 20.5 %collective-permute-start = (f32[928,128]{1,0:T(8,128)S(1)}, f32[928,128]{1,0:T(8,128)S(1)}, u32[]{:S(2)}, u32[]{:S(2)}) collective-permute-start(f32[928,128]{1,0:T(8,128)S(1)} %get-tuple-element.24), channel_id=1, source_target_pairs={{0,1},{1,0},{2,3},{3,2},{4,5},{5,4},{6,7},{7,6},{8,9},{9,8},{10,11... | collective-permute-start | bytes 1425416 | tf_op jit(solution)/shard_map/ppermute | solution.py:428
  4.7 19.8 %collective-permute-start.1 = (f32[928,128]{1,0:T(8,128)S(1)}, f32[928,128]{1,0:T(8,128)S(1)}, u32[]{:S(2)}, u32[]{:S(2)}) collective-permute-start(f32[928,128]{1,0:T(8,128)S(1)} %get-tuple-element.25), channel_id=1, source_target_pairs={{0,127},{1,2},{2,1},{3,4},{4,3},{5,6},{6,5},{7,8},{8,7},{9,10},{10... | collective-permute-start | bytes 1425416 | tf_op jit(solution)/shard_map/ppermute | solution.py:428
  14.9 0.7 %copy-start.4 = (f32[1,1,1024]{2,1,0:T(1,128)S(1)}, f32[1,1,1024]{2,1,0:T(1,128)}, u32[]{:S(2)}) copy-start(f32[1,1,1024]{2,1,0:T(1,128)} %param.17) | copy-start | bytes 12292
  14.9 0.7 %copy-start.3 = (s32[1,1,1024]{2,1,0:T(1,128)S(1)}, s32[1,1,1024]{2,1,0:T(1,128)}, u32[]{:S(2)}) copy-start(s32[1,1,1024]{2,1,0:T(1,128)} %param.18) | copy-start | bytes 12292
  14.9 0.7 %copy-start.5 = (f32[128]{0:T(128)S(1)}, f32[128]{0:T(128)}, u32[]{:S(2)}) copy-start(f32[128]{0:T(128)} %param.22) | copy-start | bytes 1540
  14.9 0.7 %copy-start.6 = (f32[128]{0:T(128)S(1)}, f32[128]{0:T(128)}, u32[]{:S(2)}) copy-start(f32[128]{0:T(128)} %param.23) | copy-start | bytes 1540
  21.0 2.1 %collective-permute-start.2 = (f32[64,128]{1,0:T(8,128)S(1)}, f32[64,128]{1,0:T(8,128)S(1)}, u32[]{:S(2)}, u32[]{:S(2)}) collective-permute-start(f32[64,128]{1,0:T(8,128)S(1)} %get-tuple-element.28.packed), channel_id=1, source_target_pairs={{0,128},{128,0},{1,129},{129,1},{2,130},{130,2},{3,131},{131,3},{4... | collective-permute-start | bytes 98312 | tf_op jit(solution)/shard_map/ppermute | solution.py:421
  25.1 2.5 %collective-permute-start.3 = (f32[128,128]{1,0:T(8,128)S(1)}, f32[128,128]{1,0:T(8,128)S(1)}, u32[]{:S(2)}, u32[]{:S(2)}) collective-permute-start(f32[128,128]{1,0:T(8,128)S(1)} %get-tuple-element.33.sent), channel_id=1, source_target_pairs={{0,128},{128,0},{1,129},{129,1},{2,130},{130,2},{3,131},{131,3},{4... | collective-permute-start | bytes 196616 | tf_op jit(solution)/shard_map/ppermute | solution.py:421

commit v3 on v2

--- a/solution.py
+++ b/solution.py
@@ -98,13 +98,8 @@
         yield i, total + here[:, :128], here[:, 128:]
 
 
-def sides():
-    odd = jnp.bitwise_and(lax.axis_index("brick"), 1)
-    even = 1 - odd
-    return (
-        (3 * even, 1 + even, (1 - 2 * odd).astype(F32)),
-        (3 * odd, 1 + odd, (2 * odd - 1).astype(F32)),
-    )
+def sides(low, high):
+    return ((0, 1, -1.0, low), (3, 2, 1.0, high))
 
 
 def rows_of_tile(number):
@@ -138,7 +133,7 @@
             pack = jnp.where(group == 4 * f + i, edge, pack)
     packed[...] = pack
     group = group[:32]
-    for (near, far, _), out in zip(sides(), (first, second)):
+    for near, far, out in ((3, 2, first), (0, 1, second)):
         pack = jnp.zeros((32, 128), F32)
         for k, plane in enumerate((near, far)):
             speed = velocity[0, plane]
@@ -164,7 +159,7 @@
     for f in range(3):
         for i in range(4):
             total[i] = partial[f, i] + unpack_z(correction, 4 * (4 * f + i), lane)
-        for (near, far, sign), side in zip(sides(), (first, second)):
+        for near, far, sign, side in sides(first, second):
             close = side[rows_of_tile(2 * f), :]
             total[near] += sign * (8.0 * close - side[rows_of_tile(2 * f + 1), :])
             total[far] += -sign * close
@@ -177,15 +172,11 @@
         for i in range(4):
             pack = jnp.where(group == 4 * f + i, edge[64 * i : 64 * i + 64], pack)
     exchanged[pl.ds(0, 64), :] = pack
-    odd = jnp.bitwise_and(lax.axis_index("brick"), 1)
-    upper = jnp.bitwise_and(lax.shift_right_logical(group[:32], 1), 1)
-    folded = jnp.where(
-        upper != odd, first[pl.ds(64 * 14, 32), :], second[pl.ds(64 * 14, 32), :]
-    )
+    edge = pl.ds(64 * 14, 32)
+    upper = jnp.bitwise_and(group[:32], 3) >= 2
+    folded = jnp.where(upper, second[edge, :], first[edge, :])
     exchanged[pl.ds(64, 32), :] = folded
-    exchanged[pl.ds(96, 32), :] = pltpu.roll(
-        jnp.where(upper != odd, first[pl.ds(64 * 14, 32), :], second[pl.ds(64 * 14, 32), :]), 64, 1
-    )
+    exchanged[pl.ds(96, 32), :] = pltpu.roll(folded, 64, 1)
 
 
 def advance_kernel(
@@ -198,7 +189,7 @@
             if f > 0:
                 value = value + deposit[f - 1, pl.ds(64 * i, 64), :]
             advanced[f, i] = value
-        for (near, far, sign), side in zip(sides(), (first, second)):
+        for near, far, sign, side in sides(first, second):
             here = velocity[0, near] * state[f, near]
             behind = velocity[0, far] * state[f, far]
             step = sign * HALF
@@ -210,7 +201,7 @@
     weights = twice(spreading())
     plane = jnp.bitwise_and(groups(), 3)
     pack = jnp.zeros((64, 128), F32)
-    for (near, far, _), side in zip(sides(), (first, second)):
+    for near, far, _, side in sides(first, second):
         for k, number in enumerate((near, far)):
             edge = matmul(parts(side[rows_of_tile(12 + k), :]), weights)
             pack = jnp.where(plane == number, edge, pack)
@@ -308,17 +299,64 @@
         self.write(b, values)
 
 
-def network_kernel(
-    count, state, cells, rows, weak, capture, mass, binding, charge,
-    rows_out, deposit,
-    table, both, rest, x_ref, t_ref, k_ref, a_ref, w_ref, c_ref, iterate, gain_both, gain_rest,
-):
-    load_matrices(weak, capture, both, rest)
+def fill_table(state, table):
     rho, eps, lam = (state[f].reshape(256, 128) for f in range(3))
     inverse = 1.0 / rho
     weak_high, weak_low = split(0.62 + 0.04 * rho + 0.05 * (lam * inverse))
     capture_high, capture_low = split(0.3 * jax.nn.sigmoid(eps * inverse))
     table[...] = jnp.concatenate([weak_high, weak_low, capture_high, capture_low], axis=1)
+
+
+def chunks(count):
+    return (count[0, 0] + CHUNK - 1) // CHUNK
+
+
+def first_kernel(
+    count, state, cells, rows, weak, capture,
+    iterate, w_out, c_out,
+    table, both, rest, x_ref, t_ref, k_ref, a_ref,
+):
+    load_matrices(weak, capture, both, rest)
+    fill_table(state, table)
+    lane = lanes(BLOCK)
+    ones = jnp.ones((256, 128), BF16)
+
+    def chunk(k, carry):
+        base = pl.multiple_of(k * CHUNK, CHUNK)
+
+        def place(b):
+            return pl.ds(pl.multiple_of(base + b * BLOCK, BLOCK), BLOCK)
+
+        for b in range(CHUNK // BLOCK):
+            cell = column(cells[pl.ds(k * (CHUNK // BLOCK) + b, 1), :])
+            row_id = lax.shift_right_logical(cell, 7)
+            hot = jnp.concatenate([row_id == lane, row_id == lane + 128], axis=1)
+            picked = matmul(jnp.where(hot, 1.0, 0.0).astype(BF16), table[...])
+            here = jnp.bitwise_and(cell, 127) == lane
+            here = jnp.concatenate([here, here, here, here], axis=1)
+            picked = jnp.where(here, picked, 0.0).astype(BF16)
+            w_out[place(b), :] = matmul(picked[:, :256], ones)
+            c_out[place(b), :] = matmul(picked[:, 256:], ones)
+
+        def write(b, values):
+            iterate[place(b), :] = values
+
+        finish = Finish(write)
+        newton(
+            base, finish.keep, lambda b, current, target: target, lambda b: rows[place(b), :],
+            both, rest, w_out, c_out, x_ref, t_ref, k_ref, a_ref, finish,
+        )
+        return carry
+
+    lax.fori_loop(0, chunks(count), chunk, 0)
+
+
+def second_kernel(
+    count, cells, rows, weak, capture, mass, binding, charge, iterate, w_ref, c_ref,
+    rows_out, deposit,
+    both, rest, x_ref, t_ref, k_ref, a_ref, gain_both, gain_rest,
+):
+    load_matrices(weak, capture, both, rest)
     gains = jnp.concatenate([column(binding[...]), column(charge[...])], axis=1)
     high, low = split(gains)
     gain_both[...] = jnp.concatenate([high, high], axis=0)
@@ -327,10 +365,9 @@
     deposit[...] = jnp.zeros(deposit.shape, F32)
     lane = lanes(BLOCK)
     sublane = lax.broadcasted_iota(jnp.int32, (256, 128), 0)
-    ones = jnp.ones((256, 128), BF16)
 
     def chunk(k, carry):
-        base = k * CHUNK
+        base = pl.multiple_of(k * CHUNK, CHUNK)
 
         def place(b):
             return pl.ds(pl.multiple_of(base + b * BLOCK, BLOCK), BLOCK)
@@ -338,37 +375,17 @@
         def inside(b):
             return pl.ds(b * BLOCK, BLOCK)
 
-        for b in range(CHUNK // BLOCK):
-            cell = column(cells[pl.ds(k * (CHUNK // BLOCK) + b, 1), :])
-            row_id = lax.shift_right_logical(cell, 7)
-            hot = jnp.concatenate([row_id == lane, row_id == lane + 128], axis=1)
-            picked = matmul(jnp.where(hot, 1.0, 0.0).astype(BF16), table[...])
-            here = jnp.bitwise_and(cell, 127) == lane
-            here = jnp.concatenate([here, here, here, here], axis=1)
-            picked = jnp.where(here, picked, 0.0).astype(BF16)
-            w_ref[inside(b), :] = matmul(picked[:, :256], ones)
-            c_ref[inside(b), :] = matmul(picked[:, 256:], ones)
-
-        def write_first(b, values):
-            iterate[inside(b), :] = values
-
-        def write_last(b, values):
+        def write(b, values):
             slot = base + b * BLOCK + lax.broadcasted_iota(jnp.int32, (BLOCK, 128), 0)
             occupied = slot < count[0, 0]
             rows_out[place(b), :] = jnp.where(occupied, values, 0.0)
             change = jnp.where(occupied, values - rows[place(b), :], 0.0)
-            high, low = split(change)
-            x_ref[inside(b), :] = jnp.concatenate([high, low], axis=1)
-
-        finish = Finish(write_first)
+            x_ref[inside(b), :] = parts(change)
+
+        finish = Finish(write)
         newton(
-            0, finish.keep, lambda b, current, target: target, lambda b: rows[place(b), :],
-            both, rest, w_ref, c_ref, x_ref, t_ref, k_ref, a_ref, finish,
-        )
-        finish = Finish(write_last)
-        newton(
-            0, finish.keep, lambda b, current, target: target - (current - rows[place(b), :]),
-            lambda b: iterate[inside(b), :],
+            base, finish.keep, lambda b, current, target: target - (current - rows[place(b), :]),
+            lambda b: iterate[place(b), :],
             both, rest, w_ref, c_ref, x_ref, t_ref, k_ref, a_ref, finish,
         )
         hots, values = [], []
@@ -383,14 +400,13 @@
                 jnp.bitwise_and(column(cell), 127) == lane, column(mass[number, :]), 0.0
             )
             gain = gain * jnp.concatenate([weight, weight], axis=1)
-            high, low = split(gain)
-            values.append(jnp.concatenate([high, low], axis=1))
+            values.append(parts(gain))
         sums = matmul(jnp.concatenate(hots, axis=1), jnp.concatenate(values, axis=0))
         deposit[0] += sums[:, :128] + sums[:, 256:384]
         deposit[1] += sums[:, 128:256] + sums[:, 384:]
         return carry
 
-    lax.fori_loop(0, (count[0, 0] + CHUNK - 1) // CHUNK, chunk, 0)
+    lax.fori_loop(0, chunks(count), chunk, 0)
 
 
 VMEM = pl.BlockSpec(memory_space=pltpu.VMEM)
@@ -421,11 +437,9 @@
     return lax.ppermute(packed, "grp", [(i, (i + 1) % halves) for i in range(halves)])
 
 
-def swap_pairs(first, second):
+def send(message, step):
     count = lax.axis_size("brick")
-    even = [(i, i ^ 1) for i in range(count)]
-    odd = [(i, (i + 1) % count if i % 2 else (i - 1) % count) for i in range(count)]
-    return lax.ppermute(first, "brick", even), lax.ppermute(second, "brick", odd)
+    return lax.ppermute(message, "brick", [(i, (i + step) % count) for i in range(count)])
 
 
 def on_device(
@@ -450,20 +464,27 @@
         edges_kernel, "edges", [whole, whole, whole, side, side, tile], (*fields, velocity),
         [pads, pltpu.VMEM(whole, F32), pltpu.SemaphoreType.DMA((4,))], 0, [HBM] * 4,
     )
-    first, second = swap_pairs(first, second)
-
-    rows = pltpu.VMEM((CHUNK, 128), F32)
-    matrices = [pltpu.VMEM((256, 256), BF16), pltpu.VMEM((128, 256), BF16)]
+    first = send(first, 1)
+
+    rows = abundance.reshape(1024, 128)
+    cells = tracer_cell.reshape(8, 128)
+    scratch = [pltpu.VMEM((256, 256), BF16), pltpu.VMEM((128, 256), BF16)]
+    scratch += [pltpu.VMEM((CHUNK, 256), BF16)] + [pltpu.VMEM((CHUNK, 128), F32)] * 3
+    flops = 6 * 2 * 1024 * 128 * 256 * 9
+    solved = call(
+        first_kernel, "newton_first", [(1024, 128)] * 3,
+        (tracer_count, state, cells, rows, weak_rates, capture_rates),
+        [pltpu.VMEM((256, 512), BF16), *scratch], flops, [SMEM],
+    )
+    second, *solved = lax.optimization_barrier((second, *solved))
+    second = send(second, -1)
     finished, deposit = call(
-        network_kernel, "network", [(1024, 128), (2, 256, 128)],
+        second_kernel, "newton_second", [(1024, 128), (2, 256, 128)],
         (
-            tracer_count, state, tracer_cell.reshape(8, 128), abundance.reshape(1024, 128),
-            weak_rates, capture_rates, tracer_mass.reshape(8, 128),
-            binding.reshape(1, 128), charge_ratio.reshape(1, 128),
+            tracer_count, cells, rows, weak_rates, capture_rates, tracer_mass.reshape(8, 128),
+            binding.reshape(1, 128), charge_ratio.reshape(1, 128), *solved,
         ),
-        [pltpu.VMEM((256, 512), BF16), *matrices, pltpu.VMEM((CHUNK, 256), BF16)]
-        + [rows] * 6 + matrices,
-        6 * 2 * 1024 * 128 * 256 * 18, [SMEM],
+        [*scratch, *scratch[:2]], flops, [SMEM],
     )
     packed, deposit = lax.optimization_barrier((packed, deposit))
     from_other = swap_halves(packed)

time: 28.8 us -> 30.6 us (1.062)
  waiting for transfers between devices: 2.55 us -> 5.18 us
  starting transfers between devices: 14.5 us -> 13.8 us
    ppermute x2, waiting for transfers between devices: 1.44 us -> 3.96 us  [send(): lax.ppermute(message, 'brick', [(i, (i + step) % count) for i in range(co...]
    ppermute x2, starting transfers between devices: 11.7 us -> 11.2 us  [send(): lax.ppermute(message, 'brick', [(i, (i + step) % count) for i in range(co...]
    pallas_call x5 -> x6, Pallas kernels: 9.52 us -> 9.38 us  [call(): pl.pallas_call(kernel, name=name, out_shape=[jax.ShapeDtypeStruct(o, F32)...]
  transfers between devices with their start and end apart: 4 -> 4, of which waited for: 3 -> 4; matrix products, arithmetic and copies ran while one was open for 0% -> 0% of each run, Pallas kernels for 21% -> 20%
where the time goes in v3:
time: 30.6 us; the launch traced here: 30.4 us
  starting transfers between devices  13.8 us (45%)
  Pallas kernels  9.38 us (31%)
  waiting for transfers between devices  5.18 us (17%)
  between operations  1.39 us (5%)
  local copies, waits for them, and re-layouts  0.69 us (2%)
    ppermute x2, starting transfers between devices, send(): lax.ppermute(message, 'brick', [(i, (i + step) % count) for i in range(co...  11.2 us
    pallas_call x6, Pallas kernels, call(): pl.pallas_call(kernel, name=name, out_shape=[jax.ShapeDtypeStruct(o, F32)...  9.38 us
    ppermute x2, waiting for transfers between devices, send(): lax.ppermute(message, 'brick', [(i, (i + step) % count) for i in range(co...  3.96 us
    ppermute x2, starting transfers between devices, swap_halves(): lax.ppermute(packed, 'grp', [(i, (i + 1) % halves) for i in range(halves)])  2.59 us
    ppermute x2, waiting for transfers between devices, swap_halves(): lax.ppermute(packed, 'grp', [(i, (i + 1) % halves) for i in range(halves)])  1.22 us
    unnamed x14, local copies, waits for them, and re-layouts  0.69 us
  transfers between devices with their start and end apart: 4, of which 4 were waited for; matrix products, arithmetic and copies ran while one was open for 0% of the time, Pallas kernels for 20%

profile of v3, /device:TPU:1, one launch (start us, length us, event | category | flops | bytes accessed | tf_op | source)
XLA Modules:
  0.0 30.4 jit_solution(12366927230596957780)
XLA Ops:
  0.6 0.0 copy-start.2
  0.6 0.0 copy-start.1
  0.7 1.8 %edges.1 = (f32[3,4,64,128]{3,2,1,0:T(8,128)S(1)}, f32[3,4,64,128]{3,2,1,0:T(8,128)S(1)}, f32[3,4,64,128]{3,2,1,0:T(8,128)S(1)}, f32[928,128]{1,0:T(8,128)S(1)},...) custom-call(f32[4,64,128]{2,1,0:T(8,128)} %density.1, f32[4,64,128]{2,1,0:T(8,128)} %energy.1, f32[4,64,128]{2,1,0:T(8,128)} %lepton.1, ...), custom_call_target="tpu_custom_call" | custom-call | bytes 2949120 | tf_op jit(solution)/shard_map/edges/pallas_call | solution.py:423
  2.4 0.0 copy-start.3
  2.4 2.1 %collective-permute-start = (f32[928,128]{1,0:T(8,128)S(1)}, f32[928,128]{1,0:T(8,128)S(1)}, u32[]{:S(2)}, u32[]{:S(2)}) collective-permute-start(f32[928,128]{1,0:T(8,128)S(1)} %get-tuple-element.31), channel_id=1, source_target_pairs={{0,1},{1,2},{2,3},{3,4},{4,5},{5,6},{6,7},{7,8},{8,9},{9,10},{10,1... | collective-permute-start | bytes 1425416 | tf_op jit(solution)/shard_map/ppermute | solution.py:442
  5.2 0.0 copy-done.2
  5.2 0.0 copy-done.1
  5.2 0.0 copy-done
  5.2 0.0 copy-done.3
  5.2 2.5 %newton_first.1 = (f32[1024,128]{1,0:T(8,128)S(1)}, f32[1024,128]{1,0:T(8,128)S(1)}, f32[1024,128]{1,0:T(8,128)S(1)}) custom-call(s32[1,1]{1,0:T(1,128)S(6)} %copy.16.count, f32[3,4,64,128]{3,2,1,0:T(8,128)S(1)} %get-tuple-element.28.state, s32[8,128]{1,0:T(8,128)S(1)} %bitcast.8, f32[1024,128]{1,0:T(8,128)S(1)} %bitcast.6, f32[128,128]{1,0:T(8,128)S(1)} %copy-done.1, ...), custom_call_target="tpu_custom_call" | custom-call | flops 3623878656 | bytes 2625540 | tf_op jit(solution)/shard_map/newton_first/pallas_call | solution.py:423
  7.8 0.0 copy-start.4
  7.8 9.1 %collective-permute-start.1 = (f32[928,128]{1,0:T(8,128)S(1)}, f32[928,128]{1,0:T(8,128)S(1)}, u32[]{:S(2)}, u32[]{:S(2)}) collective-permute-start(f32[928,128]{1,0:T(8,128)S(1)} %get-tuple-element.36), channel_id=1, source_target_pairs={{0,127},{1,0},{2,1},{3,2},{4,3},{5,4},{6,5},{7,6},{8,7},{9,8},{10,... | collective-permute-start | bytes 1425416 | tf_op jit(solution)/shard_map/ppermute | solution.py:442
  16.9 0.6 %copy-done.5 = f32[128]{0:T(128)S(1)} copy-done((f32[128]{0:T(128)S(1)}, f32[128]{0:T(128)}, u32[]{:S(2)}) %copy-start.5) | copy-done | bytes 536
  17.5 0.0 copy-done.6
  17.5 3.1 %newton_second.1 = (f32[1024,128]{1,0:T(8,128)}, f32[2,256,128]{2,1,0:T(8,128)S(1)}) custom-call(s32[1,1]{1,0:T(1,128)S(6)} %copy.16.count, s32[8,128]{1,0:T(8,128)S(1)} %bitcast.9, f32[1024,128]{1,0:T(8,128)S(1)} %bitcast.7, f32[128,128]{1,0:T(8,128)S(1)} %copy-done.1, f32[128,128]{1,0:T(8,128)S(1)} %copy-done.2, f32[8,128]{1,0:T(8,128)S(1)} %bitcast.10, ...), custom_call_target="tpu_custom_call" | custom-call | flops 3623878656 | bytes 3023876 | tf_op jit(solution)/shard_map/newton_second/pallas_call | solution.py:423
  20.6 0.9 %collective-permute-start.2 = (f32[64,128]{1,0:T(8,128)S(1)}, f32[64,128]{1,0:T(8,128)S(1)}, u32[]{:S(2)}, u32[]{:S(2)}) collective-permute-start(f32[64,128]{1,0:T(8,128)S(1)} %get-tuple-element.42.packed), channel_id=1, source_target_pairs={{0,128},{128,0},{1,129},{129,1},{2,130},{130,2},{3,131},{131,3},{4... | collective-permute-start | bytes 98312 | tf_op jit(solution)/shard_map/ppermute | solution.py:437
  21.6 0.9 %collective-permute-done.2.from_other = f32[64,128]{1,0:T(8,128)S(1)} collective-permute-done((f32[64,128]{1,0:T(8,128)S(1)}, f32[64,128]{1,0:T(8,128)S(1)}, u32[]{:S(2)}, u32[]{:S(2)}) %collective-permute-start.2) | collective-permute-done | bytes 32800 | tf_op jit(solution)/shard_map/ppermute | solution.py:437
  22.4 1.7 %collective-permute-done.first = f32[928,128]{1,0:T(8,128)S(1)} collective-permute-done((f32[928,128]{1,0:T(8,128)S(1)}, f32[928,128]{1,0:T(8,128)S(1)}, u32[]{:S(2)}, u32[]{:S(2)}) %collective-permute-start) | collective-permute-done | bytes 475168 | tf_op jit(solution)/shard_map/ppermute | solution.py:442
  24.2 2.2 %collective-permute-done.1.second = f32[928,128]{1,0:T(8,128)S(1)} collective-permute-done((f32[928,128]{1,0:T(8,128)S(1)}, f32[928,128]{1,0:T(8,128)S(1)}, u32[]{:S(2)}, u32[]{:S(2)}) %collective-permute-start.1) | collective-permute-done | bytes 475168 | tf_op jit(solution)/shard_map/ppermute | solution.py:442
  26.4 0.4 %midpoint.1 = (f32[3,4,64,128]{3,2,1,0:T(8,128)S(1)}, f32[128,128]{1,0:T(8,128)S(1)}) custom-call(f32[3,4,64,128]{3,2,1,0:T(8,128)S(1)} %get-tuple-element.28.state, f32[3,4,64,128]{3,2,1,0:T(8,128)S(1)} %get-tuple-element.29.velocity, f32[3,4,64,128]{3,2,1,0:T(8,128)S(1)} %get-tuple-element.30.partial, f32[928,128]{1,0:T(8,128)S(1)} %collective-permute-done.first, ...), custom_call_target="tpu_custom_call" | custom-call | bytes 2916352 | tf_op jit(solution)/shard_map/midpoint/pallas_call | solution.py:423
  26.8 1.6 %collective-permute-start.3 = (f32[128,128]{1,0:T(8,128)S(1)}, f32[128,128]{1,0:T(8,128)S(1)}, u32[]{:S(2)}, u32[]{:S(2)}) collective-permute-start(f32[128,128]{1,0:T(8,128)S(1)} %get-tuple-element.47.sent), channel_id=1, source_target_pairs={{0,128},{128,0},{1,129},{129,1},{2,130},{130,2},{3,131},{131,3},{4... | collective-permute-start | bytes 196616 | tf_op jit(solution)/shard_map/ppermute | solution.py:437
  28.5 0.5 %advance.1 = (f32[3,4,64,128]{3,2,1,0:T(8,128)S(1)}, f32[64,128]{1,0:T(8,128)S(1)}) custom-call(f32[3,4,64,128]{3,2,1,0:T(8,128)S(1)} %get-tuple-element.28.state, f32[3,4,64,128]{3,2,1,0:T(8,128)S(1)} %get-tuple-element.29.velocity, f32[3,4,64,128]{3,2,1,0:T(8,128)S(1)} %get-tuple-element.44.mid, f32[928,128]{1,0:T(8,128)S(1)} %collective-permute-done.first, ...), custom_call_target="tpu_custom_call" | custom-call | bytes 2818048 | tf_op jit(solution)/shard_map/advance/pallas_call | solution.py:423
  29.0 0.4 %collective-permute-done.3.from_other = f32[128,128]{1,0:T(8,128)S(1)} collective-permute-done((f32[128,128]{1,0:T(8,128)S(1)}, f32[128,128]{1,0:T(8,128)S(1)}, u32[]{:S(2)}, u32[]{:S(2)}) %collective-permute-start.3) | collective-permute-done | bytes 65568 | tf_op jit(solution)/shard_map/ppermute | solution.py:437
  29.4 1.1 %finish.1 = (f32[4,64,128]{2,1,0:T(8,128)}, f32[4,64,128]{2,1,0:T(8,128)}, f32[4,64,128]{2,1,0:T(8,128)}) custom-call(f32[3,4,64,128]{3,2,1,0:T(8,128)S(1)} %get-tuple-element.45.advanced, f32[64,128]{1,0:T(8,128)S(1)} %get-tuple-element.46.edge_speed, f32[128,128]{1,0:T(8,128)S(1)} %get-tuple-element.47.sent, f32[128,128]{1,0:T(8,128)S(1)} %collective-permute-done.3.from_other), custom_call_target="tpu_custom_call" | custom-call | bytes 950272 | tf_op jit(solution)/shard_map/finish/pallas_call | solution.py:423
  (4 shorter events, 0.0 us)
Async XLA Ops:
  0.6 4.6 %copy-start.2 = (f32[128,128]{1,0:T(8,128)S(1)}, f32[128,128]{1,0:T(8,128)}, u32[]{:S(2)}) copy-start(f32[128,128]{1,0:T(8,128)} %capture.3) | copy-start | bytes 196612
  0.6 4.6 %copy-start.1 = (f32[128,128]{1,0:T(8,128)S(1)}, f32[128,128]{1,0:T(8,128)}, u32[]{:S(2)}) copy-start(f32[128,128]{1,0:T(8,128)} %weak.3) | copy-start | bytes 196612
  0.7 4.6 %copy-start = (f32[1,1,1024,128]{3,2,1,0:T(8,128)S(1)}, f32[1,1,1024,128]{3,2,1,0:T(8,128)}, u32[]{:S(2)}) copy-start(f32[1,1,1024,128]{3,2,1,0:T(8,128)} %param.16) | copy-start | bytes 1572868
  2.4 2.8 %copy-start.3 = (s32[1,1,1024]{2,1,0:T(1,128)S(1)}, s32[1,1,1024]{2,1,0:T(1,128)}, u32[]{:S(2)}) copy-start(s32[1,1,1024]{2,1,0:T(1,128)} %param.18) | copy-start | bytes 12292
  2.4 21.7 %collective-permute-start = (f32[928,128]{1,0:T(8,128)S(1)}, f32[928,128]{1,0:T(8,128)S(1)}, u32[]{:S(2)}, u32[]{:S(2)}) collective-permute-start(f32[928,128]{1,0:T(8,128)S(1)} %get-tuple-element.31), channel_id=1, source_target_pairs={{0,1},{1,2},{2,3},{3,4},{4,5},{5,6},{6,7},{7,8},{8,9},{9,10},{10,1... | collective-permute-start | bytes 1425416 | tf_op jit(solution)/shard_map/ppermute | solution.py:442
  7.8 9.1 %copy-start.4 = (f32[1,1,1024]{2,1,0:T(1,128)S(1)}, f32[1,1,1024]{2,1,0:T(1,128)}, u32[]{:S(2)}) copy-start(f32[1,1,1024]{2,1,0:T(1,128)} %param.17) | copy-start | bytes 12292
  7.8 18.6 %collective-permute-start.1 = (f32[928,128]{1,0:T(8,128)S(1)}, f32[928,128]{1,0:T(8,128)S(1)}, u32[]{:S(2)}, u32[]{:S(2)}) collective-permute-start(f32[928,128]{1,0:T(8,128)S(1)} %get-tuple-element.36), channel_id=1, source_target_pairs={{0,127},{1,0},{2,1},{3,2},{4,3},{5,4},{6,5},{7,6},{8,7},{9,8},{10,... | collective-permute-start | bytes 1425416 | tf_op jit(solution)/shard_map/ppermute | solution.py:442
  16.9 0.7 %copy-start.5 = (f32[128]{0:T(128)S(1)}, f32[128]{0:T(128)}, u32[]{:S(2)}) copy-start(f32[128]{0:T(128)} %param.22) | copy-start | bytes 1540
  16.9 0.7 %copy-start.6 = (f32[128]{0:T(128)S(1)}, f32[128]{0:T(128)}, u32[]{:S(2)}) copy-start(f32[128]{0:T(128)} %param.23) | copy-start | bytes 1540
  20.6 1.8 %collective-permute-start.2 = (f32[64,128]{1,0:T(8,128)S(1)}, f32[64,128]{1,0:T(8,128)S(1)}, u32[]{:S(2)}, u32[]{:S(2)}) collective-permute-start(f32[64,128]{1,0:T(8,128)S(1)} %get-tuple-element.42.packed), channel_id=1, source_target_pairs={{0,128},{128,0},{1,129},{129,1},{2,130},{130,2},{3,131},{131,3},{4... | collective-permute-start | bytes 98312 | tf_op jit(solution)/shard_map/ppermute | solution.py:437
  26.8 2.5 %collective-permute-start.3 = (f32[128,128]{1,0:T(8,128)S(1)}, f32[128,128]{1,0:T(8,128)S(1)}, u32[]{:S(2)}, u32[]{:S(2)}) collective-permute-start(f32[128,128]{1,0:T(8,128)S(1)} %get-tuple-element.47.sent), channel_id=1, source_target_pairs={{0,128},{128,0},{1,129},{129,1},{2,130},{130,2},{3,131},{131,3},{4... | collective-permute-start | bytes 196616 | tf_op jit(solution)/shard_map/ppermute | solution.py:437

commit v4 on v2

--- a/solution.py
+++ b/solution.py
@@ -98,13 +98,7 @@
         yield i, total + here[:, :128], here[:, 128:]
 
 
-def sides():
-    odd = jnp.bitwise_and(lax.axis_index("brick"), 1)
-    even = 1 - odd
-    return (
-        (3 * even, 1 + even, (1 - 2 * odd).astype(F32)),
-        (3 * odd, 1 + odd, (2 * odd - 1).astype(F32)),
-    )
+SIDES = ((0, 1, -1.0), (3, 2, 1.0))
 
 
 def rows_of_tile(number):
@@ -113,7 +107,7 @@
 
 def edges_kernel(
     density, energy, lepton, speeds,
-    state, velocity, partial, first, second, packed,
+    state, velocity, partial, low_first, low_second, high, packed,
     pads, spread, sems,
 ):
     wait_speeds = pltpu.make_async_copy(speeds, velocity, sems.at[3])
@@ -138,23 +132,28 @@
             pack = jnp.where(group == 4 * f + i, edge, pack)
     packed[...] = pack
     group = group[:32]
-    for (near, far, _), out in zip(sides(), (first, second)):
+    for near, far, early, late, start in (
+        (3, 2, low_first, low_second, 0),
+        (0, 1, high, high, 416),
+    ):
         pack = jnp.zeros((32, 128), F32)
         for k, plane in enumerate((near, far)):
             speed = velocity[0, plane]
-            out[rows_of_tile(12 + k), :] = speed
+            late[pl.ds(start + 64 * (6 + k), 64), :] = speed
             for f in range(3):
                 value = state[f, plane]
-                out[rows_of_tile(2 * f + k), :] = speed * value
-                out[rows_of_tile(6 + 2 * f + k), :] = speed * (value - HALF * partial[f, plane])
+                early[rows_of_tile(2 * f + k), :] = speed * value
+                late[pl.ds(start + 64 * (2 * f + k), 64), :] = speed * (
+                    value - HALF * partial[f, plane]
+                )
                 place = 4 * f + 3 - plane
                 pack = jnp.where(group == place, spread[f, plane, pl.ds(0, 32), :], pack)
                 pack = jnp.where(group == place + 16, spread[f, plane, pl.ds(32, 32), :], pack)
-        out[pl.ds(64 * 14, 32), :] = pack
+        early[pl.ds(384, 32), :] = pack
 
 
 def midpoint_kernel(
-    state, velocity, partial, first, second, packed, from_other, deposit, mid, exchanged, total
+    state, velocity, partial, low, high, packed, from_other, deposit, mid, exchanged, total
 ):
     lane = lanes()
     correction = edge_correction(from_other[...], packed[...], lane)
@@ -164,7 +163,7 @@
     for f in range(3):
         for i in range(4):
             total[i] = partial[f, i] + unpack_z(correction, 4 * (4 * f + i), lane)
-        for (near, far, sign), side in zip(sides(), (first, second)):
+        for (near, far, sign), side in zip(SIDES, (low, high)):
             close = side[rows_of_tile(2 * f), :]
             total[near] += sign * (8.0 * close - side[rows_of_tile(2 * f + 1), :])
             total[far] += -sign * close
@@ -177,19 +176,15 @@
         for i in range(4):
             pack = jnp.where(group == 4 * f + i, edge[64 * i : 64 * i + 64], pack)
     exchanged[pl.ds(0, 64), :] = pack
-    odd = jnp.bitwise_and(lax.axis_index("brick"), 1)
-    upper = jnp.bitwise_and(lax.shift_right_logical(group[:32], 1), 1)
-    folded = jnp.where(
-        upper != odd, first[pl.ds(64 * 14, 32), :], second[pl.ds(64 * 14, 32), :]
-    )
+    edge = pl.ds(384, 32)
+    upper = jnp.bitwise_and(group[:32], 3) >= 2
+    folded = jnp.where(upper, high[edge, :], low[edge, :])
     exchanged[pl.ds(64, 32), :] = folded
-    exchanged[pl.ds(96, 32), :] = pltpu.roll(
-        jnp.where(upper != odd, first[pl.ds(64 * 14, 32), :], second[pl.ds(64 * 14, 32), :]), 64, 1
-    )
+    exchanged[pl.ds(96, 32), :] = pltpu.roll(folded, 64, 1)
 
 
 def advance_kernel(
-    state, velocity, mid, first, second, deposit, advanced, edge_speed, pads
+    state, velocity, mid, low, high, deposit, advanced, edge_speed, pads
 ):
     weights = twice(circulant())
     for f in range(3):
@@ -198,21 +193,22 @@
             if f > 0:
                 value = value + deposit[f - 1, pl.ds(64 * i, 64), :]
             advanced[f, i] = value
-        for (near, far, sign), side in zip(sides(), (first, second)):
+        for (near, far, sign), side, start in zip(SIDES, (low, high), (0, 416)):
             here = velocity[0, near] * state[f, near]
             behind = velocity[0, far] * state[f, far]
             step = sign * HALF
-            speed, speed_far = side[rows_of_tile(12), :], side[rows_of_tile(13), :]
-            close = side[rows_of_tile(6 + 2 * f), :] + step * (speed * (8.0 * here - behind))
-            remote = side[rows_of_tile(7 + 2 * f), :] - step * (speed_far * here)
+            speed, speed_far = (side[pl.ds(start + 64 * (6 + k), 64), :] for k in range(2))
+            close, remote = (side[pl.ds(start + 64 * (2 * f + k), 64), :] for k in range(2))
+            close = close + step * (speed * (8.0 * here - behind))
+            remote = remote - step * (speed_far * here)
             advanced[f, near] += (-FULL * sign) * (8.0 * close - remote)
             advanced[f, far] += (FULL * sign) * close
     weights = twice(spreading())
     plane = jnp.bitwise_and(groups(), 3)
     pack = jnp.zeros((64, 128), F32)
-    for (near, far, _), side in zip(sides(), (first, second)):
+    for (near, far, _), side, start in zip(SIDES, (low, high), (0, 416)):
         for k, number in enumerate((near, far)):
-            edge = matmul(parts(side[rows_of_tile(12 + k), :]), weights)
+            edge = matmul(parts(side[pl.ds(start + 64 * (6 + k), 64), :]), weights)
             pack = jnp.where(plane == number, edge, pack)
     edge_speed[...] = pack
 
@@ -421,11 +417,9 @@
     return lax.ppermute(packed, "grp", [(i, (i + 1) % halves) for i in range(halves)])
 
 
-def swap_pairs(first, second):
+def send(message, step):
     count = lax.axis_size("brick")
-    even = [(i, i ^ 1) for i in range(count)]
-    odd = [(i, (i + 1) % count if i % 2 else (i - 1) % count) for i in range(count)]
-    return lax.ppermute(first, "brick", even), lax.ppermute(second, "brick", odd)
+    return lax.ppermute(message, "brick", [(i, (i + step) % count) for i in range(count)])
 
 
 def on_device(
@@ -443,14 +437,17 @@
     charge_ratio,
 ):
     fields = (density, energy_field, lepton_field)
-    whole, side, tile = (3, 4, 64, 128), (928, 128), (64, 128)
+    whole, tile = (3, 4, 64, 128), (64, 128)
     pads = pltpu.VMEM((12, 80, 128), F32)
     planes = pltpu.VMEM((4, 64, 128), F32)
-    state, speeds, partial, first, second, packed = call(
-        edges_kernel, "edges", [whole, whole, whole, side, side, tile], (*fields, velocity),
+    state, speeds, partial, low_first, low_second, high, packed = call(
+        edges_kernel, "edges",
+        [whole, whole, whole, (416, 128), (512, 128), (928, 128), tile], (*fields, velocity),
         [pads, pltpu.VMEM(whole, F32), pltpu.SemaphoreType.DMA((4,))], 0, [HBM] * 4,
     )
-    first, second = swap_pairs(first, second)
+    low_first = send(low_first, 1)
+    low_second = send(low_second, 1)
+    high = send(high, -1)
 
     rows = pltpu.VMEM((CHUNK, 128), F32)
     matrices = [pltpu.VMEM((256, 256), BF16), pltpu.VMEM((128, 256), BF16)]
@@ -469,11 +466,12 @@
     from_other = swap_halves(packed)
     mid, sent = call(
         midpoint_kernel, "midpoint", [whole, (128, 128)],
-        (state, speeds, partial, first, second, packed, from_other, deposit), [planes],
+        (state, speeds, partial, low_first, high, packed, from_other, deposit), [planes],
     )
     from_other = swap_halves(sent)
     advanced, edge_speed = call(
-        advance_kernel, "advance", [whole, tile], (state, speeds, mid, first, second, deposit), [pads]
+        advance_kernel, "advance", [whole, tile],
+        (state, speeds, mid, low_second, high, deposit), [pads],
     )
     outs = call(
         finish_kernel, "finish", [(4, 64, 128)] * 3, (advanced, edge_speed, sent, from_other),

time: 28.8 us -> 27.5 us (0.955)
  starting transfers between devices: 14.5 us -> 13.9 us
  waiting for transfers between devices: 2.55 us -> 2.19 us
  Pallas kernels: 9.52 us -> 9.17 us
    ppermute x2 -> x3, waiting for transfers between devices: 1.44 us -> 0.98 us  [send(): lax.ppermute(message, 'brick', [(i, (i + step) % count) for i in range(co...]
    ppermute x2 -> x3, starting transfers between devices: 11.7 us -> 11.3 us  [send(): lax.ppermute(message, 'brick', [(i, (i + step) % count) for i in range(co...]
    pallas_call x5, Pallas kernels: 9.52 us -> 9.17 us  [call(): pl.pallas_call(kernel, name=name, out_shape=[jax.ShapeDtypeStruct(o, F32)...]
  transfers between devices with their start and end apart: 4 -> 5, of which waited for: 3 -> 3; matrix products, arithmetic and copies ran while one was open for 0% -> 0% of each run, Pallas kernels for 21% -> 23%
where the time goes in v4:
time: 27.5 us; the launch traced here: 27.3 us
  starting transfers between devices  13.9 us (51%)
  Pallas kernels  9.17 us (33%)
  waiting for transfers between devices  2.19 us (8%)
  between operations  1.39 us (5%)
  local copies, waits for them, and re-layouts  0.66 us (2%)
    ppermute x3, starting transfers between devices, send(): lax.ppermute(message, 'brick', [(i, (i + step) % count) for i in range(co...  11.3 us
    pallas_call x5, Pallas kernels, call(): pl.pallas_call(kernel, name=name, out_shape=[jax.ShapeDtypeStruct(o, F32)...  9.17 us
    ppermute x2, starting transfers between devices, swap_halves(): lax.ppermute(packed, 'grp', [(i, (i + 1) % halves) for i in range(halves)])  2.59 us
    ppermute x2, waiting for transfers between devices, swap_halves(): lax.ppermute(packed, 'grp', [(i, (i + 1) % halves) for i in range(halves)])  1.22 us
    ppermute x3, waiting for transfers between devices, send(): lax.ppermute(message, 'brick', [(i, (i + step) % count) for i in range(co...  0.98 us
    unnamed x14, local copies, waits for them, and re-layouts  0.66 us
  transfers between devices with their start and end apart: 5, of which 3 were waited for; matrix products, arithmetic and copies ran while one was open for 0% of the time, Pallas kernels for 23%

profile of v4, /device:TPU:1, one launch (start us, length us, event | category | flops | bytes accessed | tf_op | source)
XLA Modules:
  0.0 27.3 jit_solution(8026491700122463214)
XLA Ops:
  0.6 0.0 copy-start.2
  0.6 0.0 copy-start.1
  0.7 1.8 %edges.1 = (f32[3,4,64,128]{3,2,1,0:T(8,128)S(1)}, f32[3,4,64,128]{3,2,1,0:T(8,128)S(1)}, f32[3,4,64,128]{3,2,1,0:T(8,128)S(1)}, f32[416,128]{1,0:T(8,128)S(1)},...) custom-call(f32[4,64,128]{2,1,0:T(8,128)} %density.1, f32[4,64,128]{2,1,0:T(8,128)} %energy.1, ...), custom_call_target="tpu_custom_call" | custom-call | bytes 2949120 | tf_op jit(solution)/shard_map/edges/pallas_call | solution.py:403
  2.4 2.1 %collective-permute-start = (f32[416,128]{1,0:T(8,128)S(1)}, f32[416,128]{1,0:T(8,128)S(1)}, u32[]{:S(2)}, u32[]{:S(2)}) collective-permute-start(f32[416,128]{1,0:T(8,128)S(1)} %get-tuple-element.25), channel_id=1, source_target_pairs={{0,1},{1,2},{2,3},{3,4},{4,5},{5,6},{6,7},{7,8},{8,9},{9,10},{10,1... | collective-permute-start | bytes 638984 | tf_op jit(solution)/shard_map/ppermute | solution.py:422
  4.5 1.2 %collective-permute-start.3 = (f32[512,128]{1,0:T(8,128)S(1)}, f32[512,128]{1,0:T(8,128)S(1)}, u32[]{:S(2)}, u32[]{:S(2)}) collective-permute-start(f32[512,128]{1,0:T(8,128)S(1)} %get-tuple-element.32), channel_id=1, source_target_pairs={{0,1},{1,2},{2,3},{3,4},{4,5},{5,6},{6,7},{7,8},{8,9},{9,10},{10,1... | collective-permute-start | bytes 786440 | tf_op jit(solution)/shard_map/ppermute | solution.py:422
  5.8 8.0 %collective-permute-start.1 = (f32[928,128]{1,0:T(8,128)S(1)}, f32[928,128]{1,0:T(8,128)S(1)}, u32[]{:S(2)}, u32[]{:S(2)}) collective-permute-start(f32[928,128]{1,0:T(8,128)S(1)} %get-tuple-element.26), channel_id=1, source_target_pairs={{0,127},{1,0},{2,1},{3,2},{4,3},{5,4},{6,5},{7,6},{8,7},{9,8},{10,... | collective-permute-start | bytes 1425416 | tf_op jit(solution)/shard_map/ppermute | solution.py:422
  14.4 0.0 copy-start.4
  14.4 0.0 copy-start.3
  14.4 0.0 copy-start.5
  14.4 0.0 copy-start.6
  14.5 0.6 %copy-done.4 = f32[1,1,1024]{2,1,0:T(1,128)S(1)} copy-done((f32[1,1,1024]{2,1,0:T(1,128)S(1)}, f32[1,1,1024]{2,1,0:T(1,128)}, u32[]{:S(2)}) %copy-start.4) | copy-done | bytes 4120
  15.1 0.0 copy-done.3
  15.1 0.0 copy-done.5
  15.1 5.4 %network.1 = (f32[1024,128]{1,0:T(8,128)}, f32[2,256,128]{2,1,0:T(8,128)S(1)}) custom-call(s32[1,1]{1,0:T(1,128)S(6)} %copy.16.count, f32[3,4,64,128]{3,2,1,0:T(8,128)S(1)} %get-tuple-element.22.state, s32[8,128]{1,0:T(8,128)S(1)} %bitcast.7, f32[1024,128]{1,0:T(8,128)S(1)} %bitcast.6, f32[128,128]{1,0:T(8,128)S(1)} %copy-done.1, f32[128,128]{1,0:T(8,128)S(1)} %copy-done.2, ...), custom_call_target="tpu_custom_call" | custom-call | flops 7247757312 | bytes 1844228 | tf_op jit(solution)/shard_map/network/pallas_call | solution.py:403
  20.5 1.0 %collective-permute-start.2 = (f32[64,128]{1,0:T(8,128)S(1)}, f32[64,128]{1,0:T(8,128)S(1)}, u32[]{:S(2)}, u32[]{:S(2)}) collective-permute-start(f32[64,128]{1,0:T(8,128)S(1)} %get-tuple-element.29.packed), channel_id=1, source_target_pairs={{0,128},{128,0},{1,129},{129,1},{2,130},{130,2},{3,131},{131,3},{4... | collective-permute-start | bytes 98312 | tf_op jit(solution)/shard_map/ppermute | solution.py:417
  21.4 0.9 %collective-permute-done.2.from_other = f32[64,128]{1,0:T(8,128)S(1)} collective-permute-done((f32[64,128]{1,0:T(8,128)S(1)}, f32[64,128]{1,0:T(8,128)S(1)}, u32[]{:S(2)}, u32[]{:S(2)}) %collective-permute-start.2) | collective-permute-done | bytes 32800 | tf_op jit(solution)/shard_map/ppermute | solution.py:417
  22.3 0.0 collective-permute-done.low
  22.3 1.0 %collective-permute-done.1.high = f32[928,128]{1,0:T(8,128)S(1)} collective-permute-done((f32[928,128]{1,0:T(8,128)S(1)}, f32[928,128]{1,0:T(8,128)S(1)}, u32[]{:S(2)}, u32[]{:S(2)}) %collective-permute-start.1) | collective-permute-done | bytes 475168 | tf_op jit(solution)/shard_map/ppermute | solution.py:422
  23.3 0.4 %midpoint.1 = (f32[3,4,64,128]{3,2,1,0:T(8,128)S(1)}, f32[128,128]{1,0:T(8,128)S(1)}) custom-call(f32[3,4,64,128]{3,2,1,0:T(8,128)S(1)} %get-tuple-element.22.state, f32[3,4,64,128]{3,2,1,0:T(8,128)S(1)} %get-tuple-element.23.velocity, f32[3,4,64,128]{3,2,1,0:T(8,128)S(1)} %get-tuple-element.24.partial, f32[416,128]{1,0:T(8,128)S(1)} %collective-permute-done.low, ...), custom_call_target="tpu_custom_call" | custom-call | bytes 2654208 | tf_op jit(solution)/shard_map/midpoint/pallas_call | solution.py:403
  23.7 1.6 %collective-permute-start.4 = (f32[128,128]{1,0:T(8,128)S(1)}, f32[128,128]{1,0:T(8,128)S(1)}, u32[]{:S(2)}, u32[]{:S(2)}) collective-permute-start(f32[128,128]{1,0:T(8,128)S(1)} %get-tuple-element.35.sent), channel_id=1, source_target_pairs={{0,128},{128,0},{1,129},{129,1},{2,130},{130,2},{3,131},{131,3},{4... | collective-permute-start | bytes 196616 | tf_op jit(solution)/shard_map/ppermute | solution.py:417
  25.3 0.0 collective-permute-done.3.low
  25.3 0.5 %advance.1 = (f32[3,4,64,128]{3,2,1,0:T(8,128)S(1)}, f32[64,128]{1,0:T(8,128)S(1)}) custom-call(f32[3,4,64,128]{3,2,1,0:T(8,128)S(1)} %get-tuple-element.22.state, f32[3,4,64,128]{3,2,1,0:T(8,128)S(1)} %get-tuple-element.23.velocity, f32[3,4,64,128]{3,2,1,0:T(8,128)S(1)} %get-tuple-element.31.mid, f32[512,128]{1,0:T(8,128)S(1)} %collective-permute-done.3.low, ...), custom_call_target="tpu_custom_call" | custom-call | bytes 2605056 | tf_op jit(solution)/shard_map/advance/pallas_call | solution.py:403
  25.9 0.4 %collective-permute-done.4.from_other = f32[128,128]{1,0:T(8,128)S(1)} collective-permute-done((f32[128,128]{1,0:T(8,128)S(1)}, f32[128,128]{1,0:T(8,128)S(1)}, u32[]{:S(2)}, u32[]{:S(2)}) %collective-permute-start.4) | collective-permute-done | bytes 65568 | tf_op jit(solution)/shard_map/ppermute | solution.py:417
  26.2 1.1 %finish.1 = (f32[4,64,128]{2,1,0:T(8,128)}, f32[4,64,128]{2,1,0:T(8,128)}, f32[4,64,128]{2,1,0:T(8,128)}) custom-call(f32[3,4,64,128]{3,2,1,0:T(8,128)S(1)} %get-tuple-element.33.advanced, f32[64,128]{1,0:T(8,128)S(1)} %get-tuple-element.34.edge_speed, f32[128,128]{1,0:T(8,128)S(1)} %get-tuple-element.35.sent, f32[128,128]{1,0:T(8,128)S(1)} %collective-permute-done.4.from_other), custom_call_target="tpu_custom_call" | custom-call | bytes 950272 | tf_op jit(solution)/shard_map/finish/pallas_call | solution.py:403
  (5 shorter events, 0.0 us)
Async XLA Ops:
  0.6 13.8 %copy-start.2 = (f32[128,128]{1,0:T(8,128)S(1)}, f32[128,128]{1,0:T(8,128)}, u32[]{:S(2)}) copy-start(f32[128,128]{1,0:T(8,128)} %capture.1) | copy-start | bytes 196612
  0.6 13.8 %copy-start.1 = (f32[128,128]{1,0:T(8,128)S(1)}, f32[128,128]{1,0:T(8,128)}, u32[]{:S(2)}) copy-start(f32[128,128]{1,0:T(8,128)} %weak.1) | copy-start | bytes 196612
  0.7 13.8 %copy-start = (f32[1,1,1024,128]{3,2,1,0:T(8,128)S(1)}, f32[1,1,1024,128]{3,2,1,0:T(8,128)}, u32[]{:S(2)}) copy-start(f32[1,1,1024,128]{3,2,1,0:T(8,128)} %param.16) | copy-start | bytes 1572868
  2.4 19.9 %collective-permute-start = (f32[416,128]{1,0:T(8,128)S(1)}, f32[416,128]{1,0:T(8,128)S(1)}, u32[]{:S(2)}, u32[]{:S(2)}) collective-permute-start(f32[416,128]{1,0:T(8,128)S(1)} %get-tuple-element.25), channel_id=1, source_target_pairs={{0,1},{1,2},{2,3},{3,4},{4,5},{5,6},{6,7},{7,8},{8,9},{9,10},{10,1... | collective-permute-start | bytes 638984 | tf_op jit(solution)/shard_map/ppermute | solution.py:422
  4.5 20.8 %collective-permute-start.3 = (f32[512,128]{1,0:T(8,128)S(1)}, f32[512,128]{1,0:T(8,128)S(1)}, u32[]{:S(2)}, u32[]{:S(2)}) collective-permute-start(f32[512,128]{1,0:T(8,128)S(1)} %get-tuple-element.32), channel_id=1, source_target_pairs={{0,1},{1,2},{2,3},{3,4},{4,5},{5,6},{6,7},{7,8},{8,9},{9,10},{10,1... | collective-permute-start | bytes 786440 | tf_op jit(solution)/shard_map/ppermute | solution.py:422
  5.8 17.5 %collective-permute-start.1 = (f32[928,128]{1,0:T(8,128)S(1)}, f32[928,128]{1,0:T(8,128)S(1)}, u32[]{:S(2)}, u32[]{:S(2)}) collective-permute-start(f32[928,128]{1,0:T(8,128)S(1)} %get-tuple-element.26), channel_id=1, source_target_pairs={{0,127},{1,0},{2,1},{3,2},{4,3},{5,4},{6,5},{7,6},{8,7},{9,8},{10,... | collective-permute-start | bytes 1425416 | tf_op jit(solution)/shard_map/ppermute | solution.py:422
  14.4 0.7 %copy-start.4 = (f32[1,1,1024]{2,1,0:T(1,128)S(1)}, f32[1,1,1024]{2,1,0:T(1,128)}, u32[]{:S(2)}) copy-start(f32[1,1,1024]{2,1,0:T(1,128)} %param.17) | copy-start | bytes 12292
  14.4 0.7 %copy-start.3 = (s32[1,1,1024]{2,1,0:T(1,128)S(1)}, s32[1,1,1024]{2,1,0:T(1,128)}, u32[]{:S(2)}) copy-start(s32[1,1,1024]{2,1,0:T(1,128)} %param.18) | copy-start | bytes 12292
  14.4 0.7 %copy-start.5 = (f32[128]{0:T(128)S(1)}, f32[128]{0:T(128)}, u32[]{:S(2)}) copy-start(f32[128]{0:T(128)} %param.22) | copy-start | bytes 1540
  14.4 0.7 %copy-start.6 = (f32[128]{0:T(128)S(1)}, f32[128]{0:T(128)}, u32[]{:S(2)}) copy-start(f32[128]{0:T(128)} %param.23) | copy-start | bytes 1540
  20.5 1.8 %collective-permute-start.2 = (f32[64,128]{1,0:T(8,128)S(1)}, f32[64,128]{1,0:T(8,128)S(1)}, u32[]{:S(2)}, u32[]{:S(2)}) collective-permute-start(f32[64,128]{1,0:T(8,128)S(1)} %get-tuple-element.29.packed), channel_id=1, source_target_pairs={{0,128},{128,0},{1,129},{129,1},{2,130},{130,2},{3,131},{131,3},{4... | collective-permute-start | bytes 98312 | tf_op jit(solution)/shard_map/ppermute | solution.py:417
  23.7 2.5 %collective-permute-start.4 = (f32[128,128]{1,0:T(8,128)S(1)}, f32[128,128]{1,0:T(8,128)S(1)}, u32[]{:S(2)}, u32[]{:S(2)}) collective-permute-start(f32[128,128]{1,0:T(8,128)S(1)} %get-tuple-element.35.sent), channel_id=1, source_target_pairs={{0,128},{128,0},{1,129},{129,1},{2,130},{130,2},{3,131},{131,3},{4... | collective-permute-start | bytes 196616 | tf_op jit(solution)/shard_map/ppermute | solution.py:417

commit v5 on v4

--- a/solution.py
+++ b/solution.py
@@ -105,10 +105,25 @@
     return pl.ds(64 * number, 64)
 
 
+def fold(folded, edge, place, group):
+    folded = jnp.where(group == place, edge[:32], folded)
+    return jnp.where(group == place + 16, edge[32:], folded)
+
+
+def write_message(state, velocity, partial, planes, early, late):
+    for k, plane in enumerate(planes):
+        speed = velocity[0, plane]
+        late[rows_of_tile(6 + k), :] = speed
+        for f in range(3):
+            value = state[f, plane]
+            early[rows_of_tile(2 * f + k), :] = speed * value
+            late[rows_of_tile(2 * f + k), :] = speed * (value - HALF * partial[f, plane])
+
+
 def edges_kernel(
     density, energy, lepton, speeds,
-    state, velocity, partial, low_first, low_second, high, packed,
-    pads, spread, sems,
+    state, velocity, partial, low_first, low_second, folded, packed,
+    pads, sems,
 ):
     wait_speeds = pltpu.make_async_copy(speeds, velocity, sems.at[3])
     wait_speeds.start()
@@ -121,6 +136,7 @@
     weights = twice(jnp.concatenate([circulant(), spreading()], axis=1))
     group = groups()
     pack = jnp.zeros((64, 128), F32)
+    up = down = jnp.zeros((32, 128), F32)
     wait_speeds.wait()
     for f in range(3):
         copies[f].wait()
@@ -128,28 +144,21 @@
             lambda i: state[f, i], velocity, pads, f, weights
         ):
             partial[f, i] = total
-            spread[f, i] = edge
             pack = jnp.where(group == 4 * f + i, edge, pack)
+            if i < 2:
+                down = fold(down, edge, 4 * f + 3 - i, group[:32])
+            else:
+                up = fold(up, edge, 4 * f + 3 - i, group[:32])
     packed[...] = pack
-    group = group[:32]
-    for near, far, early, late, start in (
-        (3, 2, low_first, low_second, 0),
-        (0, 1, high, high, 416),
-    ):
-        pack = jnp.zeros((32, 128), F32)
-        for k, plane in enumerate((near, far)):
-            speed = velocity[0, plane]
-            late[pl.ds(start + 64 * (6 + k), 64), :] = speed
-            for f in range(3):
-                value = state[f, plane]
-                early[rows_of_tile(2 * f + k), :] = speed * value
-                late[pl.ds(start + 64 * (2 * f + k), 64), :] = speed * (
-                    value - HALF * partial[f, plane]
-                )
-                place = 4 * f + 3 - plane
-                pack = jnp.where(group == place, spread[f, plane, pl.ds(0, 32), :], pack)
-                pack = jnp.where(group == place + 16, spread[f, plane, pl.ds(32, 32), :], pack)
-        early[pl.ds(384, 32), :] = pack
+    folded[...] = down
+    low_first[pl.ds(384, 32), :] = up
+    write_message(state, velocity, partial, (3, 2), low_first, low_second)
+
+
+def backward_kernel(state, velocity, partial, folded, packed, high_first, high_second, copied):
+    copied[...] = packed[...]
+    high_first[pl.ds(384, 32), :] = folded[...]
+    write_message(state, velocity, partial, (0, 1), high_first, high_second)
 
 
 def midpoint_kernel(
@@ -193,12 +202,12 @@
             if f > 0:
                 value = value + deposit[f - 1, pl.ds(64 * i, 64), :]
             advanced[f, i] = value
-        for (near, far, sign), side, start in zip(SIDES, (low, high), (0, 416)):
+        for (near, far, sign), side in zip(SIDES, (low, high)):
             here = velocity[0, near] * state[f, near]
             behind = velocity[0, far] * state[f, far]
             step = sign * HALF
-            speed, speed_far = (side[pl.ds(start + 64 * (6 + k), 64), :] for k in range(2))
-            close, remote = (side[pl.ds(start + 64 * (2 * f + k), 64), :] for k in range(2))
+            speed, speed_far = (side[rows_of_tile(6 + k), :] for k in range(2))
+            close, remote = (side[rows_of_tile(2 * f + k), :] for k in range(2))
             close = close + step * (speed * (8.0 * here - behind))
             remote = remote - step * (speed_far * here)
             advanced[f, near] += (-FULL * sign) * (8.0 * close - remote)
@@ -206,9 +215,9 @@
     weights = twice(spreading())
     plane = jnp.bitwise_and(groups(), 3)
     pack = jnp.zeros((64, 128), F32)
-    for (near, far, _), side, start in zip(SIDES, (low, high), (0, 416)):
+    for (near, far, _), side in zip(SIDES, (low, high)):
         for k, number in enumerate((near, far)):
-            edge = matmul(parts(side[pl.ds(start + 64 * (6 + k), 64), :]), weights)
+            edge = matmul(parts(side[rows_of_tile(6 + k), :]), weights)
             pack = jnp.where(plane == number, edge, pack)
     edge_speed[...] = pack
 
@@ -440,14 +449,19 @@
     whole, tile = (3, 4, 64, 128), (64, 128)
     pads = pltpu.VMEM((12, 80, 128), F32)
     planes = pltpu.VMEM((4, 64, 128), F32)
-    state, speeds, partial, low_first, low_second, high, packed = call(
-        edges_kernel, "edges",
-        [whole, whole, whole, (416, 128), (512, 128), (928, 128), tile], (*fields, velocity),
-        [pads, pltpu.VMEM(whole, F32), pltpu.SemaphoreType.DMA((4,))], 0, [HBM] * 4,
+    messages = [(416, 128), (512, 128)]
+    state, speeds, partial, low_first, low_second, folded, packed = call(
+        edges_kernel, "edges", [whole] * 3 + messages + [(32, 128), tile], (*fields, velocity),
+        [pads, pltpu.SemaphoreType.DMA((4,))], 0, [HBM] * 4,
     )
     low_first = send(low_first, 1)
     low_second = send(low_second, 1)
-    high = send(high, -1)
+    high_first, high_second, packed = call(
+        backward_kernel, "backward", messages + [tile], (state, speeds, partial, folded, packed)
+    )
+    high_first = send(high_first, -1)
+    high_second = send(high_second, -1)
+    from_other = swap_halves(packed)
 
     rows = pltpu.VMEM((CHUNK, 128), F32)
     matrices = [pltpu.VMEM((256, 256), BF16), pltpu.VMEM((128, 256), BF16)]
@@ -462,16 +476,14 @@
         + [rows] * 6 + matrices,
         6 * 2 * 1024 * 128 * 256 * 18, [SMEM],
     )
-    packed, deposit = lax.optimization_barrier((packed, deposit))
-    from_other = swap_halves(packed)
     mid, sent = call(
         midpoint_kernel, "midpoint", [whole, (128, 128)],
-        (state, speeds, partial, low_first, high, packed, from_other, deposit), [planes],
+        (state, speeds, partial, low_first, high_first, packed, from_other, deposit), [planes],
     )
     from_other = swap_halves(sent)
     advanced, edge_speed = call(
         advance_kernel, "advance", [whole, tile],
-        (state, speeds, mid, low_second, high, deposit), [pads],
+        (state, speeds, mid, low_second, high_second, deposit), [pads],
     )
     outs = call(
         finish_kernel, "finish", [(4, 64, 128)] * 3, (advanced, edge_speed, sent, from_other),

time: 27.5 us -> 27.2 us (0.989)
  the two profiles are of different devices: /device:TPU:1 before, /device:TPU:126 now
where the time goes in v5:
time: 27.2 us; the launch traced here: 27.1 us
  waiting for transfers between devices  10.7 us (39%)
  Pallas kernels  9.14 us (34%)
  starting transfers between devices  5.16 us (19%)
  between operations  1.4 us (5%)
  local copies, waits for them, and re-layouts  0.66 us (2%)
    ppermute x4, waiting for transfers between devices, send(): lax.ppermute(message, 'brick', [(i, (i + step) % count) for i in range(co...  10.7 us
    pallas_call x6, Pallas kernels, call(): pl.pallas_call(kernel, name=name, out_shape=[jax.ShapeDtypeStruct(o, F32)...  9.14 us
    ppermute x4, starting transfers between devices, send(): lax.ppermute(message, 'brick', [(i, (i + step) % count) for i in range(co...  4.97 us
    unnamed x14, local copies, waits for them, and re-layouts  0.66 us
  transfers between devices with their start and end apart: 6, of which 2 were waited for; matrix products, arithmetic and copies ran while one was open for 0% of the time, Pallas kernels for 23%

profile of v5, /device:TPU:126, one launch (start us, length us, event | category | flops | bytes accessed | tf_op | source)
XLA Modules:
  0.0 27.1 jit_solution(9212185480039755050)
XLA Ops:
  0.6 1.7 %edges.1 = (f32[3,4,64,128]{3,2,1,0:T(8,128)S(1)}, f32[3,4,64,128]{3,2,1,0:T(8,128)S(1)}, f32[3,4,64,128]{3,2,1,0:T(8,128)S(1)}, f32[416,128]{1,0:T(8,128)S(1)},...) custom-call(f32[4,64,128]{2,1,0:T(8,128)} %density.1, f32[4,64,128]{2,1,0:T(8,128)} %energy.1, ...), custom_call_target="tpu_custom_call" | custom-call | bytes 2490368 | tf_op jit(solution)/shard_map/edges/pallas_call | solution.py:412
  2.3 2.8 %collective-permute-start = (f32[416,128]{1,0:T(8,128)S(1)}, f32[416,128]{1,0:T(8,128)S(1)}, u32[]{:S(2)}, u32[]{:S(2)}) collective-permute-start(f32[416,128]{1,0:T(8,128)S(1)} %get-tuple-element.26), channel_id=1, source_target_pairs={{0,1},{1,2},{2,3},{3,4},{4,5},{5,6},{6,7},{7,8},{8,9},{9,10},{10,1... | collective-permute-start | bytes 638984 | tf_op jit(solution)/shard_map/ppermute | solution.py:431
  5.1 1.5 %collective-permute-start.3 = (f32[512,128]{1,0:T(8,128)S(1)}, f32[512,128]{1,0:T(8,128)S(1)}, u32[]{:S(2)}, u32[]{:S(2)}) collective-permute-start(f32[512,128]{1,0:T(8,128)S(1)} %get-tuple-element.33), channel_id=1, source_target_pairs={{0,1},{1,2},{2,3},{3,4},{4,5},{5,6},{6,7},{7,8},{8,9},{9,10},{10,1... | collective-permute-start | bytes 786440 | tf_op jit(solution)/shard_map/ppermute | solution.py:431
  6.7 0.1 collective-permute-start.2
  6.8 0.6 %collective-permute-start.1 = (f32[416,128]{1,0:T(8,128)S(1)}, f32[416,128]{1,0:T(8,128)S(1)}, u32[]{:S(2)}, u32[]{:S(2)}) collective-permute-start(f32[416,128]{1,0:T(8,128)S(1)} %get-tuple-element.29), channel_id=1, source_target_pairs={{0,127},{1,0},{2,1},{3,2},{4,3},{5,4},{6,5},{7,6},{8,7},{9,8},{10,... | collective-permute-start | bytes 638984 | tf_op jit(solution)/shard_map/ppermute | solution.py:431
  7.4 0.1 collective-permute-start.4
  8.1 0.0 copy-start.4
  8.1 0.0 copy-start.3
  8.1 0.0 copy-start.5
  8.1 0.0 copy-start.6
  8.2 0.6 %copy-done.4 = f32[1,1,1024]{2,1,0:T(1,128)S(1)} copy-done((f32[1,1,1024]{2,1,0:T(1,128)S(1)}, f32[1,1,1024]{2,1,0:T(1,128)}, u32[]{:S(2)}) %copy-start.4) | copy-done | bytes 4120
  8.8 0.0 copy-done.3
  8.8 0.0 copy-done.5
  8.8 5.4 %network.1 = (f32[1024,128]{1,0:T(8,128)}, f32[2,256,128]{2,1,0:T(8,128)S(1)}) custom-call(s32[1,1]{1,0:T(1,128)S(6)} %copy.16.count, f32[3,4,64,128]{3,2,1,0:T(8,128)S(1)} %get-tuple-element.23.state, s32[8,128]{1,0:T(8,128)S(1)} %bitcast.7, f32[1024,128]{1,0:T(8,128)S(1)} %bitcast.6, f32[128,128]{1,0:T(8,128)S(1)} %copy-done.1, f32[128,128]{1,0:T(8,128)S(1)} %copy-done.2, ...), custom_call_target="tpu_custom_call" | custom-call | flops 7247757312 | bytes 1844228 | tf_op jit(solution)/shard_map/network/pallas_call | solution.py:412
  14.2 0.0 collective-permute-done.2.from_other
  14.2 0.0 collective-permute-done.low
  14.2 6.1 %collective-permute-done.1.high = f32[416,128]{1,0:T(8,128)S(1)} collective-permute-done((f32[416,128]{1,0:T(8,128)S(1)}, f32[416,128]{1,0:T(8,128)S(1)}, u32[]{:S(2)}, u32[]{:S(2)}) %collective-permute-start.1) | collective-permute-done | bytes 213024 | tf_op jit(solution)/shard_map/ppermute | solution.py:431
  20.3 0.4 %midpoint.1 = (f32[3,4,64,128]{3,2,1,0:T(8,128)S(1)}, f32[128,128]{1,0:T(8,128)S(1)}) custom-call(f32[3,4,64,128]{3,2,1,0:T(8,128)S(1)} %get-tuple-element.23.state, f32[3,4,64,128]{3,2,1,0:T(8,128)S(1)} %get-tuple-element.24.velocity, f32[3,4,64,128]{3,2,1,0:T(8,128)S(1)} %get-tuple-element.25.partial, f32[416,128]{1,0:T(8,128)S(1)} %collective-permute-done.low, ...), custom_call_target="tpu_custom_call" | custom-call | bytes 2392064 | tf_op jit(solution)/shard_map/midpoint/pallas_call | solution.py:412
  20.7 0.1 collective-permute-start.5
  20.8 0.0 collective-permute-done.3.low
  20.8 4.6 %collective-permute-done.4.high = f32[512,128]{1,0:T(8,128)S(1)} collective-permute-done((f32[512,128]{1,0:T(8,128)S(1)}, f32[512,128]{1,0:T(8,128)S(1)}, u32[]{:S(2)}, u32[]{:S(2)}) %collective-permute-start.4) | collective-permute-done | bytes 262176 | tf_op jit(solution)/shard_map/ppermute | solution.py:431
  25.5 0.5 %advance.1 = (f32[3,4,64,128]{3,2,1,0:T(8,128)S(1)}, f32[64,128]{1,0:T(8,128)S(1)}) custom-call(f32[3,4,64,128]{3,2,1,0:T(8,128)S(1)} %get-tuple-element.23.state, f32[3,4,64,128]{3,2,1,0:T(8,128)S(1)} %get-tuple-element.24.velocity, f32[3,4,64,128]{3,2,1,0:T(8,128)S(1)} %get-tuple-element.32.mid, f32[512,128]{1,0:T(8,128)S(1)} %collective-permute-done.3.low, ...), custom_call_target="tpu_custom_call" | custom-call | bytes 2392064 | tf_op jit(solution)/shard_map/advance/pallas_call | solution.py:412
  26.0 0.0 collective-permute-done.5.from_other
  26.0 1.1 %finish.1 = (f32[4,64,128]{2,1,0:T(8,128)}, f32[4,64,128]{2,1,0:T(8,128)}, f32[4,64,128]{2,1,0:T(8,128)}) custom-call(f32[3,4,64,128]{3,2,1,0:T(8,128)S(1)} %get-tuple-element.35.advanced, f32[64,128]{1,0:T(8,128)S(1)} %get-tuple-element.36.edge_speed, f32[128,128]{1,0:T(8,128)S(1)} %get-tuple-element.37.sent, f32[128,128]{1,0:T(8,128)S(1)} %collective-permute-done.5.from_other), custom_call_target="tpu_custom_call" | custom-call | bytes 950272 | tf_op jit(solution)/shard_map/finish/pallas_call | solution.py:412
  (8 shorter events, 0.1 us)
Async XLA Ops:
  2.3 11.9 %collective-permute-start = (f32[416,128]{1,0:T(8,128)S(1)}, f32[416,128]{1,0:T(8,128)S(1)}, u32[]{:S(2)}, u32[]{:S(2)}) collective-permute-start(f32[416,128]{1,0:T(8,128)S(1)} %get-tuple-element.26), channel_id=1, source_target_pairs={{0,1},{1,2},{2,3},{3,4},{4,5},{5,6},{6,7},{7,8},{8,9},{9,10},{10,1... | collective-permute-start | bytes 638984 | tf_op jit(solution)/shard_map/ppermute | solution.py:431
  5.1 15.7 %collective-permute-start.3 = (f32[512,128]{1,0:T(8,128)S(1)}, f32[512,128]{1,0:T(8,128)S(1)}, u32[]{:S(2)}, u32[]{:S(2)}) collective-permute-start(f32[512,128]{1,0:T(8,128)S(1)} %get-tuple-element.33), channel_id=1, source_target_pairs={{0,1},{1,2},{2,3},{3,4},{4,5},{5,6},{6,7},{7,8},{8,9},{9,10},{10,1... | collective-permute-start | bytes 786440 | tf_op jit(solution)/shard_map/ppermute | solution.py:431
  6.6 1.6 %copy-start = (f32[1,1,1024,128]{3,2,1,0:T(8,128)S(1)}, f32[1,1,1024,128]{3,2,1,0:T(8,128)}, u32[]{:S(2)}) copy-start(f32[1,1,1024,128]{3,2,1,0:T(8,128)} %param.16) | copy-start | bytes 1572868
  6.6 1.6 %copy-start.1 = (f32[128,128]{1,0:T(8,128)S(1)}, f32[128,128]{1,0:T(8,128)}, u32[]{:S(2)}) copy-start(f32[128,128]{1,0:T(8,128)} %weak.1) | copy-start | bytes 196612
  6.6 1.6 %copy-start.2 = (f32[128,128]{1,0:T(8,128)S(1)}, f32[128,128]{1,0:T(8,128)}, u32[]{:S(2)}) copy-start(f32[128,128]{1,0:T(8,128)} %capture.1) | copy-start | bytes 196612
  6.7 7.5 %collective-permute-start.2 = (f32[64,128]{1,0:T(8,128)S(1)}, f32[64,128]{1,0:T(8,128)S(1)}, u32[]{:S(2)}, u32[]{:S(2)}) collective-permute-start(f32[64,128]{1,0:T(8,128)S(1)} %get-tuple-element.30.packed), channel_id=1, source_target_pairs={{0,128},{128,0},{1,129},{129,1},{2,130},{130,2},{3,131},{131,3},{4... | collective-permute-start | bytes 98312 | tf_op jit(solution)/shard_map/ppermute | solution.py:426
  6.8 13.6 %collective-permute-start.1 = (f32[416,128]{1,0:T(8,128)S(1)}, f32[416,128]{1,0:T(8,128)S(1)}, u32[]{:S(2)}, u32[]{:S(2)}) collective-permute-start(f32[416,128]{1,0:T(8,128)S(1)} %get-tuple-element.29), channel_id=1, source_target_pairs={{0,127},{1,0},{2,1},{3,2},{4,3},{5,4},{6,5},{7,6},{8,7},{9,8},{10,... | collective-permute-start | bytes 638984 | tf_op jit(solution)/shard_map/ppermute | solution.py:431
  7.4 18.1 %collective-permute-start.4 = (f32[512,128]{1,0:T(8,128)S(1)}, f32[512,128]{1,0:T(8,128)S(1)}, u32[]{:S(2)}, u32[]{:S(2)}) collective-permute-start(f32[512,128]{1,0:T(8,128)S(1)} %get-tuple-element.34), channel_id=1, source_target_pairs={{0,127},{1,0},{2,1},{3,2},{4,3},{5,4},{6,5},{7,6},{8,7},{9,8},{10,... | collective-permute-start | bytes 786440 | tf_op jit(solution)/shard_map/ppermute | solution.py:431
  8.1 0.7 %copy-start.4 = (f32[1,1,1024]{2,1,0:T(1,128)S(1)}, f32[1,1,1024]{2,1,0:T(1,128)}, u32[]{:S(2)}) copy-start(f32[1,1,1024]{2,1,0:T(1,128)} %param.17) | copy-start | bytes 12292
  8.1 0.7 %copy-start.3 = (s32[1,1,1024]{2,1,0:T(1,128)S(1)}, s32[1,1,1024]{2,1,0:T(1,128)}, u32[]{:S(2)}) copy-start(s32[1,1,1024]{2,1,0:T(1,128)} %param.18) | copy-start | bytes 12292
  8.1 0.7 %copy-start.5 = (f32[128]{0:T(128)S(1)}, f32[128]{0:T(128)}, u32[]{:S(2)}) copy-start(f32[128]{0:T(128)} %param.22) | copy-start | bytes 1540
  8.1 0.7 %copy-start.6 = (f32[128]{0:T(128)S(1)}, f32[128]{0:T(128)}, u32[]{:S(2)}) copy-start(f32[128]{0:T(128)} %param.23) | copy-start | bytes 1540
  20.7 5.3 %collective-permute-start.5 = (f32[128,128]{1,0:T(8,128)S(1)}, f32[128,128]{1,0:T(8,128)S(1)}, u32[]{:S(2)}, u32[]{:S(2)}) collective-permute-start(f32[128,128]{1,0:T(8,128)S(1)} %get-tuple-element.37.sent), channel_id=1, source_target_pairs={{0,128},{128,0},{1,129},{129,1},{2,130},{130,2},{3,131},{131,3},{4... | collective-permute-start | bytes 196616 | tf_op jit(solution)/shard_map/ppermute | solution.py:426

commit v6 on v5

--- a/solution.py
+++ b/solution.py
@@ -192,9 +192,7 @@
     exchanged[pl.ds(96, 32), :] = pltpu.roll(folded, 64, 1)
 
 
-def advance_kernel(
-    state, velocity, mid, low, high, deposit, advanced, edge_speed, pads
-):
+def advance_kernel(state, velocity, mid, deposit, advanced, pads):
     weights = twice(circulant())
     for f in range(3):
         for i, total, _ in inner_differences(lambda i: mid[f, i], velocity, pads, f, weights):
@@ -202,6 +200,30 @@
             if f > 0:
                 value = value + deposit[f - 1, pl.ds(64 * i, 64), :]
             advanced[f, i] = value
+
+
+def finish_kernel(
+    state, velocity, advanced, low, high, sent, from_other,
+    density_out, energy_out, lepton_out, result, sems,
+):
+    lane = lanes()
+    plane = jnp.bitwise_and(groups(), 3)
+    weights = twice(spreading())
+    edge_speed = jnp.zeros((64, 128), F32)
+    for (near, far, _), side in zip(SIDES, (low, high)):
+        for k, number in enumerate((near, far)):
+            edge = matmul(parts(side[rows_of_tile(6 + k), :]), weights)
+            edge_speed = jnp.where(plane == number, edge, edge_speed)
+    own, side = pl.ds(0, 64), pl.ds(64, 64)
+    correction = edge_correction(from_other[own, :], sent[own, :], lane)
+    moved = edge_correction(from_other[side, :], sent[side, :], lane)
+    moved = HALF * (edge_speed * moved)
+    before, after = pltpu.roll(moved, 4, 1), pltpu.roll(moved, 124, 1)
+    below = jnp.where(plane == 0, 8.0 * moved - after, -before)
+    above = jnp.where(plane == 2, after, before - 8.0 * moved)
+    correction = FULL * (correction + jnp.where(plane < 2, below, above))
+    copies = []
+    for f, out in enumerate((density_out, energy_out, lepton_out)):
         for (near, far, sign), side in zip(SIDES, (low, high)):
             here = velocity[0, near] * state[f, near]
             behind = velocity[0, far] * state[f, far]
@@ -210,35 +232,9 @@
             close, remote = (side[rows_of_tile(2 * f + k), :] for k in range(2))
             close = close + step * (speed * (8.0 * here - behind))
             remote = remote - step * (speed_far * here)
-            advanced[f, near] += (-FULL * sign) * (8.0 * close - remote)
-            advanced[f, far] += (FULL * sign) * close
-    weights = twice(spreading())
-    plane = jnp.bitwise_and(groups(), 3)
-    pack = jnp.zeros((64, 128), F32)
-    for (near, far, _), side in zip(SIDES, (low, high)):
-        for k, number in enumerate((near, far)):
-            edge = matmul(parts(side[rows_of_tile(6 + k), :]), weights)
-            pack = jnp.where(plane == number, edge, pack)
-    edge_speed[...] = pack
-
-
-def finish_kernel(
-    advanced, edge_speed, sent, from_other, density_out, energy_out, lepton_out, result, sems
-):
-    lane = lanes()
-    own, side = pl.ds(0, 64), pl.ds(64, 64)
-    correction = edge_correction(from_other[own, :], sent[own, :], lane)
-    moved = edge_correction(from_other[side, :], sent[side, :], lane)
-    moved = HALF * (edge_speed[...] * moved)
-    before, after = pltpu.roll(moved, 4, 1), pltpu.roll(moved, 124, 1)
-    plane = jnp.bitwise_and(groups(), 3)
-    low = jnp.where(plane == 0, 8.0 * moved - after, -before)
-    high = jnp.where(plane == 2, after, before - 8.0 * moved)
-    correction = FULL * (correction + jnp.where(plane < 2, low, high))
-    copies = []
-    for f, out in enumerate((density_out, energy_out, lepton_out)):
-        for i in range(4):
-            result[f, i] = advanced[f, i] - unpack_z(correction, 4 * (4 * f + i), lane)
+            for i, part in ((near, remote - 8.0 * close), (far, close)):
+                packed = unpack_z(correction, 4 * (4 * f + i), lane)
+                result[f, i] = advanced[f, i] + (FULL * sign) * part - packed
         copies.append(pltpu.make_async_copy(result.at[f], out, sems.at[f]))
         copies[f].start()
     for copy in copies:
@@ -481,12 +477,12 @@
         (state, speeds, partial, low_first, high_first, packed, from_other, deposit), [planes],
     )
     from_other = swap_halves(sent)
-    advanced, edge_speed = call(
-        advance_kernel, "advance", [whole, tile],
-        (state, speeds, mid, low_second, high_second, deposit), [pads],
+    (advanced,) = call(
+        advance_kernel, "advance", [whole], (state, speeds, mid, deposit), [pads]
     )
     outs = call(
-        finish_kernel, "finish", [(4, 64, 128)] * 3, (advanced, edge_speed, sent, from_other),
+        finish_kernel, "finish", [(4, 64, 128)] * 3,
+        (state, speeds, advanced, low_second, high_second, sent, from_other),
         [pltpu.VMEM(whole, F32), pltpu.SemaphoreType.DMA((3,))], 0, (), pl.BlockSpec(memory_space=pl.ANY),
     )
     return (*outs, finished[None, None])

time: 27.2 us -> 26.8 us (0.985)
  waiting for transfers between devices: 10.7 us -> 10.4 us
    ppermute x4, waiting for transfers between devices: 10.7 us -> 10.4 us  [send(): lax.ppermute(message, 'brick', [(i, (i + step) % count) for i in range(co...]
where the time goes in v6:
time: 26.8 us; the launch traced here: 26.6 us
  waiting for transfers between devices  10.4 us (39%)
  Pallas kernels  9.06 us (34%)
  starting transfers between devices  5.16 us (19%)
  between operations  1.4 us (5%)
  local copies, waits for them, and re-layouts  0.66 us (2%)
    ppermute x4, waiting for transfers between devices, send(): lax.ppermute(message, 'brick', [(i, (i + step) % count) for i in range(co...  10.4 us
    pallas_call x6, Pallas kernels, call(): pl.pallas_call(kernel, name=name, out_shape=[jax.ShapeDtypeStruct(o, F32)...  9.06 us
    ppermute x4, starting transfers between devices, send(): lax.ppermute(message, 'brick', [(i, (i + step) % count) for i in range(co...  4.97 us
    unnamed x14, local copies, waits for them, and re-layouts  0.66 us
  transfers between devices with their start and end apart: 6, of which 2 were waited for; matrix products, arithmetic and copies ran while one was open for 0% of the time, Pallas kernels for 23%

profile of v6, /device:TPU:126, one launch (start us, length us, event | category | flops | bytes accessed | tf_op | source)
XLA Modules:
  0.0 26.6 jit_solution(15335952157016412101)
XLA Ops:
  0.6 1.7 %edges.1 = (f32[3,4,64,128]{3,2,1,0:T(8,128)S(1)}, f32[3,4,64,128]{3,2,1,0:T(8,128)S(1)}, f32[3,4,64,128]{3,2,1,0:T(8,128)S(1)}, f32[416,128]{1,0:T(8,128)S(1)},...) custom-call(f32[4,64,128]{2,1,0:T(8,128)} %density.1, f32[4,64,128]{2,1,0:T(8,128)} %energy.1, ...), custom_call_target="tpu_custom_call" | custom-call | bytes 2490368 | tf_op jit(solution)/shard_map/edges/pallas_call | solution.py:408
  2.3 2.8 %collective-permute-start = (f32[416,128]{1,0:T(8,128)S(1)}, f32[416,128]{1,0:T(8,128)S(1)}, u32[]{:S(2)}, u32[]{:S(2)}) collective-permute-start(f32[416,128]{1,0:T(8,128)S(1)} %get-tuple-element.24), channel_id=1, source_target_pairs={{0,1},{1,2},{2,3},{3,4},{4,5},{5,6},{6,7},{7,8},{8,9},{9,10},{10,1... | collective-permute-start | bytes 638984 | tf_op jit(solution)/shard_map/ppermute | solution.py:427
  5.1 1.5 %collective-permute-start.3 = (f32[512,128]{1,0:T(8,128)S(1)}, f32[512,128]{1,0:T(8,128)S(1)}, u32[]{:S(2)}, u32[]{:S(2)}) collective-permute-start(f32[512,128]{1,0:T(8,128)S(1)} %get-tuple-element.31), channel_id=1, source_target_pairs={{0,1},{1,2},{2,3},{3,4},{4,5},{5,6},{6,7},{7,8},{8,9},{9,10},{10,1... | collective-permute-start | bytes 786440 | tf_op jit(solution)/shard_map/ppermute | solution.py:427
  6.7 0.1 collective-permute-start.2
  6.8 0.6 %collective-permute-start.1 = (f32[416,128]{1,0:T(8,128)S(1)}, f32[416,128]{1,0:T(8,128)S(1)}, u32[]{:S(2)}, u32[]{:S(2)}) collective-permute-start(f32[416,128]{1,0:T(8,128)S(1)} %get-tuple-element.27), channel_id=1, source_target_pairs={{0,127},{1,0},{2,1},{3,2},{4,3},{5,4},{6,5},{7,6},{8,7},{9,8},{10,... | collective-permute-start | bytes 638984 | tf_op jit(solution)/shard_map/ppermute | solution.py:427
  7.4 0.1 collective-permute-start.4
  8.1 0.0 copy-start.4
  8.1 0.0 copy-start.3
  8.1 0.0 copy-start.5
  8.1 0.0 copy-start.6
  8.2 0.6 %copy-done.4 = f32[1,1,1024]{2,1,0:T(1,128)S(1)} copy-done((f32[1,1,1024]{2,1,0:T(1,128)S(1)}, f32[1,1,1024]{2,1,0:T(1,128)}, u32[]{:S(2)}) %copy-start.4) | copy-done | bytes 4120
  8.8 0.0 copy-done.3
  8.8 0.0 copy-done.5
  8.8 5.4 %network.1 = (f32[1024,128]{1,0:T(8,128)}, f32[2,256,128]{2,1,0:T(8,128)S(1)}) custom-call(s32[1,1]{1,0:T(1,128)S(6)} %copy.16.count, f32[3,4,64,128]{3,2,1,0:T(8,128)S(1)} %get-tuple-element.21.state, s32[8,128]{1,0:T(8,128)S(1)} %bitcast.7, f32[1024,128]{1,0:T(8,128)S(1)} %bitcast.6, f32[128,128]{1,0:T(8,128)S(1)} %copy-done.1, f32[128,128]{1,0:T(8,128)S(1)} %copy-done.2, ...), custom_call_target="tpu_custom_call" | custom-call | flops 7247757312 | bytes 1844228 | tf_op jit(solution)/shard_map/network/pallas_call | solution.py:408
  14.2 0.0 collective-permute-done.2.from_other
  14.2 0.0 collective-permute-done.low
  14.2 6.1 %collective-permute-done.1.high = f32[416,128]{1,0:T(8,128)S(1)} collective-permute-done((f32[416,128]{1,0:T(8,128)S(1)}, f32[416,128]{1,0:T(8,128)S(1)}, u32[]{:S(2)}, u32[]{:S(2)}) %collective-permute-start.1) | collective-permute-done | bytes 213024 | tf_op jit(solution)/shard_map/ppermute | solution.py:427
  20.3 0.4 %midpoint.1 = (f32[3,4,64,128]{3,2,1,0:T(8,128)S(1)}, f32[128,128]{1,0:T(8,128)S(1)}) custom-call(f32[3,4,64,128]{3,2,1,0:T(8,128)S(1)} %get-tuple-element.21.state, f32[3,4,64,128]{3,2,1,0:T(8,128)S(1)} %get-tuple-element.22.velocity, f32[3,4,64,128]{3,2,1,0:T(8,128)S(1)} %get-tuple-element.23.partial, f32[416,128]{1,0:T(8,128)S(1)} %collective-permute-done.low, ...), custom_call_target="tpu_custom_call" | custom-call | bytes 2392064 | tf_op jit(solution)/shard_map/midpoint/pallas_call | solution.py:408
  20.7 0.1 collective-permute-start.5
  20.8 0.4 %advance.1.advanced = f32[3,4,64,128]{3,2,1,0:T(8,128)S(1)} custom-call(f32[3,4,64,128]{3,2,1,0:T(8,128)S(1)} %get-tuple-element.21.state, f32[3,4,64,128]{3,2,1,0:T(8,128)S(1)} %get-tuple-element.22.velocity, f32[3,4,64,128]{3,2,1,0:T(8,128)S(1)} %get-tuple-element.30.mid, f32[2,256,128]{2,1,0:T(8,128)S(1)} %get-tuple-element.29.deposit), custom_call_target="tpu_custom_call" | custom-call | bytes 1835008 | tf_op jit(solution)/shard_map/advance/pallas_call | solution.py:408
  21.2 0.0 collective-permute-done.3.low
  21.2 4.2 %collective-permute-done.4.high = f32[512,128]{1,0:T(8,128)S(1)} collective-permute-done((f32[512,128]{1,0:T(8,128)S(1)}, f32[512,128]{1,0:T(8,128)S(1)}, u32[]{:S(2)}, u32[]{:S(2)}) %collective-permute-start.4) | collective-permute-done | bytes 262176 | tf_op jit(solution)/shard_map/ppermute | solution.py:427
  25.5 0.0 collective-permute-done.5.from_other
  25.5 1.2 %finish.1 = (f32[4,64,128]{2,1,0:T(8,128)}, f32[4,64,128]{2,1,0:T(8,128)}, f32[4,64,128]{2,1,0:T(8,128)}) custom-call(f32[3,4,64,128]{3,2,1,0:T(8,128)S(1)} %get-tuple-element.21.state, f32[3,4,64,128]{3,2,1,0:T(8,128)S(1)} %get-tuple-element.22.velocity, f32[3,4,64,128]{3,2,1,0:T(8,128)S(1)} %advance.1.advanced, f32[512,128]{1,0:T(8,128)S(1)} %collective-permute-done.3.low, ...), custom_call_target="tpu_custom_call" | custom-call | bytes 2228224 | tf_op jit(solution)/shard_map/finish/pallas_call | solution.py:408
  (8 shorter events, 0.1 us)
Async XLA Ops:
  2.3 11.9 %collective-permute-start = (f32[416,128]{1,0:T(8,128)S(1)}, f32[416,128]{1,0:T(8,128)S(1)}, u32[]{:S(2)}, u32[]{:S(2)}) collective-permute-start(f32[416,128]{1,0:T(8,128)S(1)} %get-tuple-element.24), channel_id=1, source_target_pairs={{0,1},{1,2},{2,3},{3,4},{4,5},{5,6},{6,7},{7,8},{8,9},{9,10},{10,1... | collective-permute-start | bytes 638984 | tf_op jit(solution)/shard_map/ppermute | solution.py:427
  5.1 16.1 %collective-permute-start.3 = (f32[512,128]{1,0:T(8,128)S(1)}, f32[512,128]{1,0:T(8,128)S(1)}, u32[]{:S(2)}, u32[]{:S(2)}) collective-permute-start(f32[512,128]{1,0:T(8,128)S(1)} %get-tuple-element.31), channel_id=1, source_target_pairs={{0,1},{1,2},{2,3},{3,4},{4,5},{5,6},{6,7},{7,8},{8,9},{9,10},{10,1... | collective-permute-start | bytes 786440 | tf_op jit(solution)/shard_map/ppermute | solution.py:427
  6.6 1.6 %copy-start = (f32[1,1,1024,128]{3,2,1,0:T(8,128)S(1)}, f32[1,1,1024,128]{3,2,1,0:T(8,128)}, u32[]{:S(2)}) copy-start(f32[1,1,1024,128]{3,2,1,0:T(8,128)} %param.16) | copy-start | bytes 1572868
  6.6 1.6 %copy-start.1 = (f32[128,128]{1,0:T(8,128)S(1)}, f32[128,128]{1,0:T(8,128)}, u32[]{:S(2)}) copy-start(f32[128,128]{1,0:T(8,128)} %weak.1) | copy-start | bytes 196612
  6.6 1.6 %copy-start.2 = (f32[128,128]{1,0:T(8,128)S(1)}, f32[128,128]{1,0:T(8,128)}, u32[]{:S(2)}) copy-start(f32[128,128]{1,0:T(8,128)} %capture.1) | copy-start | bytes 196612
  6.7 7.5 %collective-permute-start.2 = (f32[64,128]{1,0:T(8,128)S(1)}, f32[64,128]{1,0:T(8,128)S(1)}, u32[]{:S(2)}, u32[]{:S(2)}) collective-permute-start(f32[64,128]{1,0:T(8,128)S(1)} %get-tuple-element.28.packed), channel_id=1, source_target_pairs={{0,128},{128,0},{1,129},{129,1},{2,130},{130,2},{3,131},{131,3},{4... | collective-permute-start | bytes 98312 | tf_op jit(solution)/shard_map/ppermute | solution.py:422
  6.8 13.6 %collective-permute-start.1 = (f32[416,128]{1,0:T(8,128)S(1)}, f32[416,128]{1,0:T(8,128)S(1)}, u32[]{:S(2)}, u32[]{:S(2)}) collective-permute-start(f32[416,128]{1,0:T(8,128)S(1)} %get-tuple-element.27), channel_id=1, source_target_pairs={{0,127},{1,0},{2,1},{3,2},{4,3},{5,4},{6,5},{7,6},{8,7},{9,8},{10,... | collective-permute-start | bytes 638984 | tf_op jit(solution)/shard_map/ppermute | solution.py:427
  7.4 18.1 %collective-permute-start.4 = (f32[512,128]{1,0:T(8,128)S(1)}, f32[512,128]{1,0:T(8,128)S(1)}, u32[]{:S(2)}, u32[]{:S(2)}) collective-permute-start(f32[512,128]{1,0:T(8,128)S(1)} %get-tuple-element.32), channel_id=1, source_target_pairs={{0,127},{1,0},{2,1},{3,2},{4,3},{5,4},{6,5},{7,6},{8,7},{9,8},{10,... | collective-permute-start | bytes 786440 | tf_op jit(solution)/shard_map/ppermute | solution.py:427
  8.1 0.7 %copy-start.4 = (f32[1,1,1024]{2,1,0:T(1,128)S(1)}, f32[1,1,1024]{2,1,0:T(1,128)}, u32[]{:S(2)}) copy-start(f32[1,1,1024]{2,1,0:T(1,128)} %param.17) | copy-start | bytes 12292
  8.1 0.7 %copy-start.3 = (s32[1,1,1024]{2,1,0:T(1,128)S(1)}, s32[1,1,1024]{2,1,0:T(1,128)}, u32[]{:S(2)}) copy-start(s32[1,1,1024]{2,1,0:T(1,128)} %param.18) | copy-start | bytes 12292
  8.1 0.7 %copy-start.5 = (f32[128]{0:T(128)S(1)}, f32[128]{0:T(128)}, u32[]{:S(2)}) copy-start(f32[128]{0:T(128)} %param.22) | copy-start | bytes 1540
  8.1 0.7 %copy-start.6 = (f32[128]{0:T(128)S(1)}, f32[128]{0:T(128)}, u32[]{:S(2)}) copy-start(f32[128]{0:T(128)} %param.23) | copy-start | bytes 1540
  20.7 4.7 %collective-permute-start.5 = (f32[128,128]{1,0:T(8,128)S(1)}, f32[128,128]{1,0:T(8,128)S(1)}, u32[]{:S(2)}, u32[]{:S(2)}) collective-permute-start(f32[128,128]{1,0:T(8,128)S(1)} %get-tuple-element.33.sent), channel_id=1, source_target_pairs={{0,128},{128,0},{1,129},{129,1},{2,130},{130,2},{3,131},{131,3},{4... | collective-permute-start | bytes 196616 | tf_op jit(solution)/shard_map/ppermute | solution.py:422

commit v7 on v6

--- a/solution.py
+++ b/solution.py
@@ -118,6 +118,18 @@
             value = state[f, plane]
             early[rows_of_tile(2 * f + k), :] = speed * value
             late[rows_of_tile(2 * f + k), :] = speed * (value - HALF * partial[f, plane])
+
+
+def is_odd():
+    return jnp.full((64, 128), jnp.bitwise_and(lax.axis_index("brick"), 1)) == 1
+
+
+def chosen(odd, when_odd, when_even, start_odd=0, start_even=0):
+    return lambda number: jnp.where(
+        odd,
+        when_odd[pl.ds(start_odd + 64 * number, 64), :],
+        when_even[pl.ds(start_even + 64 * number, 64), :],
+    )
 
 
 def edges_kernel(
@@ -155,26 +167,40 @@
     write_message(state, velocity, partial, (3, 2), low_first, low_second)
 
 
-def backward_kernel(state, velocity, partial, folded, packed, high_first, high_second, copied):
-    copied[...] = packed[...]
+def pair_kernel(state, velocity, partial, folded, low_first, pair):
+    even = 1 - jnp.bitwise_and(lax.axis_index("brick"), 1)
+    edge = pl.ds(384, 32)
+    pair[edge, :] = jnp.where(is_odd()[:32], folded[...], low_first[edge, :])
+    write_message(
+        state, velocity, partial, (3 * even, 1 + even),
+        pair.at[pl.ds(0, 416)], pair.at[pl.ds(416, 512)],
+    )
+
+
+def backward_kernel(
+    state, velocity, partial, folded, pair, from_other, high_first, high_second
+):
     high_first[pl.ds(384, 32), :] = folded[...]
     write_message(state, velocity, partial, (0, 1), high_first, high_second)
 
 
 def midpoint_kernel(
-    state, velocity, partial, low, high, packed, from_other, deposit, mid, exchanged, total
+    state, velocity, partial, forward, backward, pair, packed, from_other, deposit,
+    mid, exchanged, total,
 ):
     lane = lanes()
     correction = edge_correction(from_other[...], packed[...], lane)
     group = groups()
     weights = twice(spreading())
     pack = jnp.zeros((64, 128), F32)
+    odd = is_odd()
+    low, high = chosen(odd, pair, forward), chosen(odd, backward, pair)
     for f in range(3):
         for i in range(4):
             total[i] = partial[f, i] + unpack_z(correction, 4 * (4 * f + i), lane)
         for (near, far, sign), side in zip(SIDES, (low, high)):
-            close = side[rows_of_tile(2 * f), :]
-            total[near] += sign * (8.0 * close - side[rows_of_tile(2 * f + 1), :])
+            close = side(2 * f)
+            total[near] += sign * (8.0 * close - side(2 * f + 1))
             total[far] += -sign * close
         speed_z = []
         for i in range(4):
@@ -187,7 +213,10 @@
     exchanged[pl.ds(0, 64), :] = pack
     edge = pl.ds(384, 32)
     upper = jnp.bitwise_and(group[:32], 3) >= 2
-    folded = jnp.where(upper, high[edge, :], low[edge, :])
+    odd = odd[:32]
+    high = jnp.where(odd, backward[edge, :], pair[edge, :])
+    low = jnp.where(odd, pair[edge, :], forward[edge, :])
+    folded = jnp.where(upper, high, low)
     exchanged[pl.ds(64, 32), :] = folded
     exchanged[pl.ds(96, 32), :] = pltpu.roll(folded, 64, 1)
 
@@ -203,16 +232,18 @@
 
 
 def finish_kernel(
-    state, velocity, advanced, low, high, sent, from_other,
+    state, velocity, advanced, forward, backward, pair, sent, from_other,
     density_out, energy_out, lepton_out, result, sems,
 ):
     lane = lanes()
     plane = jnp.bitwise_and(groups(), 3)
     weights = twice(spreading())
     edge_speed = jnp.zeros((64, 128), F32)
+    odd = is_odd()
+    low, high = chosen(odd, pair, forward, 416, 0), chosen(odd, backward, pair, 0, 416)
     for (near, far, _), side in zip(SIDES, (low, high)):
         for k, number in enumerate((near, far)):
-            edge = matmul(parts(side[rows_of_tile(6 + k), :]), weights)
+            edge = matmul(parts(side(6 + k)), weights)
             edge_speed = jnp.where(plane == number, edge, edge_speed)
     own, side = pl.ds(0, 64), pl.ds(64, 64)
     correction = edge_correction(from_other[own, :], sent[own, :], lane)
@@ -228,8 +259,8 @@
             here = velocity[0, near] * state[f, near]
             behind = velocity[0, far] * state[f, far]
             step = sign * HALF
-            speed, speed_far = (side[rows_of_tile(6 + k), :] for k in range(2))
-            close, remote = (side[rows_of_tile(2 * f + k), :] for k in range(2))
+            speed, speed_far = side(6), side(7)
+            close, remote = side(2 * f), side(2 * f + 1)
             close = close + step * (speed * (8.0 * here - behind))
             remote = remote - step * (speed_far * here)
             for i, part in ((near, remote - 8.0 * close), (far, close)):
@@ -422,9 +453,15 @@
     return lax.ppermute(packed, "grp", [(i, (i + 1) % halves) for i in range(halves)])
 
 
-def send(message, step):
+def send(message, step, kinds):
     count = lax.axis_size("brick")
-    return lax.ppermute(message, "brick", [(i, (i + step) % count) for i in range(count)])
+    pairs = [(i, (i + step) % count) for i in range(count) if i % 2 in kinds]
+    return lax.ppermute(message, "brick", pairs)
+
+
+def swap_even_pairs(message):
+    count = lax.axis_size("brick")
+    return lax.ppermute(message, "brick", [(i, i ^ 1) for i in range(count)])
 
 
 def on_device(
@@ -450,14 +487,18 @@
         edges_kernel, "edges", [whole] * 3 + messages + [(32, 128), tile], (*fields, velocity),
         [pads, pltpu.SemaphoreType.DMA((4,))], 0, [HBM] * 4,
     )
-    low_first = send(low_first, 1)
-    low_second = send(low_second, 1)
-    high_first, high_second, packed = call(
-        backward_kernel, "backward", messages + [tile], (state, speeds, partial, folded, packed)
-    )
-    high_first = send(high_first, -1)
-    high_second = send(high_second, -1)
+    (pair,) = call(
+        pair_kernel, "pair", [(928, 128)], (state, speeds, partial, folded, low_first)
+    )
+    low_first = send(low_first, 1, (1,))
+    low_second = send(low_second, 1, (1,))
     from_other = swap_halves(packed)
+    high_first, high_second = call(
+        backward_kernel, "backward", messages, (state, speeds, partial, folded, pair, from_other)
+    )
+    pair = swap_even_pairs(pair)
+    high_first = send(high_first, -1, (0,))
+    high_second = send(high_second, -1, (0,))
 
     rows = pltpu.VMEM((CHUNK, 128), F32)
     matrices = [pltpu.VMEM((256, 256), BF16), pltpu.VMEM((128, 256), BF16)]
@@ -474,7 +515,7 @@
     )
     mid, sent = call(
         midpoint_kernel, "midpoint", [whole, (128, 128)],
-        (state, speeds, partial, low_first, high_first, packed, from_other, deposit), [planes],
+        (state, speeds, partial, low_first, high_first, pair, packed, from_other, deposit), [planes],
     )
     from_other = swap_halves(sent)
     (advanced,) = call(
@@ -482,7 +523,7 @@
     )
     outs = call(
         finish_kernel, "finish", [(4, 64, 128)] * 3,
-        (state, speeds, advanced, low_second, high_second, sent, from_other),
+        (state, speeds, advanced, low_second, high_second, pair, sent, from_other),
         [pltpu.VMEM(whole, F32), pltpu.SemaphoreType.DMA((3,))], 0, (), pl.BlockSpec(memory_space=pl.ANY),
     )
     return (*outs, finished[None, None])

time: 26.8 us -> 31.5 us (1.18)
  the two profiles are of different devices: /device:TPU:126 before, /device:TPU:1 now
where the time goes in v7:
time: 31.5 us; the launch traced here: 31.3 us
  starting transfers between devices  19.1 us (61%)
  Pallas kernels  9.1 us (29%)
  between operations  1.46 us (5%)
  waiting for transfers between devices  1.04 us (3%)
  local copies, waits for them, and re-layouts  0.67 us (2%)
    ppermute x4, starting transfers between devices, send(): return lax.ppermute(message, 'brick', pairs)  13.6 us
    pallas_call x7, Pallas kernels, call(): pl.pallas_call(kernel, name=name, out_shape=[jax.ShapeDtypeStruct(o, F32)...  9.1 us
    ppermute x2, starting transfers between devices, swap_halves(): lax.ppermute(packed, 'grp', [(i, (i + 1) % halves) for i in range(halves)])  4.01 us
    ppermute x1, starting transfers between devices, swap_even_pairs(): return lax.ppermute(message, 'brick', [(i, i ^ 1) for i in range(count)])  1.41 us
    ppermute x4, waiting for transfers between devices, send(): return lax.ppermute(message, 'brick', pairs)  1.03 us
    unnamed x14, local copies, waits for them, and re-layouts  0.67 us
  transfers between devices with their start and end apart: 7, of which 1 were waited for; matrix products, arithmetic and copies ran while one was open for 0% of the time, Pallas kernels for 20%

profile of v7, /device:TPU:1, one launch (start us, length us, event | category | flops | bytes accessed | tf_op | source)
XLA Modules:
  0.0 31.3 jit_solution(3811420871062361958)
XLA Ops:
  0.6 1.7 %edges.1 = (f32[3,4,64,128]{3,2,1,0:T(8,128)S(1)}, f32[3,4,64,128]{3,2,1,0:T(8,128)S(1)}, f32[3,4,64,128]{3,2,1,0:T(8,128)S(1)}, f32[416,128]{1,0:T(8,128)S(1)},...) custom-call(f32[4,64,128]{2,1,0:T(8,128)} %density.1, f32[4,64,128]{2,1,0:T(8,128)} %energy.1, ...), custom_call_target="tpu_custom_call" | custom-call | bytes 2490368 | tf_op jit(solution)/shard_map/edges/pallas_call | solution.py:439
  2.3 3.3 %collective-permute-start.1 = (f32[64,128]{1,0:T(8,128)S(1)}, f32[64,128]{1,0:T(8,128)S(1)}, u32[]{:S(2)}, u32[]{:S(2)}) collective-permute-start(f32[64,128]{1,0:T(8,128)S(1)} %get-tuple-element.25.packed), channel_id=1, source_target_pairs={{0,128},{128,0},{1,129},{129,1},{2,130},{130,2},{3,131},{131,3},{4... | collective-permute-start | bytes 98312 | tf_op jit(solution)/shard_map/ppermute | solution.py:453
  5.7 1.3 %collective-permute-start = (f32[416,128]{1,0:T(8,128)S(1)}, f32[416,128]{1,0:T(8,128)S(1)}, u32[]{:S(2)}, u32[]{:S(2)}) collective-permute-start(f32[416,128]{1,0:T(8,128)S(1)} %get-tuple-element.23.low_first), channel_id=1, source_target_pairs={{1,2},{3,4},{5,6},{7,8},{9,10},{11,12},{13,14},{15,16},{17,18},{19... | collective-permute-start | bytes 638984 | tf_op jit(solution)/shard_map/ppermute | solution.py:459
  6.9 1.3 %collective-permute-start.4 = (f32[512,128]{1,0:T(8,128)S(1)}, f32[512,128]{1,0:T(8,128)S(1)}, u32[]{:S(2)}, u32[]{:S(2)}) collective-permute-start(f32[512,128]{1,0:T(8,128)S(1)} %get-tuple-element.29), channel_id=1, source_target_pairs={{1,2},{3,4},{5,6},{7,8},{9,10},{11,12},{13,14},{15,16},{17,18},{19... | collective-permute-start | bytes 786440 | tf_op jit(solution)/shard_map/ppermute | solution.py:459
  8.3 1.4 %collective-permute-start.3 = (f32[928,128]{1,0:T(8,128)S(1)}, f32[928,128]{1,0:T(8,128)S(1)}, u32[]{:S(2)}, u32[]{:S(2)}) collective-permute-start(f32[928,128]{1,0:T(8,128)S(1)} %pair.1), channel_id=1, source_target_pairs={{0,1},{1,0},{2,3},{3,2},{4,5},{5,4},{6,7},{7,6},{8,9},{9,8},{10,11... | collective-permute-start | bytes 1425416 | tf_op jit(solution)/shard_map/ppermute | solution.py:464
  10.4 0.0 copy-start
  10.4 0.0 copy-start.1
  10.4 0.0 copy-start.2
  10.5 9.8 %collective-permute-start.2 = (f32[416,128]{1,0:T(8,128)S(1)}, f32[416,128]{1,0:T(8,128)S(1)}, u32[]{:S(2)}, u32[]{:S(2)}) collective-permute-start(f32[416,128]{1,0:T(8,128)S(1)} %get-tuple-element.26), channel_id=1, source_target_pairs={{0,127},{2,1},{4,3},{6,5},{8,7},{10,9},{12,11},{14,13},{16,15},{18... | collective-permute-start | bytes 638984 | tf_op jit(solution)/shard_map/ppermute | solution.py:459
  20.2 1.3 %collective-permute-start.5 = (f32[512,128]{1,0:T(8,128)S(1)}, f32[512,128]{1,0:T(8,128)S(1)}, u32[]{:S(2)}, u32[]{:S(2)}) collective-permute-start(f32[512,128]{1,0:T(8,128)S(1)} %get-tuple-element.30), channel_id=1, source_target_pairs={{0,127},{2,1},{4,3},{6,5},{8,7},{10,9},{12,11},{14,13},{16,15},{18... | collective-permute-start | bytes 786440 | tf_op jit(solution)/shard_map/ppermute | solution.py:459
  21.5 0.0 copy-start.4
  21.6 0.0 copy-start.3
  21.6 0.0 copy-start.5
  21.6 0.0 copy-start.6
  21.6 0.6 %copy-done.4 = f32[1,1,1024]{2,1,0:T(1,128)S(1)} copy-done((f32[1,1,1024]{2,1,0:T(1,128)S(1)}, f32[1,1,1024]{2,1,0:T(1,128)}, u32[]{:S(2)}) %copy-start.4) | copy-done | bytes 4120
  22.2 0.0 copy-done.3
  22.3 5.4 %network.1 = (f32[1024,128]{1,0:T(8,128)}, f32[2,256,128]{2,1,0:T(8,128)S(1)}) custom-call(s32[1,1]{1,0:T(1,128)S(6)} %copy.16.count, f32[3,4,64,128]{3,2,1,0:T(8,128)S(1)} %get-tuple-element.20.state, s32[8,128]{1,0:T(8,128)S(1)} %bitcast.7, f32[1024,128]{1,0:T(8,128)S(1)} %bitcast.6, f32[128,128]{1,0:T(8,128)S(1)} %copy-done.1, f32[128,128]{1,0:T(8,128)S(1)} %copy-done.2, ...), custom_call_target="tpu_custom_call" | custom-call | flops 7247757312 | bytes 1844228 | tf_op jit(solution)/shard_map/network/pallas_call | solution.py:439
  27.6 0.0 collective-permute-done.forward
  27.6 0.0 collective-permute-done.2.backward
  27.6 0.4 %midpoint.1 = (f32[3,4,64,128]{3,2,1,0:T(8,128)S(1)}, f32[128,128]{1,0:T(8,128)S(1)}) custom-call(f32[3,4,64,128]{3,2,1,0:T(8,128)S(1)} %get-tuple-element.20.state, f32[3,4,64,128]{3,2,1,0:T(8,128)S(1)} %get-tuple-element.21.velocity, f32[3,4,64,128]{3,2,1,0:T(8,128)S(1)} %get-tuple-element.22.partial, f32[416,128]{1,0:T(8,128)S(1)} %collective-permute-done.forward, ...), custom_call_target="tpu_custom_call" | custom-call | bytes 2867200 | tf_op jit(solution)/shard_map/midpoint/pallas_call | solution.py:439
  28.1 0.7 %collective-permute-start.6 = (f32[128,128]{1,0:T(8,128)S(1)}, f32[128,128]{1,0:T(8,128)S(1)}, u32[]{:S(2)}, u32[]{:S(2)}) collective-permute-start(f32[128,128]{1,0:T(8,128)S(1)} %get-tuple-element.31.sent), channel_id=1, source_target_pairs={{0,128},{128,0},{1,129},{129,1},{2,130},{130,2},{3,131},{131,3},{4... | collective-permute-start | bytes 196616 | tf_op jit(solution)/shard_map/ppermute | solution.py:453
  28.7 0.4 %advance.1.advanced = f32[3,4,64,128]{3,2,1,0:T(8,128)S(1)} custom-call(f32[3,4,64,128]{3,2,1,0:T(8,128)S(1)} %get-tuple-element.20.state, f32[3,4,64,128]{3,2,1,0:T(8,128)S(1)} %get-tuple-element.21.velocity, f32[3,4,64,128]{3,2,1,0:T(8,128)S(1)} %get-tuple-element.28.mid, f32[2,256,128]{2,1,0:T(8,128)S(1)} %get-tuple-element.27.deposit), custom_call_target="tpu_custom_call" | custom-call | bytes 1835008 | tf_op jit(solution)/shard_map/advance/pallas_call | solution.py:439
  29.1 1.0 %collective-permute-done.5.backward = f32[512,128]{1,0:T(8,128)S(1)} collective-permute-done((f32[512,128]{1,0:T(8,128)S(1)}, f32[512,128]{1,0:T(8,128)S(1)}, u32[]{:S(2)}, u32[]{:S(2)}) %collective-permute-start.5) | collective-permute-done | bytes 262176 | tf_op jit(solution)/shard_map/ppermute | solution.py:459
  30.2 1.2 %finish.1 = (f32[4,64,128]{2,1,0:T(8,128)}, f32[4,64,128]{2,1,0:T(8,128)}, f32[4,64,128]{2,1,0:T(8,128)}) custom-call(f32[3,4,64,128]{3,2,1,0:T(8,128)S(1)} %get-tuple-element.20.state, f32[3,4,64,128]{3,2,1,0:T(8,128)S(1)} %get-tuple-element.21.velocity, f32[3,4,64,128]{3,2,1,0:T(8,128)S(1)} %advance.1.advanced, ...), custom_call_target="tpu_custom_call" | custom-call | bytes 2703360 | tf_op jit(solution)/shard_map/finish/pallas_call | solution.py:439
  (11 shorter events, 0.1 us)
Async XLA Ops:
  2.3 8.1 %collective-permute-start.1 = (f32[64,128]{1,0:T(8,128)S(1)}, f32[64,128]{1,0:T(8,128)S(1)}, u32[]{:S(2)}, u32[]{:S(2)}) collective-permute-start(f32[64,128]{1,0:T(8,128)S(1)} %get-tuple-element.25.packed), channel_id=1, source_target_pairs={{0,128},{128,0},{1,129},{129,1},{2,130},{130,2},{3,131},{131,3},{4... | collective-permute-start | bytes 98312 | tf_op jit(solution)/shard_map/ppermute | solution.py:453
  5.7 22.0 %collective-permute-start = (f32[416,128]{1,0:T(8,128)S(1)}, f32[416,128]{1,0:T(8,128)S(1)}, u32[]{:S(2)}, u32[]{:S(2)}) collective-permute-start(f32[416,128]{1,0:T(8,128)S(1)} %get-tuple-element.23.low_first), channel_id=1, source_target_pairs={{1,2},{3,4},{5,6},{7,8},{9,10},{11,12},{13,14},{15,16},{17,18},{19... | collective-permute-start | bytes 638984 | tf_op jit(solution)/shard_map/ppermute | solution.py:459
  6.9 22.2 %collective-permute-start.4 = (f32[512,128]{1,0:T(8,128)S(1)}, f32[512,128]{1,0:T(8,128)S(1)}, u32[]{:S(2)}, u32[]{:S(2)}) collective-permute-start(f32[512,128]{1,0:T(8,128)S(1)} %get-tuple-element.29), channel_id=1, source_target_pairs={{1,2},{3,4},{5,6},{7,8},{9,10},{11,12},{13,14},{15,16},{17,18},{19... | collective-permute-start | bytes 786440 | tf_op jit(solution)/shard_map/ppermute | solution.py:459
  8.3 19.3 %collective-permute-start.3 = (f32[928,128]{1,0:T(8,128)S(1)}, f32[928,128]{1,0:T(8,128)S(1)}, u32[]{:S(2)}, u32[]{:S(2)}) collective-permute-start(f32[928,128]{1,0:T(8,128)S(1)} %pair.1), channel_id=1, source_target_pairs={{0,1},{1,0},{2,3},{3,2},{4,5},{5,4},{6,7},{7,6},{8,9},{9,8},{10,11... | collective-permute-start | bytes 1425416 | tf_op jit(solution)/shard_map/ppermute | solution.py:464
  10.4 11.2 %copy-start = (f32[1,1,1024,128]{3,2,1,0:T(8,128)S(1)}, f32[1,1,1024,128]{3,2,1,0:T(8,128)}, u32[]{:S(2)}) copy-start(f32[1,1,1024,128]{3,2,1,0:T(8,128)} %param.16) | copy-start | bytes 1572868
  10.4 11.2 %copy-start.1 = (f32[128,128]{1,0:T(8,128)S(1)}, f32[128,128]{1,0:T(8,128)}, u32[]{:S(2)}) copy-start(f32[128,128]{1,0:T(8,128)} %weak.1) | copy-start | bytes 196612
  10.4 11.2 %copy-start.2 = (f32[128,128]{1,0:T(8,128)S(1)}, f32[128,128]{1,0:T(8,128)}, u32[]{:S(2)}) copy-start(f32[128,128]{1,0:T(8,128)} %capture.1) | copy-start | bytes 196612
  10.5 17.2 %collective-permute-start.2 = (f32[416,128]{1,0:T(8,128)S(1)}, f32[416,128]{1,0:T(8,128)S(1)}, u32[]{:S(2)}, u32[]{:S(2)}) collective-permute-start(f32[416,128]{1,0:T(8,128)S(1)} %get-tuple-element.26), channel_id=1, source_target_pairs={{0,127},{2,1},{4,3},{6,5},{8,7},{10,9},{12,11},{14,13},{16,15},{18... | collective-permute-start | bytes 638984 | tf_op jit(solution)/shard_map/ppermute | solution.py:459
  20.2 9.9 %collective-permute-start.5 = (f32[512,128]{1,0:T(8,128)S(1)}, f32[512,128]{1,0:T(8,128)S(1)}, u32[]{:S(2)}, u32[]{:S(2)}) collective-permute-start(f32[512,128]{1,0:T(8,128)S(1)} %get-tuple-element.30), channel_id=1, source_target_pairs={{0,127},{2,1},{4,3},{6,5},{8,7},{10,9},{12,11},{14,13},{16,15},{18... | collective-permute-start | bytes 786440 | tf_op jit(solution)/shard_map/ppermute | solution.py:459
  21.5 0.7 %copy-start.4 = (f32[1,1,1024]{2,1,0:T(1,128)S(1)}, f32[1,1,1024]{2,1,0:T(1,128)}, u32[]{:S(2)}) copy-start(f32[1,1,1024]{2,1,0:T(1,128)} %param.17) | copy-start | bytes 12292
  21.6 0.7 %copy-start.3 = (s32[1,1,1024]{2,1,0:T(1,128)S(1)}, s32[1,1,1024]{2,1,0:T(1,128)}, u32[]{:S(2)}) copy-start(s32[1,1,1024]{2,1,0:T(1,128)} %param.18) | copy-start | bytes 12292
  21.6 0.7 %copy-start.5 = (f32[128]{0:T(128)S(1)}, f32[128]{0:T(128)}, u32[]{:S(2)}) copy-start(f32[128]{0:T(128)} %param.22) | copy-start | bytes 1540
  21.6 0.7 %copy-start.6 = (f32[128]{0:T(128)S(1)}, f32[128]{0:T(128)}, u32[]{:S(2)}) copy-start(f32[128]{0:T(128)} %param.23) | copy-start | bytes 1540
  28.1 2.1 %collective-permute-start.6 = (f32[128,128]{1,0:T(8,128)S(1)}, f32[128,128]{1,0:T(8,128)S(1)}, u32[]{:S(2)}, u32[]{:S(2)}) collective-permute-start(f32[128,128]{1,0:T(8,128)S(1)} %get-tuple-element.31.sent), channel_id=1, source_target_pairs={{0,128},{128,0},{1,129},{129,1},{2,130},{130,2},{3,131},{131,3},{4... | collective-permute-start | bytes 196616 | tf_op jit(solution)/shard_map/ppermute | solution.py:453

commit v8 on v6

--- a/solution.py
+++ b/solution.py
@@ -80,9 +80,12 @@
     )
 
 
-def inner_differences(get, velocity, pads, f, weights):
+def z_products(get, velocity, f, weights):
     speed_z = [parts(velocity[2, i] * get(i)) for i in range(4)]
-    along_z = matmul(jnp.concatenate(speed_z, axis=0), weights)
+    return matmul(jnp.concatenate(speed_z, axis=0), weights)
+
+
+def xy_differences(get, velocity, pads, f):
     for i in range(4):
         plane = [velocity[0, j] * get(j) for j in range(4) if 0 < abs(j - i) < 3]
         if i == 0:
@@ -93,9 +96,7 @@
             total = 8.0 * (plane[2] - plane[1]) + plane[0]
         else:
             total = plane[0] - 8.0 * plane[1]
-        total = total + along_y(velocity[1, i] * get(i), pads.at[4 * f + i])
-        here = along_z[64 * i : 64 * i + 64]
-        yield i, total + here[:, :128], here[:, 128:]
+        yield i, total + along_y(velocity[1, i] * get(i), pads.at[4 * f + i])
 
 
 SIDES = ((0, 1, -1.0), (3, 2, 1.0))
@@ -110,20 +111,16 @@
     return jnp.where(group == place + 16, edge[32:], folded)
 
 
-def write_message(state, velocity, partial, planes, early, late):
+def write_late(state, velocity, partial, planes, late):
     for k, plane in enumerate(planes):
-        speed = velocity[0, plane]
-        late[rows_of_tile(6 + k), :] = speed
         for f in range(3):
-            value = state[f, plane]
-            early[rows_of_tile(2 * f + k), :] = speed * value
-            late[rows_of_tile(2 * f + k), :] = speed * (value - HALF * partial[f, plane])
+            late[rows_of_tile(2 * f + k), :] = velocity[0, plane] * (
+                state[f, plane] - HALF * partial[f, plane]
+            )
 
 
 def edges_kernel(
-    density, energy, lepton, speeds,
-    state, velocity, partial, low_first, low_second, folded, packed,
-    pads, sems,
+    density, energy, lepton, speeds, state, velocity, slopes, low_first, folded, packed, sems
 ):
     wait_speeds = pltpu.make_async_copy(speeds, velocity, sems.at[3])
     wait_speeds.start()
@@ -140,32 +137,47 @@
     wait_speeds.wait()
     for f in range(3):
         copies[f].wait()
-        for i, total, edge in inner_differences(
-            lambda i: state[f, i], velocity, pads, f, weights
-        ):
-            partial[f, i] = total
+        product = z_products(lambda i: state[f, i], velocity, f, weights)
+        for i in range(4):
+            slopes[f, i] = product[64 * i : 64 * i + 64, :128]
+            edge = product[64 * i : 64 * i + 64, 128:]
             pack = jnp.where(group == 4 * f + i, edge, pack)
             if i < 2:
                 down = fold(down, edge, 4 * f + 3 - i, group[:32])
             else:
                 up = fold(up, edge, 4 * f + 3 - i, group[:32])
+                low_first[rows_of_tile(2 * f + 3 - i), :] = velocity[0, i] * state[f, i]
     packed[...] = pack
     folded[...] = down
     low_first[pl.ds(384, 32), :] = up
-    write_message(state, velocity, partial, (3, 2), low_first, low_second)
-
-
-def backward_kernel(state, velocity, partial, folded, packed, high_first, high_second, copied):
-    copied[...] = packed[...]
+    for k in range(2):
+        low_first[pl.ds(416 + 64 * k, 64), :] = velocity[0, 3 - k]
+
+
+def messages_kernel(
+    state, velocity, slopes, folded, packed,
+    partial, low_second, high_first, high_second, copied,
+    pads,
+):
+    for f in range(3):
+        for i, total in xy_differences(lambda i: state[f, i], velocity, pads, f):
+            partial[f, i] = total + slopes[f, i]
+            if i < 2:
+                high_first[rows_of_tile(2 * f + i), :] = velocity[0, i] * state[f, i]
+    write_late(state, velocity, partial, (3, 2), low_second)
+    write_late(state, velocity, partial, (0, 1), high_second)
     high_first[pl.ds(384, 32), :] = folded[...]
-    write_message(state, velocity, partial, (0, 1), high_first, high_second)
+    for k in range(2):
+        high_second[rows_of_tile(6 + k), :] = velocity[0, k]
+    copied[pl.ds(0, 64), :] = packed[...]
+    copied[pl.ds(64, 464), :] = jnp.zeros((464, 128), F32)
 
 
 def midpoint_kernel(
     state, velocity, partial, low, high, packed, from_other, deposit, mid, exchanged, total
 ):
     lane = lanes()
-    correction = edge_correction(from_other[...], packed[...], lane)
+    correction = edge_correction(from_other[pl.ds(0, 64), :], packed[...], lane)
     group = groups()
     weights = twice(spreading())
     pack = jnp.zeros((64, 128), F32)
@@ -195,24 +207,29 @@
 def advance_kernel(state, velocity, mid, deposit, advanced, pads):
     weights = twice(circulant())
     for f in range(3):
-        for i, total, _ in inner_differences(lambda i: mid[f, i], velocity, pads, f, weights):
-            value = state[f, i] - FULL * total
+        slopes = z_products(lambda i: mid[f, i], velocity, f, weights)
+        for i, total in xy_differences(lambda i: mid[f, i], velocity, pads, f):
+            value = state[f, i] - FULL * (total + slopes[64 * i : 64 * i + 64])
             if f > 0:
                 value = value + deposit[f - 1, pl.ds(64 * i, 64), :]
             advanced[f, i] = value
 
 
 def finish_kernel(
-    state, velocity, advanced, low, high, sent, from_other,
+    state, velocity, advanced, low_first, low, high, sent, from_other,
     density_out, energy_out, lepton_out, result, sems,
 ):
     lane = lanes()
     plane = jnp.bitwise_and(groups(), 3)
     weights = twice(spreading())
     edge_speed = jnp.zeros((64, 128), F32)
-    for (near, far, _), side in zip(SIDES, (low, high)):
-        for k, number in enumerate((near, far)):
-            edge = matmul(parts(side[rows_of_tile(6 + k), :]), weights)
+    speeds = (
+        [low_first[pl.ds(416 + 64 * k, 64), :] for k in range(2)],
+        [high[rows_of_tile(6 + k), :] for k in range(2)],
+    )
+    for (near, far, _), pair in zip(SIDES, speeds):
+        for number, values in zip((near, far), pair):
+            edge = matmul(parts(values), weights)
             edge_speed = jnp.where(plane == number, edge, edge_speed)
     own, side = pl.ds(0, 64), pl.ds(64, 64)
     correction = edge_correction(from_other[own, :], sent[own, :], lane)
@@ -224,11 +241,10 @@
     correction = FULL * (correction + jnp.where(plane < 2, below, above))
     copies = []
     for f, out in enumerate((density_out, energy_out, lepton_out)):
-        for (near, far, sign), side in zip(SIDES, (low, high)):
+        for (near, far, sign), side, (speed, speed_far) in zip(SIDES, (low, high), speeds):
             here = velocity[0, near] * state[f, near]
             behind = velocity[0, far] * state[f, far]
             step = sign * HALF
-            speed, speed_far = (side[rows_of_tile(6 + k), :] for k in range(2))
             close, remote = (side[rows_of_tile(2 * f + k), :] for k in range(2))
             close = close + step * (speed * (8.0 * here - behind))
             remote = remote - step * (speed_far * here)
@@ -445,19 +461,19 @@
     whole, tile = (3, 4, 64, 128), (64, 128)
     pads = pltpu.VMEM((12, 80, 128), F32)
     planes = pltpu.VMEM((4, 64, 128), F32)
-    messages = [(416, 128), (512, 128)]
-    state, speeds, partial, low_first, low_second, folded, packed = call(
-        edges_kernel, "edges", [whole] * 3 + messages + [(32, 128), tile], (*fields, velocity),
-        [pads, pltpu.SemaphoreType.DMA((4,))], 0, [HBM] * 4,
+    state, speeds, slopes, low_first, folded, packed = call(
+        edges_kernel, "edges", [whole] * 3 + [(544, 128), (32, 128), tile], (*fields, velocity),
+        [pltpu.SemaphoreType.DMA((4,))], 0, [HBM] * 4,
     )
     low_first = send(low_first, 1)
+    partial, low_second, high_first, high_second, copied = call(
+        messages_kernel, "messages", [whole, (384, 128), (416, 128), (512, 128), (528, 128)],
+        (state, speeds, slopes, folded, packed), [pads],
+    )
     low_second = send(low_second, 1)
-    high_first, high_second, packed = call(
-        backward_kernel, "backward", messages + [tile], (state, speeds, partial, folded, packed)
-    )
     high_first = send(high_first, -1)
     high_second = send(high_second, -1)
-    from_other = swap_halves(packed)
+    from_other = swap_halves(copied)
 
     rows = pltpu.VMEM((CHUNK, 128), F32)
     matrices = [pltpu.VMEM((256, 256), BF16), pltpu.VMEM((128, 256), BF16)]
@@ -482,7 +498,7 @@
     )
     outs = call(
         finish_kernel, "finish", [(4, 64, 128)] * 3,
-        (state, speeds, advanced, low_second, high_second, sent, from_other),
+        (state, speeds, advanced, low_first, low_second, high_second, sent, from_other),
         [pltpu.VMEM(whole, F32), pltpu.SemaphoreType.DMA((3,))], 0, (), pl.BlockSpec(memory_space=pl.ANY),
     )
     return (*outs, finished[None, None])

time: 26.8 us -> 26.8 us (level)
  the two profiles are of different devices: /device:TPU:126 before, /device:TPU:1 now
where the time goes in v8:
time: 26.8 us; the launch traced here: 26.6 us
  starting transfers between devices  14.4 us (54%)
  Pallas kernels  9.4 us (35%)
  between operations  1.4 us (5%)
  waiting for transfers between devices  0.79 us (3%)
  local copies, waits for them, and re-layouts  0.66 us (2%)
    ppermute x4, starting transfers between devices, send(): lax.ppermute(message, 'brick', [(i, (i + step) % count) for i in range(co...  12.8 us
    pallas_call x6, Pallas kernels, call(): pl.pallas_call(kernel, name=name, out_shape=[jax.ShapeDtypeStruct(o, F32)...  9.4 us
    ppermute x2, starting transfers between devices, swap_halves(): lax.ppermute(packed, 'grp', [(i, (i + 1) % halves) for i in range(halves)])  1.61 us
    ppermute x2, waiting for transfers between devices, swap_halves(): lax.ppermute(packed, 'grp', [(i, (i + 1) % halves) for i in range(halves)])  0.78 us
    unnamed x14, local copies, waits for them, and re-layouts  0.66 us
  transfers between devices with their start and end apart: 6, of which 1 were waited for; matrix products, arithmetic and copies ran while one was open for 0% of the time, Pallas kernels for 25%

profile of v8, /device:TPU:1, one launch (start us, length us, event | category | flops | bytes accessed | tf_op | source)
XLA Modules:
  0.0 26.6 jit_solution(1457453316928547527)
XLA Ops:
  0.6 1.7 %edges.1 = (f32[3,4,64,128]{3,2,1,0:T(8,128)S(1)}, f32[3,4,64,128]{3,2,1,0:T(8,128)S(1)}, f32[3,4,64,128]{3,2,1,0:T(8,128)S(1)}, f32[544,128]{1,0:T(8,128)S(1)},...) custom-call(f32[4,64,128]{2,1,0:T(8,128)} %density.1, f32[4,64,128]{2,1,0:T(8,128)} %energy.1, f32[4,64,128]{2,1,0:T(8,128)} %lepton.1, ...), custom_call_target="tpu_custom_call" | custom-call | bytes 2293760 | tf_op jit(solution)/shard_map/edges/pallas_call | solution.py:424
  2.3 2.1 %collective-permute-start = (f32[544,128]{1,0:T(8,128)S(1)}, f32[544,128]{1,0:T(8,128)S(1)}, u32[]{:S(2)}, u32[]{:S(2)}) collective-permute-start(f32[544,128]{1,0:T(8,128)S(1)} %get-tuple-element.28), channel_id=1, source_target_pairs={{0,1},{1,2},{2,3},{3,4},{4,5},{5,6},{6,7},{7,8},{8,9},{9,10},{10,1... | collective-permute-start | bytes 835592 | tf_op jit(solution)/shard_map/ppermute | solution.py:443
  4.4 0.3 %messages.1 = (f32[3,4,64,128]{3,2,1,0:T(8,128)S(1)}, f32[384,128]{1,0:T(8,128)S(1)}, f32[416,128]{1,0:T(8,128)S(1)}, f32[512,128]{1,0:T(8,128)S(1)}, f32[528,128]{1,0:T(8,128)S(1)}) custom-call(f32[3,4,64,128]{3,2,1,0:T(8,128)S(1)} %get-tuple-element.22.state, f32[3,4,64,128]{3,2,1,0:T(8,128)S(1)} %get-tuple-element.23.velocity, ...), custom_call_target="tpu_custom_call" | custom-call | bytes 2564096 | tf_op jit(solution)/shard_map/messages/pallas_call | solution.py:424
  4.7 1.3 %collective-permute-start.3 = (f32[384,128]{1,0:T(8,128)S(1)}, f32[384,128]{1,0:T(8,128)S(1)}, u32[]{:S(2)}, u32[]{:S(2)}) collective-permute-start(f32[384,128]{1,0:T(8,128)S(1)} %get-tuple-element.33), channel_id=1, source_target_pairs={{0,1},{1,2},{2,3},{3,4},{4,5},{5,6},{6,7},{7,8},{8,9},{9,10},{10,1... | collective-permute-start | bytes 589832 | tf_op jit(solution)/shard_map/ppermute | solution.py:443
  6.0 7.9 %collective-permute-start.1 = (f32[416,128]{1,0:T(8,128)S(1)}, f32[416,128]{1,0:T(8,128)S(1)}, u32[]{:S(2)}, u32[]{:S(2)}) collective-permute-start(f32[416,128]{1,0:T(8,128)S(1)} %get-tuple-element.29), channel_id=1, source_target_pairs={{0,127},{1,0},{2,1},{3,2},{4,3},{5,4},{6,5},{7,6},{8,7},{9,8},{10,... | collective-permute-start | bytes 638984 | tf_op jit(solution)/shard_map/ppermute | solution.py:443
  14.0 1.4 %collective-permute-start.4 = (f32[512,128]{1,0:T(8,128)S(1)}, f32[512,128]{1,0:T(8,128)S(1)}, u32[]{:S(2)}, u32[]{:S(2)}) collective-permute-start(f32[512,128]{1,0:T(8,128)S(1)} %get-tuple-element.34), channel_id=1, source_target_pairs={{0,127},{1,0},{2,1},{3,2},{4,3},{5,4},{6,5},{7,6},{8,7},{9,8},{10,... | collective-permute-start | bytes 786440 | tf_op jit(solution)/shard_map/ppermute | solution.py:443
  15.4 1.5 %collective-permute-start.2 = (f32[528,128]{1,0:T(8,128)S(1)}, f32[528,128]{1,0:T(8,128)S(1)}, u32[]{:S(2)}, u32[]{:S(2)}) collective-permute-start(f32[528,128]{1,0:T(8,128)S(1)} %get-tuple-element.30), channel_id=1, source_target_pairs={{0,128},{128,0},{1,129},{129,1},{2,130},{130,2},{3,131},{131,3},{4... | collective-permute-start | bytes 811016 | tf_op jit(solution)/shard_map/ppermute | solution.py:438
  17.5 0.0 copy-start.4
  17.6 0.0 copy-start.3
  17.6 0.0 copy-start.5
  17.6 0.0 copy-start.6
  17.6 0.6 %copy-done.4 = f32[1,1,1024]{2,1,0:T(1,128)S(1)} copy-done((f32[1,1,1024]{2,1,0:T(1,128)S(1)}, f32[1,1,1024]{2,1,0:T(1,128)}, u32[]{:S(2)}) %copy-start.4) | copy-done | bytes 4120
  18.2 0.0 copy-done.3
  18.3 5.4 %network.1 = (f32[1024,128]{1,0:T(8,128)}, f32[2,256,128]{2,1,0:T(8,128)S(1)}) custom-call(s32[1,1]{1,0:T(1,128)S(6)} %copy.16.count, f32[3,4,64,128]{3,2,1,0:T(8,128)S(1)} %get-tuple-element.22.state, s32[8,128]{1,0:T(8,128)S(1)} %bitcast.7, f32[1024,128]{1,0:T(8,128)S(1)} %bitcast.6, f32[128,128]{1,0:T(8,128)S(1)} %copy-done.1, f32[128,128]{1,0:T(8,128)S(1)} %copy-done.2, ...), custom_call_target="tpu_custom_call" | custom-call | flops 7247757312 | bytes 1844228 | tf_op jit(solution)/shard_map/network/pallas_call | solution.py:424
  23.6 0.0 collective-permute-done.1.high
  23.7 0.0 collective-permute-done.2.from_other
  23.7 0.0 collective-permute-done.low.low_first
  23.7 0.4 %midpoint.1 = (f32[3,4,64,128]{3,2,1,0:T(8,128)S(1)}, f32[128,128]{1,0:T(8,128)S(1)}) custom-call(f32[3,4,64,128]{3,2,1,0:T(8,128)S(1)} %get-tuple-element.22.state, f32[3,4,64,128]{3,2,1,0:T(8,128)S(1)} %get-tuple-element.23.velocity, f32[3,4,64,128]{3,2,1,0:T(8,128)S(1)} %get-tuple-element.27.partial, f32[544,128]{1,0:T(8,128)S(1)} %collective-permute-done.low.low_first, ...), custom_call_target="tpu_custom_call" | custom-call | bytes 2695168 | tf_op jit(solution)/shard_map/midpoint/pallas_call | solution.py:424
  24.1 0.1 collective-permute-start.5
  24.2 0.4 %advance.1.advanced = f32[3,4,64,128]{3,2,1,0:T(8,128)S(1)} custom-call(f32[3,4,64,128]{3,2,1,0:T(8,128)S(1)} %get-tuple-element.22.state, f32[3,4,64,128]{3,2,1,0:T(8,128)S(1)} %get-tuple-element.23.velocity, f32[3,4,64,128]{3,2,1,0:T(8,128)S(1)} %get-tuple-element.32.mid, f32[2,256,128]{2,1,0:T(8,128)S(1)} %get-tuple-element.31.deposit), custom_call_target="tpu_custom_call" | custom-call | bytes 1835008 | tf_op jit(solution)/shard_map/advance/pallas_call | solution.py:424
  24.6 0.0 collective-permute-done.3.low
  24.7 0.0 collective-permute-done.4.high
  24.7 0.8 %collective-permute-done.5.from_other = f32[128,128]{1,0:T(8,128)S(1)} collective-permute-done((f32[128,128]{1,0:T(8,128)S(1)}, f32[128,128]{1,0:T(8,128)S(1)}, u32[]{:S(2)}, u32[]{:S(2)}) %collective-permute-start.5) | collective-permute-done | bytes 65568 | tf_op jit(solution)/shard_map/ppermute | solution.py:438
  25.4 1.2 %finish.1 = (f32[4,64,128]{2,1,0:T(8,128)}, f32[4,64,128]{2,1,0:T(8,128)}, f32[4,64,128]{2,1,0:T(8,128)}) custom-call(f32[3,4,64,128]{3,2,1,0:T(8,128)S(1)} %get-tuple-element.22.state, f32[3,4,64,128]{3,2,1,0:T(8,128)S(1)} %get-tuple-element.23.velocity, f32[3,4,64,128]{3,2,1,0:T(8,128)S(1)} %advance.1.advanced, ...), custom_call_target="tpu_custom_call" | custom-call | bytes 2441216 | tf_op jit(solution)/shard_map/finish/pallas_call | solution.py:424
  (8 shorter events, 0.0 us)
Async XLA Ops:
  2.3 21.3 %collective-permute-start = (f32[544,128]{1,0:T(8,128)S(1)}, f32[544,128]{1,0:T(8,128)S(1)}, u32[]{:S(2)}, u32[]{:S(2)}) collective-permute-start(f32[544,128]{1,0:T(8,128)S(1)} %get-tuple-element.28), channel_id=1, source_target_pairs={{0,1},{1,2},{2,3},{3,4},{4,5},{5,6},{6,7},{7,8},{8,9},{9,10},{10,1... | collective-permute-start | bytes 835592 | tf_op jit(solution)/shard_map/ppermute | solution.py:443
  4.4 13.1 %copy-start = (f32[1,1,1024,128]{3,2,1,0:T(8,128)S(1)}, f32[1,1,1024,128]{3,2,1,0:T(8,128)}, u32[]{:S(2)}) copy-start(f32[1,1,1024,128]{3,2,1,0:T(8,128)} %param.16) | copy-start | bytes 1572868
  4.4 13.2 %copy-start.1 = (f32[128,128]{1,0:T(8,128)S(1)}, f32[128,128]{1,0:T(8,128)}, u32[]{:S(2)}) copy-start(f32[128,128]{1,0:T(8,128)} %weak.1) | copy-start | bytes 196612
  4.4 13.2 %copy-start.2 = (f32[128,128]{1,0:T(8,128)S(1)}, f32[128,128]{1,0:T(8,128)}, u32[]{:S(2)}) copy-start(f32[128,128]{1,0:T(8,128)} %capture.1) | copy-start | bytes 196612
  4.7 19.9 %collective-permute-start.3 = (f32[384,128]{1,0:T(8,128)S(1)}, f32[384,128]{1,0:T(8,128)S(1)}, u32[]{:S(2)}, u32[]{:S(2)}) collective-permute-start(f32[384,128]{1,0:T(8,128)S(1)} %get-tuple-element.33), channel_id=1, source_target_pairs={{0,1},{1,2},{2,3},{3,4},{4,5},{5,6},{6,7},{7,8},{8,9},{9,10},{10,1... | collective-permute-start | bytes 589832 | tf_op jit(solution)/shard_map/ppermute | solution.py:443
  6.0 17.6 %collective-permute-start.1 = (f32[416,128]{1,0:T(8,128)S(1)}, f32[416,128]{1,0:T(8,128)S(1)}, u32[]{:S(2)}, u32[]{:S(2)}) collective-permute-start(f32[416,128]{1,0:T(8,128)S(1)} %get-tuple-element.29), channel_id=1, source_target_pairs={{0,127},{1,0},{2,1},{3,2},{4,3},{5,4},{6,5},{7,6},{8,7},{9,8},{10,... | collective-permute-start | bytes 638984 | tf_op jit(solution)/shard_map/ppermute | solution.py:443
  14.0 10.7 %collective-permute-start.4 = (f32[512,128]{1,0:T(8,128)S(1)}, f32[512,128]{1,0:T(8,128)S(1)}, u32[]{:S(2)}, u32[]{:S(2)}) collective-permute-start(f32[512,128]{1,0:T(8,128)S(1)} %get-tuple-element.34), channel_id=1, source_target_pairs={{0,127},{1,0},{2,1},{3,2},{4,3},{5,4},{6,5},{7,6},{8,7},{9,8},{10,... | collective-permute-start | bytes 786440 | tf_op jit(solution)/shard_map/ppermute | solution.py:443
  15.4 8.3 %collective-permute-start.2 = (f32[528,128]{1,0:T(8,128)S(1)}, f32[528,128]{1,0:T(8,128)S(1)}, u32[]{:S(2)}, u32[]{:S(2)}) collective-permute-start(f32[528,128]{1,0:T(8,128)S(1)} %get-tuple-element.30), channel_id=1, source_target_pairs={{0,128},{128,0},{1,129},{129,1},{2,130},{130,2},{3,131},{131,3},{4... | collective-permute-start | bytes 811016 | tf_op jit(solution)/shard_map/ppermute | solution.py:438
  17.5 0.7 %copy-start.4 = (f32[1,1,1024]{2,1,0:T(1,128)S(1)}, f32[1,1,1024]{2,1,0:T(1,128)}, u32[]{:S(2)}) copy-start(f32[1,1,1024]{2,1,0:T(1,128)} %param.17) | copy-start | bytes 12292
  17.6 0.7 %copy-start.3 = (s32[1,1,1024]{2,1,0:T(1,128)S(1)}, s32[1,1,1024]{2,1,0:T(1,128)}, u32[]{:S(2)}) copy-start(s32[1,1,1024]{2,1,0:T(1,128)} %param.18) | copy-start | bytes 12292
  17.6 0.7 %copy-start.5 = (f32[128]{0:T(128)S(1)}, f32[128]{0:T(128)}, u32[]{:S(2)}) copy-start(f32[128]{0:T(128)} %param.22) | copy-start | bytes 1540
  17.6 0.7 %copy-start.6 = (f32[128]{0:T(128)S(1)}, f32[128]{0:T(128)}, u32[]{:S(2)}) copy-start(f32[128]{0:T(128)} %param.23) | copy-start | bytes 1540
  24.1 1.3 %collective-permute-start.5 = (f32[128,128]{1,0:T(8,128)S(1)}, f32[128,128]{1,0:T(8,128)S(1)}, u32[]{:S(2)}, u32[]{:S(2)}) collective-permute-start(f32[128,128]{1,0:T(8,128)S(1)} %get-tuple-element.35.sent), channel_id=1, source_target_pairs={{0,128},{128,0},{1,129},{129,1},{2,130},{130,2},{3,131},{131,3},{4... | collective-permute-start | bytes 196616 | tf_op jit(solution)/shard_map/ppermute | solution.py:438

commit v9 on v8

--- a/solution.py
+++ b/solution.py
@@ -120,7 +120,9 @@
 
 
 def edges_kernel(
-    density, energy, lepton, speeds, state, velocity, slopes, low_first, folded, packed, sems
+    density, energy, lepton, speeds, cells_in, mass_in, binding_in, charge_in,
+    state, velocity, slopes, low_first, folded, packed, cells, mass, binding, charge,
+    sems,
 ):
     wait_speeds = pltpu.make_async_copy(speeds, velocity, sems.at[3])
     wait_speeds.start()
@@ -128,7 +130,15 @@
         pltpu.make_async_copy(ref, state.at[f], sems.at[f])
         for f, ref in enumerate((density, energy, lepton))
     ]
-    for copy in copies:
+    small = [
+        pltpu.make_async_copy(source, target, sems.at[4 + n])
+        for n, (source, target) in enumerate(
+            (
+                (cells_in, cells), (mass_in, mass), (binding_in, binding), (charge_in, charge),
+            )
+        )
+    ]
+    for copy in copies + small:
         copy.start()
     weights = twice(jnp.concatenate([circulant(), spreading()], axis=1))
     group = groups()
@@ -152,6 +162,8 @@
     low_first[pl.ds(384, 32), :] = up
     for k in range(2):
         low_first[pl.ds(416 + 64 * k, 64), :] = velocity[0, 3 - k]
+    for copy in small:
+        copy.wait()
 
 
 def messages_kernel(
@@ -330,6 +342,7 @@
     rows_out, deposit,
     table, both, rest, x_ref, t_ref, k_ref, a_ref, w_ref, c_ref, iterate, gain_both, gain_rest,
 ):
+    occupied_slots = count[0, 0]
     load_matrices(weak, capture, both, rest)
     rho, eps, lam = (state[f].reshape(256, 128) for f in range(3))
     inverse = 1.0 / rho
@@ -371,7 +384,7 @@
 
         def write_last(b, values):
             slot = base + b * BLOCK + lax.broadcasted_iota(jnp.int32, (BLOCK, 128), 0)
-            occupied = slot < count[0, 0]
+            occupied = slot < occupied_slots
             rows_out[place(b), :] = jnp.where(occupied, values, 0.0)
             change = jnp.where(occupied, values - rows[place(b), :], 0.0)
             high, low = split(change)
@@ -407,15 +420,15 @@
         deposit[1] += sums[:, 128:256] + sums[:, 384:]
         return carry
 
-    lax.fori_loop(0, (count[0, 0] + CHUNK - 1) // CHUNK, chunk, 0)
+    lax.fori_loop(0, (occupied_slots + CHUNK - 1) // CHUNK, chunk, 0)
 
 
 VMEM = pl.BlockSpec(memory_space=pltpu.VMEM)
+HBM = pl.BlockSpec(memory_space=pltpu.HBM)
 SMEM = pl.BlockSpec(memory_space=pltpu.SMEM)
-HBM = pl.BlockSpec(memory_space=pltpu.HBM)
-
-
-def call(kernel, name, outs, args, scratch=(), flops=0, first=(), out=VMEM):
+
+
+def call(kernel, name, outs, args, scratch=(), flops=0, first=(), out=VMEM, integers=()):
     args = [
         pltpu.with_memory_space_constraint(a, pltpu.HBM) if s is HBM else a
         for a, s in zip(args, list(first) + [None] * len(args))
@@ -424,7 +437,9 @@
     return pl.pallas_call(
         kernel,
         name=name,
-        out_shape=[jax.ShapeDtypeStruct(o, F32) for o in outs],
+        out_shape=[
+            jax.ShapeDtypeStruct(o, jnp.int32 if n in integers else F32) for n, o in enumerate(outs)
+        ],
         in_specs=list(first) + [VMEM] * (len(args) - len(first)),
         out_specs=[out] * len(outs),
         scratch_shapes=list(scratch),
@@ -461,9 +476,15 @@
     whole, tile = (3, 4, 64, 128), (64, 128)
     pads = pltpu.VMEM((12, 80, 128), F32)
     planes = pltpu.VMEM((4, 64, 128), F32)
-    state, speeds, slopes, low_first, folded, packed = call(
-        edges_kernel, "edges", [whole] * 3 + [(544, 128), (32, 128), tile], (*fields, velocity),
-        [pltpu.SemaphoreType.DMA((4,))], 0, [HBM] * 4,
+    small, row = (8, 128), (1, 128)
+    state, speeds, slopes, low_first, folded, packed, cells, mass, *tables = call(
+        edges_kernel, "edges",
+        [whole] * 3 + [(544, 128), (32, 128), tile, small, small, row, row],
+        (
+            *fields, velocity, tracer_cell.reshape(small), tracer_mass.reshape(small),
+            binding.reshape(row), charge_ratio.reshape(row),
+        ),
+        [pltpu.SemaphoreType.DMA((8,))], 0, [HBM] * 8, VMEM, (6,),
     )
     low_first = send(low_first, 1)
     partial, low_second, high_first, high_second, copied = call(
@@ -480,9 +501,8 @@
     finished, deposit = call(
         network_kernel, "network", [(1024, 128), (2, 256, 128)],
         (
-            tracer_count, state, tracer_cell.reshape(8, 128), abundance.reshape(1024, 128),
-            weak_rates, capture_rates, tracer_mass.reshape(8, 128),
-            binding.reshape(1, 128), charge_ratio.reshape(1, 128),
+            tracer_count, state, cells, abundance.reshape(1024, 128),
+            weak_rates, capture_rates, mass, *tables,
         ),
         [pltpu.VMEM((256, 512), BF16), *matrices, pltpu.VMEM((CHUNK, 256), BF16)]
         + [rows] * 6 + matrices,

time: 26.8 us -> 26.1 us (0.974)
  local copies, waits for them, and re-layouts: 0.66 us -> 0.01 us
    unnamed x14 -> x6, local copies, waits for them, and re-layouts: 0.66 us -> 0.01 us
  transfers between devices with their start and end apart: 6 -> 6, of which waited for: 1 -> 2; matrix products, arithmetic and copies ran while one was open for 0% -> 0% of each run, Pallas kernels for 25% -> 25%
where the time goes in v9:
time: 26.1 us; the launch traced here: 26 us
  starting transfers between devices  14.4 us (55%)
  Pallas kernels  9.45 us (36%)
  between operations  1.35 us (5%)
  waiting for transfers between devices  0.8 us (3%)
    ppermute x4, starting transfers between devices, send(): lax.ppermute(message, 'brick', [(i, (i + step) % count) for i in range(co...  12.8 us
    pallas_call x6, Pallas kernels, call(): pl.pallas_call(kernel, name=name, out_shape=[jax.ShapeDtypeStruct(o, jnp....  9.45 us
    ppermute x2, starting transfers between devices, swap_halves(): lax.ppermute(packed, 'grp', [(i, (i + 1) % halves) for i in range(halves)])  1.61 us
    ppermute x2, waiting for transfers between devices, swap_halves(): lax.ppermute(packed, 'grp', [(i, (i + 1) % halves) for i in range(halves)])  0.71 us
  transfers between devices with their start and end apart: 6, of which 2 were waited for; matrix products, arithmetic and copies ran while one was open for 0% of the time, Pallas kernels for 25%

profile of v9, /device:TPU:1, one launch (start us, length us, event | category | flops | bytes accessed | tf_op | source)
XLA Modules:
  0.0 26.0 jit_solution(14458093613760806720)
XLA Ops:
  0.6 1.7 %edges.1 = (f32[3,4,64,128]{3,2,1,0:T(8,128)S(1)}, f32[3,4,64,128]{3,2,1,0:T(8,128)S(1)}, f32[3,4,64,128]{3,2,1,0:T(8,128)S(1)}, f32[544,128]{1,0:T(8,128)S(1)},...) custom-call(f32[4,64,128]{2,1,0:T(8,128)} %density.1, ...), custom_call_target="tpu_custom_call" | custom-call | bytes 2312192 | tf_op jit(solution)/shard_map/edges/pallas_call | solution.py:437
  2.4 2.1 %collective-permute-start = (f32[544,128]{1,0:T(8,128)S(1)}, f32[544,128]{1,0:T(8,128)S(1)}, u32[]{:S(2)}, u32[]{:S(2)}) collective-permute-start(f32[544,128]{1,0:T(8,128)S(1)} %get-tuple-element.32), channel_id=1, source_target_pairs={{0,1},{1,2},{2,3},{3,4},{4,5},{5,6},{6,7},{7,8},{8,9},{9,10},{10,1... | collective-permute-start | bytes 835592 | tf_op jit(solution)/shard_map/ppermute | solution.py:458
  4.5 0.0 copy-start
  4.5 0.0 copy-start.1
  4.5 0.0 copy-start.2
  4.5 0.3 %messages.1 = (f32[3,4,64,128]{3,2,1,0:T(8,128)S(1)}, f32[384,128]{1,0:T(8,128)S(1)}, f32[416,128]{1,0:T(8,128)S(1)}, f32[512,128]{1,0:T(8,128)S(1)}, f32[528,128]{1,0:T(8,128)S(1)}) custom-call(f32[3,4,64,128]{3,2,1,0:T(8,128)S(1)} %get-tuple-element.26.state, f32[3,4,64,128]{3,2,1,0:T(8,128)S(1)} %get-tuple-element.27.velocity, ...), custom_call_target="tpu_custom_call" | custom-call | bytes 2564096 | tf_op jit(solution)/shard_map/messages/pallas_call | solution.py:437
  4.8 1.3 %collective-permute-start.3 = (f32[384,128]{1,0:T(8,128)S(1)}, f32[384,128]{1,0:T(8,128)S(1)}, u32[]{:S(2)}, u32[]{:S(2)}) collective-permute-start(f32[384,128]{1,0:T(8,128)S(1)} %get-tuple-element.41), channel_id=1, source_target_pairs={{0,1},{1,2},{2,3},{3,4},{4,5},{5,6},{6,7},{7,8},{8,9},{9,10},{10,1... | collective-permute-start | bytes 589832 | tf_op jit(solution)/shard_map/ppermute | solution.py:458
  6.1 7.9 %collective-permute-start.1 = (f32[416,128]{1,0:T(8,128)S(1)}, f32[416,128]{1,0:T(8,128)S(1)}, u32[]{:S(2)}, u32[]{:S(2)}) collective-permute-start(f32[416,128]{1,0:T(8,128)S(1)} %get-tuple-element.33), channel_id=1, source_target_pairs={{0,127},{1,0},{2,1},{3,2},{4,3},{5,4},{6,5},{7,6},{8,7},{9,8},{10,... | collective-permute-start | bytes 638984 | tf_op jit(solution)/shard_map/ppermute | solution.py:458
  14.0 1.4 %collective-permute-start.4 = (f32[512,128]{1,0:T(8,128)S(1)}, f32[512,128]{1,0:T(8,128)S(1)}, u32[]{:S(2)}, u32[]{:S(2)}) collective-permute-start(f32[512,128]{1,0:T(8,128)S(1)} %get-tuple-element.42), channel_id=1, source_target_pairs={{0,127},{1,0},{2,1},{3,2},{4,3},{5,4},{6,5},{7,6},{8,7},{9,8},{10,... | collective-permute-start | bytes 786440 | tf_op jit(solution)/shard_map/ppermute | solution.py:458
  15.4 1.5 %collective-permute-start.2 = (f32[528,128]{1,0:T(8,128)S(1)}, f32[528,128]{1,0:T(8,128)S(1)}, u32[]{:S(2)}, u32[]{:S(2)}) collective-permute-start(f32[528,128]{1,0:T(8,128)S(1)} %get-tuple-element.34), channel_id=1, source_target_pairs={{0,128},{128,0},{1,129},{129,1},{2,130},{130,2},{3,131},{131,3},{4... | collective-permute-start | bytes 811016 | tf_op jit(solution)/shard_map/ppermute | solution.py:453
  17.6 0.0 copy-done
  17.6 0.0 copy-done.1
  17.6 0.0 copy-done.2
  17.6 5.4 %network.1 = (f32[1024,128]{1,0:T(8,128)}, f32[2,256,128]{2,1,0:T(8,128)S(1)}) custom-call(s32[1,1]{1,0:T(1,128)S(6)} %copy.16.count, f32[3,4,64,128]{3,2,1,0:T(8,128)S(1)} %get-tuple-element.26.state, s32[8,128]{1,0:T(8,128)S(1)} %get-tuple-element.35.cells, f32[1024,128]{1,0:T(8,128)S(1)} %bitcast.6, f32[128,128]{1,0:T(8,128)S(1)} %copy-done.1, ...), custom_call_target="tpu_custom_call" | custom-call | flops 7247757312 | bytes 1844228 | tf_op jit(solution)/shard_map/network/pallas_call | solution.py:437
  23.0 0.0 collective-permute-done.1.high
  23.0 0.0 collective-permute-done.2.from_other
  23.0 0.0 collective-permute-done.low.low_first
  23.0 0.4 %midpoint.1 = (f32[3,4,64,128]{3,2,1,0:T(8,128)S(1)}, f32[128,128]{1,0:T(8,128)S(1)}) custom-call(f32[3,4,64,128]{3,2,1,0:T(8,128)S(1)} %get-tuple-element.26.state, f32[3,4,64,128]{3,2,1,0:T(8,128)S(1)} %get-tuple-element.27.velocity, f32[3,4,64,128]{3,2,1,0:T(8,128)S(1)} %get-tuple-element.31.partial, f32[544,128]{1,0:T(8,128)S(1)} %collective-permute-done.low.low_first, ...), custom_call_target="tpu_custom_call" | custom-call | bytes 2695168 | tf_op jit(solution)/shard_map/midpoint/pallas_call | solution.py:437
  23.5 0.1 collective-permute-start.5
  23.6 0.4 %advance.1.advanced = f32[3,4,64,128]{3,2,1,0:T(8,128)S(1)} custom-call(f32[3,4,64,128]{3,2,1,0:T(8,128)S(1)} %get-tuple-element.26.state, f32[3,4,64,128]{3,2,1,0:T(8,128)S(1)} %get-tuple-element.27.velocity, f32[3,4,64,128]{3,2,1,0:T(8,128)S(1)} %get-tuple-element.40.mid, f32[2,256,128]{2,1,0:T(8,128)S(1)} %get-tuple-element.39.deposit), custom_call_target="tpu_custom_call" | custom-call | bytes 1835008 | tf_op jit(solution)/shard_map/advance/pallas_call | solution.py:437
  24.0 0.1 collective-permute-done.3.low
  24.1 0.0 collective-permute-done.4.high
  24.1 0.7 %collective-permute-done.5.from_other = f32[128,128]{1,0:T(8,128)S(1)} collective-permute-done((f32[128,128]{1,0:T(8,128)S(1)}, f32[128,128]{1,0:T(8,128)S(1)}, u32[]{:S(2)}, u32[]{:S(2)}) %collective-permute-start.5) | collective-permute-done | bytes 65568 | tf_op jit(solution)/shard_map/ppermute | solution.py:453
  24.8 1.2 %finish.1 = (f32[4,64,128]{2,1,0:T(8,128)}, f32[4,64,128]{2,1,0:T(8,128)}, f32[4,64,128]{2,1,0:T(8,128)}) custom-call(f32[3,4,64,128]{3,2,1,0:T(8,128)S(1)} %get-tuple-element.26.state, f32[3,4,64,128]{3,2,1,0:T(8,128)S(1)} %get-tuple-element.27.velocity, f32[3,4,64,128]{3,2,1,0:T(8,128)S(1)} %advance.1.advanced, ...), custom_call_target="tpu_custom_call" | custom-call | bytes 2441216 | tf_op jit(solution)/shard_map/finish/pallas_call | solution.py:437
Async XLA Ops:
  2.4 20.6 %collective-permute-start = (f32[544,128]{1,0:T(8,128)S(1)}, f32[544,128]{1,0:T(8,128)S(1)}, u32[]{:S(2)}, u32[]{:S(2)}) collective-permute-start(f32[544,128]{1,0:T(8,128)S(1)} %get-tuple-element.32), channel_id=1, source_target_pairs={{0,1},{1,2},{2,3},{3,4},{4,5},{5,6},{6,7},{7,8},{8,9},{9,10},{10,1... | collective-permute-start | bytes 835592 | tf_op jit(solution)/shard_map/ppermute | solution.py:458
  4.5 13.1 %copy-start = (f32[1,1,1024,128]{3,2,1,0:T(8,128)S(1)}, f32[1,1,1024,128]{3,2,1,0:T(8,128)}, u32[]{:S(2)}) copy-start(f32[1,1,1024,128]{3,2,1,0:T(8,128)} %param.16) | copy-start | bytes 1572868
  4.5 13.1 %copy-start.1 = (f32[128,128]{1,0:T(8,128)S(1)}, f32[128,128]{1,0:T(8,128)}, u32[]{:S(2)}) copy-start(f32[128,128]{1,0:T(8,128)} %weak.1) | copy-start | bytes 196612
  4.5 13.1 %copy-start.2 = (f32[128,128]{1,0:T(8,128)S(1)}, f32[128,128]{1,0:T(8,128)}, u32[]{:S(2)}) copy-start(f32[128,128]{1,0:T(8,128)} %capture.1) | copy-start | bytes 196612
  4.8 19.3 %collective-permute-start.3 = (f32[384,128]{1,0:T(8,128)S(1)}, f32[384,128]{1,0:T(8,128)S(1)}, u32[]{:S(2)}, u32[]{:S(2)}) collective-permute-start(f32[384,128]{1,0:T(8,128)S(1)} %get-tuple-element.41), channel_id=1, source_target_pairs={{0,1},{1,2},{2,3},{3,4},{4,5},{5,6},{6,7},{7,8},{8,9},{9,10},{10,1... | collective-permute-start | bytes 589832 | tf_op jit(solution)/shard_map/ppermute | solution.py:458
  6.1 16.9 %collective-permute-start.1 = (f32[416,128]{1,0:T(8,128)S(1)}, f32[416,128]{1,0:T(8,128)S(1)}, u32[]{:S(2)}, u32[]{:S(2)}) collective-permute-start(f32[416,128]{1,0:T(8,128)S(1)} %get-tuple-element.33), channel_id=1, source_target_pairs={{0,127},{1,0},{2,1},{3,2},{4,3},{5,4},{6,5},{7,6},{8,7},{9,8},{10,... | collective-permute-start | bytes 638984 | tf_op jit(solution)/shard_map/ppermute | solution.py:458
  14.0 10.1 %collective-permute-start.4 = (f32[512,128]{1,0:T(8,128)S(1)}, f32[512,128]{1,0:T(8,128)S(1)}, u32[]{:S(2)}, u32[]{:S(2)}) collective-permute-start(f32[512,128]{1,0:T(8,128)S(1)} %get-tuple-element.42), channel_id=1, source_target_pairs={{0,127},{1,0},{2,1},{3,2},{4,3},{5,4},{6,5},{7,6},{8,7},{9,8},{10,... | collective-permute-start | bytes 786440 | tf_op jit(solution)/shard_map/ppermute | solution.py:458
  15.4 7.6 %collective-permute-start.2 = (f32[528,128]{1,0:T(8,128)S(1)}, f32[528,128]{1,0:T(8,128)S(1)}, u32[]{:S(2)}, u32[]{:S(2)}) collective-permute-start(f32[528,128]{1,0:T(8,128)S(1)} %get-tuple-element.34), channel_id=1, source_target_pairs={{0,128},{128,0},{1,129},{129,1},{2,130},{130,2},{3,131},{131,3},{4... | collective-permute-start | bytes 811016 | tf_op jit(solution)/shard_map/ppermute | solution.py:453
  23.5 1.3 %collective-permute-start.5 = (f32[128,128]{1,0:T(8,128)S(1)}, f32[128,128]{1,0:T(8,128)S(1)}, u32[]{:S(2)}, u32[]{:S(2)}) collective-permute-start(f32[128,128]{1,0:T(8,128)S(1)} %get-tuple-element.43.sent), channel_id=1, source_target_pairs={{0,128},{128,0},{1,129},{129,1},{2,130},{130,2},{3,131},{131,3},{4... | collective-permute-start | bytes 196616 | tf_op jit(solution)/shard_map/ppermute | solution.py:453

commit v10 on v9

--- a/solution.py
+++ b/solution.py
@@ -181,15 +181,14 @@
     high_first[pl.ds(384, 32), :] = folded[...]
     for k in range(2):
         high_second[rows_of_tile(6 + k), :] = velocity[0, k]
-    copied[pl.ds(0, 64), :] = packed[...]
-    copied[pl.ds(64, 464), :] = jnp.zeros((464, 128), F32)
+    copied[...] = packed[...]
 
 
 def midpoint_kernel(
     state, velocity, partial, low, high, packed, from_other, deposit, mid, exchanged, total
 ):
     lane = lanes()
-    correction = edge_correction(from_other[pl.ds(0, 64), :], packed[...], lane)
+    correction = edge_correction(from_other[...], packed[...], lane)
     group = groups()
     weights = twice(spreading())
     pack = jnp.zeros((64, 128), F32)
@@ -307,11 +306,14 @@
         t_ref[at, :] = target
         put(b, target)
         start(b, target)
+    ahead = {b: products(b) for b in range(2)}
     for sweep in range(SWEEPS):
         for b in range(blocks):
             at = pl.ds(b * BLOCK, BLOCK)
             here = pl.ds(base + b * BLOCK, BLOCK)
-            product = products(b)
+            product = ahead.pop(b)
+            if b + 2 < blocks or sweep < SWEEPS - 1:
+                ahead[(b + 2) % blocks] = products((b + 2) % blocks)
             before = finish.last[b]
             update = t_ref[at, :] + (
                 w_ref[here, :] * product[:, :128]
@@ -488,7 +490,7 @@
     )
     low_first = send(low_first, 1)
     partial, low_second, high_first, high_second, copied = call(
-        messages_kernel, "messages", [whole, (384, 128), (416, 128), (512, 128), (528, 128)],
+        messages_kernel, "messages", [whole, (384, 128), (416, 128), (512, 128), tile],
         (state, speeds, slopes, folded, packed), [pads],
     )
     low_second = send(low_second, 1)

time: 26.1 us -> 26.7 us (1.023)
  the two profiles are of different devices: /device:TPU:1 before, /device:TPU:126 now
where the time goes in v10:
time: 26.7 us; the launch traced here: 26.6 us
  waiting for transfers between devices  10.9 us (41%)
  Pallas kernels  9.27 us (35%)
  starting transfers between devices  5.1 us (19%)
  between operations  1.37 us (5%)
    ppermute x4, waiting for transfers between devices, send(): lax.ppermute(message, 'brick', [(i, (i + step) % count) for i in range(co...  10.9 us
    pallas_call x6, Pallas kernels, call(): pl.pallas_call(kernel, name=name, out_shape=[jax.ShapeDtypeStruct(o, jnp....  9.27 us
    ppermute x4, starting transfers between devices, send(): lax.ppermute(message, 'brick', [(i, (i + step) % count) for i in range(co...  4.92 us
  transfers between devices with their start and end apart: 6, of which 2 were waited for; matrix products, arithmetic and copies ran while one was open for 0% of the time, Pallas kernels for 24%

profile of v10, /device:TPU:126, one launch (start us, length us, event | category | flops | bytes accessed | tf_op | source)
XLA Modules:
  0.0 26.6 jit_solution(17154490568605690894)
XLA Ops:
  0.6 1.7 %edges.1 = (f32[3,4,64,128]{3,2,1,0:T(8,128)S(1)}, f32[3,4,64,128]{3,2,1,0:T(8,128)S(1)}, f32[3,4,64,128]{3,2,1,0:T(8,128)S(1)}, f32[544,128]{1,0:T(8,128)S(1)},...) custom-call(f32[4,64,128]{2,1,0:T(8,128)} %density.1, ...), custom_call_target="tpu_custom_call" | custom-call | bytes 2312192 | tf_op jit(solution)/shard_map/edges/pallas_call | solution.py:439
  2.4 2.8 %collective-permute-start = (f32[544,128]{1,0:T(8,128)S(1)}, f32[544,128]{1,0:T(8,128)S(1)}, u32[]{:S(2)}, u32[]{:S(2)}) collective-permute-start(f32[544,128]{1,0:T(8,128)S(1)} %get-tuple-element.32), channel_id=1, source_target_pairs={{0,1},{1,2},{2,3},{3,4},{4,5},{5,6},{6,7},{7,8},{8,9},{9,10},{10,1... | collective-permute-start | bytes 835592 | tf_op jit(solution)/shard_map/ppermute | solution.py:460
  5.2 0.0 copy-start
  5.2 0.0 copy-start.1
  5.2 0.0 copy-start.2
  5.2 0.3 messages.1
  5.4 0.1 collective-permute-start.2
  5.5 1.6 %collective-permute-start.3 = (f32[384,128]{1,0:T(8,128)S(1)}, f32[384,128]{1,0:T(8,128)S(1)}, u32[]{:S(2)}, u32[]{:S(2)}) collective-permute-start(f32[384,128]{1,0:T(8,128)S(1)} %get-tuple-element.41), channel_id=1, source_target_pairs={{0,1},{1,2},{2,3},{3,4},{4,5},{5,6},{6,7},{7,8},{8,9},{9,10},{10,1... | collective-permute-start | bytes 589832 | tf_op jit(solution)/shard_map/ppermute | solution.py:460
  7.1 0.5 %collective-permute-start.1 = (f32[416,128]{1,0:T(8,128)S(1)}, f32[416,128]{1,0:T(8,128)S(1)}, u32[]{:S(2)}, u32[]{:S(2)}) collective-permute-start(f32[416,128]{1,0:T(8,128)S(1)} %get-tuple-element.33), channel_id=1, source_target_pairs={{0,127},{1,0},{2,1},{3,2},{4,3},{5,4},{6,5},{7,6},{8,7},{9,8},{10,... | collective-permute-start | bytes 638984 | tf_op jit(solution)/shard_map/ppermute | solution.py:460
  7.6 0.0 collective-permute-start.4
  8.3 0.0 copy-done
  8.3 0.0 copy-done.1
  8.3 0.0 copy-done.2
  8.3 5.3 %network.1 = (f32[1024,128]{1,0:T(8,128)}, f32[2,256,128]{2,1,0:T(8,128)S(1)}) custom-call(s32[1,1]{1,0:T(1,128)S(6)} %copy.16.count, f32[3,4,64,128]{3,2,1,0:T(8,128)S(1)} %get-tuple-element.26.state, s32[8,128]{1,0:T(8,128)S(1)} %get-tuple-element.35.cells, f32[1024,128]{1,0:T(8,128)S(1)} %bitcast.6, f32[128,128]{1,0:T(8,128)S(1)} %copy-done.1, ...), custom_call_target="tpu_custom_call" | custom-call | flops 7247757312 | bytes 1844228 | tf_op jit(solution)/shard_map/network/pallas_call | solution.py:439
  13.7 0.0 collective-permute-done.2.from_other
  13.7 6.9 %collective-permute-done.1.high = f32[416,128]{1,0:T(8,128)S(1)} collective-permute-done((f32[416,128]{1,0:T(8,128)S(1)}, f32[416,128]{1,0:T(8,128)S(1)}, u32[]{:S(2)}, u32[]{:S(2)}) %collective-permute-start.1) | collective-permute-done | bytes 213024 | tf_op jit(solution)/shard_map/ppermute | solution.py:460
  20.6 0.0 collective-permute-done.low.low_first
  20.6 0.4 %midpoint.1 = (f32[3,4,64,128]{3,2,1,0:T(8,128)S(1)}, f32[128,128]{1,0:T(8,128)S(1)}) custom-call(f32[3,4,64,128]{3,2,1,0:T(8,128)S(1)} %get-tuple-element.26.state, f32[3,4,64,128]{3,2,1,0:T(8,128)S(1)} %get-tuple-element.27.velocity, f32[3,4,64,128]{3,2,1,0:T(8,128)S(1)} %get-tuple-element.31.partial, f32[544,128]{1,0:T(8,128)S(1)} %collective-permute-done.low.low_first, ...), custom_call_target="tpu_custom_call" | custom-call | bytes 2457600 | tf_op jit(solution)/shard_map/midpoint/pallas_call | solution.py:439
  21.0 0.1 collective-permute-start.5
  21.1 0.4 %advance.1.advanced = f32[3,4,64,128]{3,2,1,0:T(8,128)S(1)} custom-call(f32[3,4,64,128]{3,2,1,0:T(8,128)S(1)} %get-tuple-element.26.state, f32[3,4,64,128]{3,2,1,0:T(8,128)S(1)} %get-tuple-element.27.velocity, f32[3,4,64,128]{3,2,1,0:T(8,128)S(1)} %get-tuple-element.40.mid, f32[2,256,128]{2,1,0:T(8,128)S(1)} %get-tuple-element.39.deposit), custom_call_target="tpu_custom_call" | custom-call | bytes 1835008 | tf_op jit(solution)/shard_map/advance/pallas_call | solution.py:439
  21.5 0.0 collective-permute-done.3.low
  21.5 3.9 %collective-permute-done.4.high = f32[512,128]{1,0:T(8,128)S(1)} collective-permute-done((f32[512,128]{1,0:T(8,128)S(1)}, f32[512,128]{1,0:T(8,128)S(1)}, u32[]{:S(2)}, u32[]{:S(2)}) %collective-permute-start.4) | collective-permute-done | bytes 262176 | tf_op jit(solution)/shard_map/ppermute | solution.py:460
  25.4 0.0 collective-permute-done.5.from_other
  25.5 1.2 %finish.1 = (f32[4,64,128]{2,1,0:T(8,128)}, f32[4,64,128]{2,1,0:T(8,128)}, f32[4,64,128]{2,1,0:T(8,128)}) custom-call(f32[3,4,64,128]{3,2,1,0:T(8,128)S(1)} %get-tuple-element.26.state, f32[3,4,64,128]{3,2,1,0:T(8,128)S(1)} %get-tuple-element.27.velocity, f32[3,4,64,128]{3,2,1,0:T(8,128)S(1)} %advance.1.advanced, ...), custom_call_target="tpu_custom_call" | custom-call | bytes 2441216 | tf_op jit(solution)/shard_map/finish/pallas_call | solution.py:439
Async XLA Ops:
  2.4 18.2 %collective-permute-start = (f32[544,128]{1,0:T(8,128)S(1)}, f32[544,128]{1,0:T(8,128)S(1)}, u32[]{:S(2)}, u32[]{:S(2)}) collective-permute-start(f32[544,128]{1,0:T(8,128)S(1)} %get-tuple-element.32), channel_id=1, source_target_pairs={{0,1},{1,2},{2,3},{3,4},{4,5},{5,6},{6,7},{7,8},{8,9},{9,10},{10,1... | collective-permute-start | bytes 835592 | tf_op jit(solution)/shard_map/ppermute | solution.py:460
  5.2 3.2 %copy-start = (f32[1,1,1024,128]{3,2,1,0:T(8,128)S(1)}, f32[1,1,1024,128]{3,2,1,0:T(8,128)}, u32[]{:S(2)}) copy-start(f32[1,1,1024,128]{3,2,1,0:T(8,128)} %param.16) | copy-start | bytes 1572868
  5.2 3.2 %copy-start.1 = (f32[128,128]{1,0:T(8,128)S(1)}, f32[128,128]{1,0:T(8,128)}, u32[]{:S(2)}) copy-start(f32[128,128]{1,0:T(8,128)} %weak.1) | copy-start | bytes 196612
  5.2 3.2 %copy-start.2 = (f32[128,128]{1,0:T(8,128)S(1)}, f32[128,128]{1,0:T(8,128)}, u32[]{:S(2)}) copy-start(f32[128,128]{1,0:T(8,128)} %capture.1) | copy-start | bytes 196612
  5.4 8.3 %collective-permute-start.2 = (f32[64,128]{1,0:T(8,128)S(1)}, f32[64,128]{1,0:T(8,128)S(1)}, u32[]{:S(2)}, u32[]{:S(2)}) collective-permute-start(f32[64,128]{1,0:T(8,128)S(1)} %get-tuple-element.34), channel_id=1, source_target_pairs={{0,128},{128,0},{1,129},{129,1},{2,130},{130,2},{3,131},{131,3},{4... | collective-permute-start | bytes 98312 | tf_op jit(solution)/shard_map/ppermute | solution.py:455
  5.5 16.0 %collective-permute-start.3 = (f32[384,128]{1,0:T(8,128)S(1)}, f32[384,128]{1,0:T(8,128)S(1)}, u32[]{:S(2)}, u32[]{:S(2)}) collective-permute-start(f32[384,128]{1,0:T(8,128)S(1)} %get-tuple-element.41), channel_id=1, source_target_pairs={{0,1},{1,2},{2,3},{3,4},{4,5},{5,6},{6,7},{7,8},{8,9},{9,10},{10,1... | collective-permute-start | bytes 589832 | tf_op jit(solution)/shard_map/ppermute | solution.py:460
  7.1 13.5 %collective-permute-start.1 = (f32[416,128]{1,0:T(8,128)S(1)}, f32[416,128]{1,0:T(8,128)S(1)}, u32[]{:S(2)}, u32[]{:S(2)}) collective-permute-start(f32[416,128]{1,0:T(8,128)S(1)} %get-tuple-element.33), channel_id=1, source_target_pairs={{0,127},{1,0},{2,1},{3,2},{4,3},{5,4},{6,5},{7,6},{8,7},{9,8},{10,... | collective-permute-start | bytes 638984 | tf_op jit(solution)/shard_map/ppermute | solution.py:460
  7.6 17.8 %collective-permute-start.4 = (f32[512,128]{1,0:T(8,128)S(1)}, f32[512,128]{1,0:T(8,128)S(1)}, u32[]{:S(2)}, u32[]{:S(2)}) collective-permute-start(f32[512,128]{1,0:T(8,128)S(1)} %get-tuple-element.42), channel_id=1, source_target_pairs={{0,127},{1,0},{2,1},{3,2},{4,3},{5,4},{6,5},{7,6},{8,7},{9,8},{10,... | collective-permute-start | bytes 786440 | tf_op jit(solution)/shard_map/ppermute | solution.py:460
  21.0 4.4 %collective-permute-start.5 = (f32[128,128]{1,0:T(8,128)S(1)}, f32[128,128]{1,0:T(8,128)S(1)}, u32[]{:S(2)}, u32[]{:S(2)}) collective-permute-start(f32[128,128]{1,0:T(8,128)S(1)} %get-tuple-element.43.sent), channel_id=1, source_target_pairs={{0,128},{128,0},{1,129},{129,1},{2,130},{130,2},{3,131},{131,3},{4... | collective-permute-start | bytes 196616 | tf_op jit(solution)/shard_map/ppermute | solution.py:455
